TPU v7x, 256 devices: a whole 4x4x8 slice. The times are simulated.
256 devices in a mesh: grp: 8 (over x, y_hi), intra: 32 (over y_lo, z, core).
Axes of the slice: x: 4, y: 4 (y_hi: 2, y_lo: 2; y = y_hi * 2 + y_lo), z: 8, core: 2. Of those that a mesh axis runs over, the one named last changes fastest.
Arguments:
- tokens: bfloat16 [65536, 8192], P(('grp', 'intra')), may hold values from -24 to 24
- cotangent: bfloat16 [65536, 512], P(('grp', 'intra')), may hold values from -6 to 6
- next_tokens: bfloat16 [65536, 8192], P(('grp', 'intra')), may hold values from -6 to 6
- master: float32 [8192, 512], P(('grp', 'intra')), may hold values from -0.0625 to 0.0625
- moment_one: float32 [8192, 512], P(('grp', 'intra')), may hold values from -0.012 to 0.012
- moment_two: float32 [8192, 512], P(('grp', 'intra')), may hold values from 1e-06 to 0.0001
Outputs:
- new_master: float32 [8192, 512], P(('grp', 'intra'))
- new_moment_one: float32 [8192, 512], P(('grp', 'intra'))
- new_moment_two: float32 [8192, 512], P(('grp', 'intra'))
- next_out: bfloat16 [65536, 512], P(('grp', 'intra'))
All inputs are finite; a program needn't handle non-finite values.
Results may differ from a plain program's by a relative error of at most 0.0049.
Values may be sent and summed in bfloat16 or wider, within the bound.
No kernel may reach another device: no remote copies, remote signals or barrier semaphores. Data moves between devices by JAX's collectives and lax.ppermute only.
A program may use at most 128 MiB of HBM per device.

v0:
```python
import jax
import jax.numpy as jnp
from jax import lax
from jax.sharding import PartitionSpec as P


def on_device(tokens, cotangent, next_tokens, master, moment_one, moment_two):
    groups = lax.axis_size("grp")
    members = lax.axis_size("intra")
    shard_rows = master.shape[0]
    token_rows = tokens.shape[0]
    total_tokens = token_rows * groups * members
    summed = lax.psum_scatter(
        lax.dot_general(
            tokens, cotangent, (((0,), (0,)), ((), ())), preferred_element_type=jnp.float32
        ),
        ("grp", "intra"),
        scatter_dimension=0,
        tiled=True,
    )
    gradient = summed * (1.0 / total_tokens)
    new_moment_one = 0.9 * moment_one + 0.1 * gradient
    new_moment_two = 0.999 * moment_two + 0.001 * gradient * gradient
    first = new_moment_one / (1.0 - 0.9**10)
    second = new_moment_two / (1.0 - 0.999**10)
    new_master = master - 0.01 * (first / (jnp.sqrt(second) + 1e-08) + 0.1 * master)
    weights = new_master.astype(jnp.bfloat16)
    copies = lax.all_gather(weights[None], "grp", axis=0, tiled=True)
    split_tokens = next_tokens.reshape(token_rows, groups, members * shard_rows)
    result = jnp.einsum(
        "tgk,gkf->tf",
        split_tokens,
        lax.all_gather(copies, "intra", axis=1, tiled=True),
        preferred_element_type=jnp.float32,
    )
    return (new_master, new_moment_one, new_moment_two, result.astype(jnp.bfloat16))


def solution(mesh):
    in_specs = (
        P(("grp", "intra"), None),
        P(("grp", "intra"), None),
        P(("grp", "intra"), None),
        P(("grp", "intra"), None),
        P(("grp", "intra"), None),
        P(("grp", "intra"), None),
    )
    out_specs = (
        P(("grp", "intra"), None),
        P(("grp", "intra"), None),
        P(("grp", "intra"), None),
        P(("grp", "intra"), None),
    )
    return jax.shard_map(
        on_device, mesh=mesh, in_specs=in_specs, out_specs=out_specs, check_vma=False
    )
```

profile of v0, /device:TPU:1, one launch (start us, length us, event | category | flops | bytes accessed | tf_op | source)
XLA Modules:
  0.0 1435.3 jit_solution(4685853197337945626)
XLA Ops:
  7.2 0.0 copy-start
  7.2 0.0 reduce-scatter.2.cloned.1.call-start
  7.2 0.9 copy-done
  8.1 10.3 fusion.13
  18.4 0.0 copy-start.1
  18.4 0.0 copy-start.2
  18.4 0.0 copy-start.3
  18.4 0.0 reduce-scatter.2.cloned.1.call-update
  18.5 0.0 all-gather.3.cloned.1.call-start
  18.5 1292.8 %reduce-scatter.2.cloned.1.call-done = f32[32,512]{1,0:T(8,128)} async-done(((f32[8192,512]{1,0:T(8,128)}), f32[32,512]{1,0:T(8,128)}) %reduce-scatter.2.cloned.1.call-update) | async-done | bytes 65552 | tf_op jit(solution)/shard_map/reduce_scatter | solution.py:13
  1311.3 0.0 copy-done.1
  1311.3 0.0 copy-done.2
  1311.3 0.0 copy-done.3
  1311.3 1.5 fusion.12
  1312.8 30.0 %all-gather = bf16[256,512]{1,0:T(8,128)(2,1)} all-gather(bf16[32,512]{1,0:T(8,128)(2,1)S(1)} %get-tuple-element.8), channel_id=2, replica_groups=mesh['grp'=8,'intra'=32] {'grp'}, dimensions={0}, use_global_device_ids=true | all-gather | bytes 294912 | tf_op jit(solution)/shard_map/all_gather | solution.py:28
  1342.8 0.0 all-gather.3.cloned.1.call-update
  1342.9 77.8 %all-gather.3.cloned.1.call-done = bf16[8,1024,512]{2,1,0:T(8,128)(2,1)} async-done(((bf16[8,32,512]{2,1,0:T(8,128)(2,1)}), bf16[8,1024,512]{2,1,0:T(8,128)(2,1)}) %all-gather.3.cloned.1.call-update) | async-done | bytes 8388624 | tf_op jit(solution)/shard_map/all_gather | solution.py:33
  1420.7 6.9 fusion.9
  1427.6 0.8 copy.11
Async XLA Ops:
  7.2 1.0 copy-start
  7.2 1304.1 %reduce-scatter.2.cloned.1.call-start = ((), (), s32[]{:S(2)}) async-start(), calls=%async_computation.1 | async-start | bytes 16842752 | tf_op jit(solution)/shard_map/reduce_scatter | solution.py:13
  18.4 1292.8 %copy-start.1 = (f32[32,512]{1,0:T(8,128)S(1)}, f32[32,512]{1,0:T(8,128)}, u32[]{:S(2)}) copy-start(f32[32,512]{1,0:T(8,128)} %param.9) | copy-start | bytes 196612
  18.4 1292.8 %copy-start.2 = (f32[32,512]{1,0:T(8,128)S(1)}, f32[32,512]{1,0:T(8,128)}, u32[]{:S(2)}) copy-start(f32[32,512]{1,0:T(8,128)} %param.10) | copy-start | bytes 196612
  18.4 1292.8 %copy-start.3 = (f32[32,512]{1,0:T(8,128)S(1)}, f32[32,512]{1,0:T(8,128)}, u32[]{:S(2)}) copy-start(f32[32,512]{1,0:T(8,128)} %param.11) | copy-start | bytes 196612
  18.5 1402.2 %all-gather.3.cloned.1.call-start = ((), (), s32[]{:S(2)}) async-start(), calls=%async_computation.2 | async-start | bytes 8650752 | tf_op jit(solution)/shard_map/all_gather | solution.py:33
Sparse Core Ops, SparseCore 0:
  18.6 1292.6 reduce-scatter.1
  1343.0 77.6 all-gather.2
where the time goes:
time: 1440 us
  waiting for transfers between devices  1370 us (95%)
  blocking collectives  30 us (2%)
  matrix products  17.2 us (1%)
    reduce_scatter x1, waiting for transfers between devices, on_device(): lax.psum_scatter(lax.dot_general(tokens, cotangent, (((0,), (0,)), ((), (...  1290 us
    all_gather x1, waiting for transfers between devices, on_device(): lax.all_gather(copies, 'intra', axis=1, tiled=True)  77.8 us
    all_gather x1, blocking collectives, on_device(): copies = lax.all_gather(weights[None], 'grp', axis=0, tiled=True)  30 us
  transfers between devices with their start and end apart: 2, of which 2 were waited for; matrix products, arithmetic and copies ran while one was open for 0% of the time, Pallas kernels for 0%

commit v1 on v0

v1 whole, which is shorter than its diff:
```python
import functools

import jax
import jax.numpy as jnp
from jax import lax
from jax.experimental import pallas as pl
from jax.experimental.pallas import tpu as pltpu
from jax.sharding import PartitionSpec as P

AXES = ("grp", "intra")
DEVICES = 256
VMEM_LIMIT = 48 * 1024 * 1024


def coordinates(d):
    return d // 64, d // 16 % 4, d // 2 % 8, d % 2


def flat(x, y, z, c):
    return (x % 4) * 64 + (y % 4) * 16 + (z % 8) * 2 + c


def near(z, c):
    return z ^ 1 if c == 0 else ((z + 1) % 8 if z % 2 else (z - 1) % 8)


def far(z, c):
    return near(z // 2, c) % 4 * 2 + z % 2 if c == 0 or z // 2 % 2 else (z // 2 - 1) % 4 * 2 + z % 2


def neighbour(d, da, dz, wide):
    x, y, z, c = coordinates(d)
    if dz:
        z = near(z, c) if wide else far(z, c)
    if (c == 0) == wide:
        x = x + da
    else:
        y = y + da
    return flat(x, y, z, c)


def groups(wide):
    seen = {}
    for d in range(DEVICES):
        members = []
        for parity in range(2):
            _, _, z, _ = coordinates(d)
            here = (z if wide else z // 2) % 2
            for a in range(4):
                x, y, z, c = coordinates(neighbour(d, 0, int(here != parity), wide))
                members.append(flat(a, y, z, c) if (c == 0) == wide else flat(x, a, z, c))
        seen[tuple(members)] = None
    return [list(members) for members in seen]


def home(d, flip):
    x, y, z, c = coordinates(d)
    return flat(x % 2 + 2 * c, y, z ^ (4 * flip), x // 2)


def permute(value, target):
    return lax.ppermute(value, AXES, [(d, target(d)) for d in range(DEVICES)])


OFFSETS = [(1, 0), (3, 0), (0, 1), (2, 0), (1, 1), (3, 1), (2, 1)]


def block_at(c, j, g):
    x_lo, y = j // 4, j % 4
    z2, z1, z0, k = g // 8, g // 4 % 2, g // 2 % 2, g % 2
    first, second = 2 * k + x_lo, y
    a = jnp.where(c == 0, first, second)
    b = jnp.where(c == 0, second, first)
    return z0 * 64 + a * 16 + z1 * 8 + b * 2 + z2


def gradient_kernel(rows, core_ref, mine_ref, theirs_ref, my_cot_ref, their_cot_ref, out_ref):
    c, j = core_ref[0], pl.program_id(0)
    dims = (((0,), (0,)), ((), ()))
    total = lax.dot_general(mine_ref[...], my_cot_ref[...], dims, preferred_element_type=jnp.float32)
    total += lax.dot_general(theirs_ref[...], their_cot_ref[...], dims, preferred_element_type=jnp.float32)
    total = total.astype(out_ref.dtype)
    for g in range(total.shape[0] // rows):
        out_ref[block_at(c, j, g)] = total[g * rows : (g + 1) * rows]


def gradient_blocks(core, tokens, theirs, my_cot, their_cot, rows):
    t, f = my_cot.shape
    half = theirs.shape[1]
    wide = 16 * rows
    steps = half // wide
    return pl.pallas_call(
        functools.partial(gradient_kernel, rows),
        grid_spec=pltpu.PrefetchScalarGridSpec(
            num_scalar_prefetch=1,
            grid=(steps,),
            in_specs=[
                pl.BlockSpec((t, wide), lambda j, core: (0, core[0] * steps + j)),
                pl.BlockSpec((t, wide), lambda j, core: (0, j)),
                pl.BlockSpec((t, f), lambda j, core: (0, 0)),
                pl.BlockSpec((t, f), lambda j, core: (0, 0)),
            ],
            out_specs=pl.BlockSpec((half // rows, rows, f), lambda j, core: (0, 0, 0)),
        ),
        out_shape=jax.ShapeDtypeStruct((half // rows, rows, f), jnp.bfloat16),
        compiler_params=pltpu.CompilerParams(vmem_limit_bytes=VMEM_LIMIT),
        cost_estimate=pl.CostEstimate(
            flops=4 * t * half * f, bytes_accessed=4 * t * half + 2 * half * f, transcendentals=0
        ),
        name="gradient_blocks",
    )(core, tokens, theirs, my_cot, their_cot)


def place_kernel(where_ref, *refs):
    out_ref = refs[-1]
    for i, ref in enumerate(refs[:-1]):
        out_ref[where_ref[i]] = ref[...]


def place(where, pieces):
    n = len(pieces)
    return pl.pallas_call(
        place_kernel,
        in_specs=[pl.BlockSpec(memory_space=pltpu.SMEM)] + [pl.BlockSpec(memory_space=pltpu.VMEM)] * n,
        out_specs=pl.BlockSpec(memory_space=pltpu.VMEM),
        out_shape=jax.ShapeDtypeStruct((n,) + pieces[0].shape, pieces[0].dtype),
        name="place",
    )(where, *pieces)


def forward_kernel(rows, n, at_ref, mine_ref, theirs_ref, *refs):
    pieces, (my_out, their_out, weights, total, sems) = refs[:n], refs[n:]
    c, j = at_ref[n], pl.program_id(0)
    t = mine_ref.shape[0]

    @pl.when(j == 0)
    def _():
        copies = [
            pltpu.make_async_copy(piece, weights.at[at_ref[i]], sems.at[i]) for i, piece in enumerate(pieces)
        ]
        for copy in copies:
            copy.start()
        total[...] = jnp.zeros_like(total)
        for copy in copies:
            copy.wait()

    blocks = []
    for g in range(mine_ref.shape[1] // rows):
        at = block_at(c, j, g)
        blocks.append(weights[at // 16, at % 16])
    chunk = jnp.concatenate(blocks, axis=0)
    total[:t] += jnp.dot(mine_ref[...], chunk, preferred_element_type=jnp.float32)
    total[t:] += jnp.dot(theirs_ref[...], chunk, preferred_element_type=jnp.float32)

    @pl.when(j == pl.num_programs(0) - 1)
    def _():
        my_out[...] = total[:t]
        their_out[...] = total[t:].astype(their_out.dtype)


def forward(at, tokens, theirs, pieces, rows):
    t, half = theirs.shape
    n, per, _, f = (len(pieces),) + pieces[0].shape
    wide = 16 * rows
    steps = half // wide
    return pl.pallas_call(
        functools.partial(forward_kernel, rows, n),
        grid_spec=pltpu.PrefetchScalarGridSpec(
            num_scalar_prefetch=1,
            grid=(steps,),
            in_specs=[
                pl.BlockSpec((t, wide), lambda j, at: (0, at[n] * steps + j)),
                pl.BlockSpec((t, wide), lambda j, at: (0, j)),
            ]
            + [pl.BlockSpec(memory_space=pl.ANY)] * n,
            out_specs=[pl.BlockSpec((t, f), lambda j, at: (0, 0))] * 2,
            scratch_shapes=[
                pltpu.VMEM((n, per, rows, f), jnp.bfloat16),
                pltpu.VMEM((2 * t, f), jnp.float32),
                pltpu.SemaphoreType.DMA((n,)),
            ],
        ),
        out_shape=[
            jax.ShapeDtypeStruct((t, f), jnp.float32),
            jax.ShapeDtypeStruct((t, f), jnp.bfloat16),
        ],
        compiler_params=pltpu.CompilerParams(vmem_limit_bytes=VMEM_LIMIT),
        cost_estimate=pl.CostEstimate(
            flops=4 * t * half * f, bytes_accessed=4 * t * half + 2 * half * f, transcendentals=0
        ),
        name="forward",
    )(at, tokens, theirs, *pieces)


def summed(stacked):
    return stacked.astype(jnp.float32).sum(axis=0)


def on_device(tokens, cotangent, next_tokens, master, moment_one, moment_two):
    rows, f = master.shape
    t, d = tokens.shape
    half = d // 2
    me = lax.axis_index("grp") * 32 + lax.axis_index("intra")
    x, y, z, c = coordinates(me)
    other_core = lambda v: permute(v, lambda d: d ^ 1)

    def other_half(v):
        return jnp.where(c == 0, v[:, half:], v[:, :half])

    theirs = other_core(other_half(tokens))
    their_cot = other_core(cotangent)
    core = jnp.reshape(c, (1,)).astype(jnp.int32)

    partial = gradient_blocks(core, tokens, theirs, cotangent, their_cot, rows)
    partial = partial.reshape(8, 16, rows, f)
    partial = lax.all_to_all(partial, AXES, 0, 0, tiled=True, axis_index_groups=groups(True))
    partial = summed(partial).astype(jnp.bfloat16).reshape(8, 2, rows, f)
    partial = lax.all_to_all(partial, AXES, 0, 0, tiled=True, axis_index_groups=groups(False))
    partial = summed(partial)
    z2 = z // 4
    same = jnp.where(z2 == 0, partial[0], partial[1]).astype(jnp.bfloat16)
    twin = jnp.where(z2 == 0, partial[1], partial[0]).astype(jnp.bfloat16)
    same = permute(same, lambda d: home(d, 0))
    twin = permute(twin, lambda d: home(d, 1))
    total = same.astype(jnp.float32) + twin.astype(jnp.float32)

    gradient = total * (1.0 / (t * DEVICES))
    new_moment_one = 0.9 * moment_one + 0.1 * gradient
    new_moment_two = 0.999 * moment_two + 0.001 * gradient * gradient
    first = new_moment_one / (1.0 - 0.9**10)
    second = new_moment_two / (1.0 - 0.999**10)
    new_master = master - 0.01 * (first / (jnp.sqrt(second) + 1e-08) + 0.1 * master)
    weights = new_master.astype(jnp.bfloat16)

    next_theirs = other_core(other_half(next_tokens))
    same = permute(weights, lambda d: home(d, 0))
    twin = permute(weights, lambda d: home(d, 1))
    two = jnp.where(z2 == 0, jnp.stack([same, twin]), jnp.stack([twin, same]))
    offsets = OFFSETS + [(0, 0)]

    def places(a, parity):
        return [(parity ^ dz) * 4 + (a - da) % 4 for da, dz in offsets]

    a, b = jnp.where(c == 0, x, y), jnp.where(c == 0, y, x)
    pieces = [permute(two, lambda d: neighbour(d, da, dz, False)) for da, dz in OFFSETS] + [two]
    where = jnp.stack(places(b, z // 2 % 2)).astype(jnp.int32)
    sixteen = place(where, pieces).reshape(16, rows, f)
    pieces = [permute(sixteen, lambda d: neighbour(d, da, dz, True)) for da, dz in OFFSETS] + [sixteen]
    at = jnp.stack(places(a, z % 2) + [c]).astype(jnp.int32)
    my_out, their_out = forward(at, next_tokens, next_theirs, pieces, rows)
    result = my_out + other_core(their_out).astype(jnp.float32)
    return (new_master, new_moment_one, new_moment_two, result.astype(jnp.bfloat16))


def solution(mesh):
    spec = P(AXES, None)
    return jax.shard_map(on_device, mesh=mesh, in_specs=(spec,) * 6, out_specs=(spec,) * 4, check_vma=False)
```

time: 1440 us -> 169 us (0.12)
  waiting for transfers between devices: 1370 us -> 57.7 us
  starting transfers between devices: 0.08 us -> 37.9 us
  Pallas kernels: 0 us -> 18.7 us
  matrix products: 17.2 us -> 0 us
    reduce_scatter x1 -> x0, waiting for transfers between devices: 1290 us -> none  [on_device(): lax.psum_scatter(lax.dot_general(tokens, cotangent, (((0,), (0,)), ((), (...]
    all_gather x1 -> x0, waiting for transfers between devices: 77.8 us -> none  [on_device(): lax.all_gather(copies, 'intra', axis=1, tiled=True)]
    ppermute x0 -> x22, waiting for transfers between devices: none -> 50 us  [permute(): return lax.ppermute(value, AXES, [(d, target(d)) for d in range(DEVICES)])]
    all_to_all x0 -> x1, blocking collectives: none -> 36.2 us  [on_device(): lax.all_to_all(partial, AXES, 0, 0, tiled=True, axis_index_groups=groups(...]
    ppermute x0 -> x22, starting transfers between devices: none -> 33.9 us  [permute(): return lax.ppermute(value, AXES, [(d, target(d)) for d in range(DEVICES)])]
    all_gather x1 -> x0, blocking collectives: 30 us -> none  [on_device(): copies = lax.all_gather(weights[None], 'grp', axis=0, tiled=True)]
    pallas_call x0 -> x3, Pallas kernels: none -> 18.7 us  [the longest x1 8.52 us: forward(): pl.pallas_call(functools.partial(forward_kernel, rows, n), grid_spec=pltp...]
    dot_general x2 -> x0, matrix products: 17.2 us -> none  [the longest x1 10.3 us: on_device(): lax.dot_general(tokens, cotangent, (((0,), (0,)), ((), ())), preferred_el...]
  transfers between devices with their start and end apart: 2 -> 23, of which waited for: 2 -> 12; matrix products, arithmetic and copies ran while one was open for 0% -> 3% of each run, Pallas kernels for 0% -> 1%
where the time goes in v1:
time: 169 us; the launch traced here: 166 us
  waiting for transfers between devices  57.7 us (34%)
  starting transfers between devices  37.9 us (22%)
  blocking collectives  36.2 us (21%)
  Pallas kernels  18.7 us (11%)
  other arithmetic  11.8 us (7%)
  local copies, waits for them, and re-layouts  2.43 us (1%)
    ppermute x22, waiting for transfers between devices, permute(): return lax.ppermute(value, AXES, [(d, target(d)) for d in range(DEVICES)])  50 us
    all_to_all x1, blocking collectives, on_device(): lax.all_to_all(partial, AXES, 0, 0, tiled=True, axis_index_groups=groups(...  36.2 us
    ppermute x22, starting transfers between devices, permute(): return lax.ppermute(value, AXES, [(d, target(d)) for d in range(DEVICES)])  33.9 us
    pallas_call x1, Pallas kernels, forward(): pl.pallas_call(functools.partial(forward_kernel, rows, n), grid_spec=pltp...  8.52 us
    pallas_call x1, Pallas kernels, gradient_blocks(): pl.pallas_call(functools.partial(gradient_kernel, rows), grid_spec=pltpu....  8.29 us
    all_to_all x1, waiting for transfers between devices, on_device(): lax.all_to_all(partial, AXES, 0, 0, tiled=True, axis_index_groups=groups(...  7.7 us
    select_n x2, other arithmetic, other_half(): return jnp.where(c == 0, v[:, half:], v[:, :half])  6.31 us
    all_to_all x1, starting transfers between devices, on_device(): lax.all_to_all(partial, AXES, 0, 0, tiled=True, axis_index_groups=groups(...  4.03 us
  transfers between devices with their start and end apart: 23, of which 12 were waited for; matrix products, arithmetic and copies ran while one was open for 3% of the time, Pallas kernels for 1%

profile of v1, /device:TPU:1, one launch (start us, length us, event | category | flops | bytes accessed | tf_op | source)
XLA Modules:
  0.0 165.7 jit_solution(10303035111149875108)
XLA Ops:
  0.7 2.5 %slice_select_fusion.1 = bf16[256,4096]{1,0:T(8,128)(2,1)S(1)} fusion(bf16[256,8192]{1,0:T(8,128)(2,1)} %mine_ref.2, pred[]{:T(512)S(6)} %eq.34), kind=kLoop, calls=%fused_computation.1 | loop fusion | flops 1048576 | bytes 6291457 | tf_op jit(solution)/shard_map/jit(_where)/select_n | solution.py:208
  3.1 3.3 %collective-permute-start = (bf16[256,4096]{1,0:T(8,128)(2,1)S(1)}, bf16[256,4096]{1,0:T(8,128)(2,1)S(1)}, u32[]{:S(2)}, u32[]{:S(2)}) collective-permute-start(bf16[256,4096]{1,0:T(8,128)(2,1)S(1)} %slice_select_fusion.1), channel_id=1, source_target_pairs={{0,1},{1,0},{2,3},{3,2},{4,5},{5,4},{6,7},{7,6},{8,9},{9,8},{10,11... | collective-permute-start | bytes 6291464 | tf_op jit(solution)/shard_map/ppermute | solution.py:62
  6.6 4.1 %collective-permute-done.1.their_cot_ref = bf16[256,512]{1,0:T(8,128)(2,1)S(1)} collective-permute-done((bf16[256,512]{1,0:T(8,128)(2,1)S(1)}, bf16[256,512]{1,0:T(8,128)(2,1)S(1)}, u32[]{:S(2)}, u32[]{:S(2)}) %collective-permute-start.1) | collective-permute-done | bytes 262176 | tf_op jit(solution)/shard_map/ppermute | solution.py:62
  10.6 8.3 %gradient_blocks.1 = bf16[128,32,512]{2,1,0:T(8,128)(2,1)} custom-call(s32[1]{0:T(128)} %bitcast.core_ref, bf16[256,8192]{1,0:T(8,128)(2,1)} %mine_ref.2, bf16[256,4096]{1,0:T(8,128)(2,1)S(1)} %collective-permute-done.theirs_ref, bf16[256,512]{1,0:T(8,128)(2,1)S(1)} %copy-done.1, bf16[256,512]{1,0:T(8,128)(2,1)S(1)} %collective-permute-done.1.their_cot_ref), custom_call_target="tpu_custom_call" | custom-call | flops 2147483648 | bytes 8388608 | tf_op jit(solution)/shard_map/gradient_blocks/pallas_call | solution.py:92
  18.9 36.2 %all_to_all.10 = bf16[8,16,32,512]{3,2,1,0:T(8,128)(2,1)} all-to-all(bf16[8,16,32,512]{3,2,1,0:T(8,128)(2,1)} %bitcast.34), channel_id=1, replica_groups={{0,64,128,192,2,66,130,194},{1,17,33,49,15,31,47,63},{5,21,37,53,3,19,3..., dimensions={0} | all-to-all | bytes 8388608 | tf_op jit(solution)/shard_map/all_to_all | solution.py:216
  55.1 3.9 %reduce_sum.21 = bf16[16,32,512]{2,1,0:T(8,128)(2,1)} reduce(bf16[8,16,32,512]{3,2,1,0:T(8,128)(2,1)} %all_to_all.10, bf16[]{:T(256)} %constant.168.clone.1), dimensions={0}, to_apply=%region_0.1 | reduce | flops 1835008 | bytes 4718594 | tf_op jit(solution)/shard_map/reduce_sum | solution.py:196
  59.0 4.0 %all-to-all-start.1 = ((bf16[8,2,32,512]{3,2,1,0:T(8,128)(2,1)}), bf16[8,2,32,512]{3,2,1,0:T(8,128)(2,1)S(1)}, u32[]{:S(2)}, u32[]{:S(2)}) async-start(bf16[8,2,32,512]{3,2,1,0:T(8,128)(2,1)} %bitcast.2), calls=%async_computation.1 | async-start | bytes 1048576 | tf_op jit(solution)/shard_map/all_to_all | solution.py:218
  63.1 3.8 %slice_select_fusion = bf16[256,4096]{1,0:T(8,128)(2,1)} fusion(bf16[256,8192]{1,0:T(8,128)(2,1)} %mine_ref.3, pred[]{:T(512)S(6)} %eq.34), kind=kLoop, calls=%fused_computation | loop fusion | flops 1048576 | bytes 6291457 | tf_op jit(solution)/shard_map/jit(_where)/select_n | solution.py:208
  66.9 7.7 %all-to-all-done.1 = bf16[8,2,32,512]{3,2,1,0:T(8,128)(2,1)S(1)} async-done(((bf16[8,2,32,512]{3,2,1,0:T(8,128)(2,1)}), bf16[8,2,32,512]{3,2,1,0:T(8,128)(2,1)S(1)}, u32[]{:S(2)}, u32[]{:S(2)}) %all-to-all-start.1) | async-done | bytes 524320 | tf_op jit(solution)/shard_map/all_to_all | solution.py:218
  74.7 4.3 %collective-permute-start.3 = (bf16[32,512]{1,0:T(8,128)(2,1)S(1)}, bf16[32,512]{1,0:T(8,128)(2,1)S(1)}, u32[]{:S(2)}, u32[]{:S(2)}) collective-permute-start(bf16[32,512]{1,0:T(8,128)(2,1)S(1)} %get-tuple-element.13), channel_id=1, source_target_pairs={{0,8},{1,136},{2,10},{3,138},{4,12},{5,140},{6,14},{7,142},{8,0},{... | collective-permute-start | bytes 98312 | tf_op jit(solution)/shard_map/ppermute | solution.py:62
  79.0 2.4 %collective-permute-start.2 = (bf16[32,512]{1,0:T(8,128)(2,1)S(1)}, bf16[32,512]{1,0:T(8,128)(2,1)S(1)}, u32[]{:S(2)}, u32[]{:S(2)}) collective-permute-start(bf16[32,512]{1,0:T(8,128)(2,1)S(1)} %get-tuple-element.12), channel_id=1, source_target_pairs={{0,0},{1,128},{2,2},{3,130},{4,4},{5,132},{6,6},{7,134},{8,8},{9,1... | collective-permute-start | bytes 98312 | tf_op jit(solution)/shard_map/ppermute | solution.py:62
  81.4 3.1 %collective-permute-done.3 = bf16[32,512]{1,0:T(8,128)(2,1)S(1)} collective-permute-done((bf16[32,512]{1,0:T(8,128)(2,1)S(1)}, bf16[32,512]{1,0:T(8,128)(2,1)S(1)}, u32[]{:S(2)}, u32[]{:S(2)}) %collective-permute-start.3) | collective-permute-done | bytes 32800 | tf_op jit(solution)/shard_map/ppermute | solution.py:62
  84.5 1.2 collective-permute-done.2
  86.4 3.8 %collective-permute-start.6 = (bf16[32,512]{1,0:T(8,128)(2,1)S(1)}, bf16[32,512]{1,0:T(8,128)(2,1)S(1)}, u32[]{:S(2)}, u32[]{:S(2)}) collective-permute-start(bf16[32,512]{1,0:T(8,128)(2,1)S(1)} %get-tuple-element.8), channel_id=1, source_target_pairs={{0,8},{1,136},{2,10},{3,138},{4,12},{5,140},{6,14},{7,142},{8,0},{... | collective-permute-start | bytes 98312 | tf_op jit(solution)/shard_map/ppermute | solution.py:62
  90.3 2.3 %collective-permute-start.5 = (bf16[32,512]{1,0:T(8,128)(2,1)S(1)}, bf16[32,512]{1,0:T(8,128)(2,1)S(1)}, u32[]{:S(2)}, u32[]{:S(2)}) collective-permute-start(bf16[32,512]{1,0:T(8,128)(2,1)S(1)} %get-tuple-element.8), channel_id=1, source_target_pairs={{0,0},{1,128},{2,2},{3,130},{4,4},{5,132},{6,6},{7,134},{8,8},{9,1... | collective-permute-start | bytes 98312 | tf_op jit(solution)/shard_map/ppermute | solution.py:62
  92.6 3.5 %collective-permute-done.6 = bf16[32,512]{1,0:T(8,128)(2,1)S(1)} collective-permute-done((bf16[32,512]{1,0:T(8,128)(2,1)S(1)}, bf16[32,512]{1,0:T(8,128)(2,1)S(1)}, u32[]{:S(2)}, u32[]{:S(2)}) %collective-permute-start.6) | collective-permute-done | bytes 32800 | tf_op jit(solution)/shard_map/ppermute | solution.py:62
  97.1 2.7 %collective-permute-start.8 = (bf16[2,32,512]{2,1,0:T(8,128)(2,1)S(1)}, bf16[2,32,512]{2,1,0:T(8,128)(2,1)S(1)}, u32[]{:S(2)}, u32[]{:S(2)}) collective-permute-start(bf16[2,32,512]{2,1,0:T(8,128)(2,1)S(1)} %maximum_select_fusion.refs_7_), channel_id=1, source_target_pairs={{0,48},{1,193},{2,50},{3,195},{4,52},{5,197},{6,54},{7,199},{8,56}... | collective-permute-start | bytes 196616 | tf_op jit(solution)/shard_map/ppermute | solution.py:62
  99.8 1.6 collective-permute-done.7.refs_0_
  101.4 2.2 %collective-permute-start.11 = (bf16[2,32,512]{2,1,0:T(8,128)(2,1)S(1)}, bf16[2,32,512]{2,1,0:T(8,128)(2,1)S(1)}, u32[]{:S(2)}, u32[]{:S(2)}) collective-permute-start(bf16[2,32,512]{2,1,0:T(8,128)(2,1)S(1)} %maximum_select_fusion.refs_7_), channel_id=1, source_target_pairs={{0,20},{1,77},{2,22},{3,79},{4,16},{5,73},{6,18},{7,75},{8,28},{9,... | collective-permute-start | bytes 196616 | tf_op jit(solution)/shard_map/ppermute | solution.py:62
  103.6 3.5 %collective-permute-start.12 = (bf16[2,32,512]{2,1,0:T(8,128)(2,1)S(1)}, bf16[2,32,512]{2,1,0:T(8,128)(2,1)S(1)}, u32[]{:S(2)}, u32[]{:S(2)}) collective-permute-start(bf16[2,32,512]{2,1,0:T(8,128)(2,1)S(1)} %maximum_select_fusion.refs_7_), channel_id=1, source_target_pairs={{0,52},{1,205},{2,54},{3,207},{4,48},{5,201},{6,50},{7,203},{8,60}... | collective-permute-start | bytes 196616 | tf_op jit(solution)/shard_map/ppermute | solution.py:62
  107.1 3.4 %collective-permute-start.13 = (bf16[2,32,512]{2,1,0:T(8,128)(2,1)S(1)}, bf16[2,32,512]{2,1,0:T(8,128)(2,1)S(1)}, u32[]{:S(2)}, u32[]{:S(2)}) collective-permute-start(bf16[2,32,512]{2,1,0:T(8,128)(2,1)S(1)} %maximum_select_fusion.refs_7_), channel_id=1, source_target_pairs={{0,36},{1,141},{2,38},{3,143},{4,32},{5,137},{6,34},{7,139},{8,44}... | collective-permute-start | bytes 196616 | tf_op jit(solution)/shard_map/ppermute | solution.py:62
  111.2 4.1 %collective-permute-done.13.refs_6_ = bf16[2,32,512]{2,1,0:T(8,128)(2,1)S(1)} collective-permute-done((bf16[2,32,512]{2,1,0:T(8,128)(2,1)S(1)}, bf16[2,32,512]{2,1,0:T(8,128)(2,1)S(1)}, u32[]{:S(2)}, u32[]{:S(2)}) %collective-permute-start.13) | collective-permute-done | bytes 65568 | tf_op jit(solution)/shard_map/ppermute | solution.py:62
  116.0 1.9 %place.1 = bf16[8,2,32,512]{3,2,1,0:T(8,128)(2,1)} custom-call(s32[8]{0:T(128)} %stack.86.where_ref, bf16[2,32,512]{2,1,0:T(8,128)(2,1)} %copy-done.6, bf16[2,32,512]{2,1,0:T(8,128)(2,1)} %copy-done.7, bf16[2,32,512]{2,1,0:T(8,128)(2,1)} %copy-done.8, bf16[2,32,512]{2,1,0:T(8,128)(2,1)} %copy-done.9, bf16[2,32,512]{2,1,0:T(8,128)(2,1)} %copy-done.10, ...), custom_call_target="tpu_custom_call" | custom-call | tf_op jit(solution)/shard_map/place/pallas_call | solution.py:122
  117.9 2.7 %collective-permute-start.15 = (bf16[16,32,512]{2,1,0:T(8,128)(2,1)}, bf16[16,32,512]{2,1,0:T(8,128)(2,1)S(1)}, u32[]{:S(2)}, u32[]{:S(2)}) collective-permute-start(bf16[16,32,512]{2,1,0:T(8,128)(2,1)} %bitcast.27), channel_id=1, source_target_pairs={{0,192},{1,49},{2,194},{3,51},{4,196},{5,53},{6,198},{7,55},{8,200... | collective-permute-start | bytes 1572872 | tf_op jit(solution)/shard_map/ppermute | solution.py:62
  121.5 1.1 collective-permute-start.17
  122.6 0.9 collective-permute-start.18
  123.6 15.3 %collective-permute-done.14.refs_0_ = bf16[16,32,512]{2,1,0:T(8,128)(2,1)S(1)} collective-permute-done((bf16[16,32,512]{2,1,0:T(8,128)(2,1)}, bf16[16,32,512]{2,1,0:T(8,128)(2,1)S(1)}, u32[]{:S(2)}, u32[]{:S(2)}) %collective-permute-start.14) | collective-permute-done | bytes 524320 | tf_op jit(solution)/shard_map/ppermute | solution.py:62
  139.1 10.5 %collective-permute-done.19.refs_5_ = bf16[16,32,512]{2,1,0:T(8,128)(2,1)S(1)} collective-permute-done((bf16[16,32,512]{2,1,0:T(8,128)(2,1)}, bf16[16,32,512]{2,1,0:T(8,128)(2,1)S(1)}, u32[]{:S(2)}, u32[]{:S(2)}) %collective-permute-start.19) | collective-permute-done | bytes 524320 | tf_op jit(solution)/shard_map/ppermute | solution.py:62
  149.7 4.1 %collective-permute-done.20.refs_6_ = bf16[16,32,512]{2,1,0:T(8,128)(2,1)} collective-permute-done((bf16[16,32,512]{2,1,0:T(8,128)(2,1)}, bf16[16,32,512]{2,1,0:T(8,128)(2,1)}, u32[]{:S(2)}, u32[]{:S(2)}) %collective-permute-start.20) | collective-permute-done | bytes 524320 | tf_op jit(solution)/shard_map/ppermute | solution.py:62
  153.8 1.0 copy-done
  154.8 8.5 %forward.1 = (f32[256,512]{1,0:T(8,128)S(1)}, bf16[256,512]{1,0:T(8,128)(2,1)S(1)}) custom-call(s32[9]{0:T(128)S(1)} %stack.77.at_ref, bf16[256,8192]{1,0:T(8,128)(2,1)} %mine_ref.3, bf16[256,4096]{1,0:T(8,128)(2,1)} %collective-permute-done.4.theirs_ref, bf16[16,32,512]{2,1,0:T(8,128)(2,1)S(1)} %collective-permute-done.14.refs_0_, ...), custom_call_target="tpu_custom_call" | custom-call | flops 2147483648 | bytes 8388608 | tf_op jit(solution)/shard_map/forward/pallas_call | solution.py:166
  163.4 1.5 collective-permute-done.21
  (54 shorter events, 5.2 us)
Async XLA Ops:
  0.6 5.8 %copy-start.1 = (bf16[256,512]{1,0:T(8,128)(2,1)S(1)}, bf16[256,512]{1,0:T(8,128)(2,1)}, u32[]{:S(2)}) copy-start(bf16[256,512]{1,0:T(8,128)(2,1)} %my_cot_ref.1) | copy-start | bytes 786436
  3.1 7.5 %collective-permute-start = (bf16[256,4096]{1,0:T(8,128)(2,1)S(1)}, bf16[256,4096]{1,0:T(8,128)(2,1)S(1)}, u32[]{:S(2)}, u32[]{:S(2)}) collective-permute-start(bf16[256,4096]{1,0:T(8,128)(2,1)S(1)} %slice_select_fusion.1), channel_id=1, source_target_pairs={{0,1},{1,0},{2,3},{3,2},{4,5},{5,4},{6,7},{7,6},{8,9},{9,8},{10,11... | collective-permute-start | bytes 6291464 | tf_op jit(solution)/shard_map/ppermute | solution.py:62
  6.5 4.2 %collective-permute-start.1 = (bf16[256,512]{1,0:T(8,128)(2,1)S(1)}, bf16[256,512]{1,0:T(8,128)(2,1)S(1)}, u32[]{:S(2)}, u32[]{:S(2)}) collective-permute-start(bf16[256,512]{1,0:T(8,128)(2,1)S(1)} %copy-done.1), channel_id=1, source_target_pairs={{0,1},{1,0},{2,3},{3,2},{4,5},{5,4},{6,7},{7,6},{8,9},{9,8},{10,11... | collective-permute-start | bytes 786440 | tf_op jit(solution)/shard_map/ppermute | solution.py:62
  59.0 15.6 %all-to-all-start.1 = ((bf16[8,2,32,512]{3,2,1,0:T(8,128)(2,1)}), bf16[8,2,32,512]{3,2,1,0:T(8,128)(2,1)S(1)}, u32[]{:S(2)}, u32[]{:S(2)}) async-start(bf16[8,2,32,512]{3,2,1,0:T(8,128)(2,1)} %bitcast.2), calls=%async_computation.1 | async-start | bytes 1048576 | tf_op jit(solution)/shard_map/all_to_all | solution.py:218
  63.0 22.7 %copy-start.3 = (f32[32,512]{1,0:T(8,128)S(1)}, f32[32,512]{1,0:T(8,128)}, u32[]{:S(2)}) copy-start(f32[32,512]{1,0:T(8,128)} %param.9) | copy-start | bytes 196612
  63.0 22.7 %copy-start.4 = (f32[32,512]{1,0:T(8,128)S(1)}, f32[32,512]{1,0:T(8,128)}, u32[]{:S(2)}) copy-start(f32[32,512]{1,0:T(8,128)} %param.10) | copy-start | bytes 196612
  63.0 22.7 %copy-start.5 = (f32[32,512]{1,0:T(8,128)S(1)}, f32[32,512]{1,0:T(8,128)}, u32[]{:S(2)}) copy-start(f32[32,512]{1,0:T(8,128)} %param.11) | copy-start | bytes 196612
  66.9 55.8 %collective-permute-start.4 = (bf16[256,4096]{1,0:T(8,128)(2,1)}, bf16[256,4096]{1,0:T(8,128)(2,1)}, u32[]{:S(2)}, u32[]{:S(2)}) collective-permute-start(bf16[256,4096]{1,0:T(8,128)(2,1)} %slice_select_fusion), channel_id=1, source_target_pairs={{0,1},{1,0},{2,3},{3,2},{4,5},{5,4},{6,7},{7,6},{8,9},{9,8},{10,11... | collective-permute-start | bytes 6291464 | tf_op jit(solution)/shard_map/ppermute | solution.py:62
  74.7 9.8 %collective-permute-start.3 = (bf16[32,512]{1,0:T(8,128)(2,1)S(1)}, bf16[32,512]{1,0:T(8,128)(2,1)S(1)}, u32[]{:S(2)}, u32[]{:S(2)}) collective-permute-start(bf16[32,512]{1,0:T(8,128)(2,1)S(1)} %get-tuple-element.13), channel_id=1, source_target_pairs={{0,8},{1,136},{2,10},{3,138},{4,12},{5,140},{6,14},{7,142},{8,0},{... | collective-permute-start | bytes 98312 | tf_op jit(solution)/shard_map/ppermute | solution.py:62
  79.0 6.7 %collective-permute-start.2 = (bf16[32,512]{1,0:T(8,128)(2,1)S(1)}, bf16[32,512]{1,0:T(8,128)(2,1)S(1)}, u32[]{:S(2)}, u32[]{:S(2)}) collective-permute-start(bf16[32,512]{1,0:T(8,128)(2,1)S(1)} %get-tuple-element.12), channel_id=1, source_target_pairs={{0,0},{1,128},{2,2},{3,130},{4,4},{5,132},{6,6},{7,134},{8,8},{9,1... | collective-permute-start | bytes 98312 | tf_op jit(solution)/shard_map/ppermute | solution.py:62
  86.4 9.7 %collective-permute-start.6 = (bf16[32,512]{1,0:T(8,128)(2,1)S(1)}, bf16[32,512]{1,0:T(8,128)(2,1)S(1)}, u32[]{:S(2)}, u32[]{:S(2)}) collective-permute-start(bf16[32,512]{1,0:T(8,128)(2,1)S(1)} %get-tuple-element.8), channel_id=1, source_target_pairs={{0,8},{1,136},{2,10},{3,138},{4,12},{5,140},{6,14},{7,142},{8,0},{... | collective-permute-start | bytes 98312 | tf_op jit(solution)/shard_map/ppermute | solution.py:62
  90.3 6.7 %collective-permute-start.5 = (bf16[32,512]{1,0:T(8,128)(2,1)S(1)}, bf16[32,512]{1,0:T(8,128)(2,1)S(1)}, u32[]{:S(2)}, u32[]{:S(2)}) collective-permute-start(bf16[32,512]{1,0:T(8,128)(2,1)S(1)} %get-tuple-element.8), channel_id=1, source_target_pairs={{0,0},{1,128},{2,2},{3,130},{4,4},{5,132},{6,6},{7,134},{8,8},{9,1... | collective-permute-start | bytes 98312 | tf_op jit(solution)/shard_map/ppermute | solution.py:62
  97.0 18.3 %copy-start.2 = (bf16[2,32,512]{2,1,0:T(8,128)(2,1)}, bf16[2,32,512]{2,1,0:T(8,128)(2,1)S(1)}, u32[]{:S(2)}) copy-start(bf16[2,32,512]{2,1,0:T(8,128)(2,1)S(1)} %maximum_select_fusion.refs_7_) | copy-start | bytes 196612
  97.0 4.4 %collective-permute-start.7 = (bf16[2,32,512]{2,1,0:T(8,128)(2,1)S(1)}, bf16[2,32,512]{2,1,0:T(8,128)(2,1)S(1)}, u32[]{:S(2)}, u32[]{:S(2)}) collective-permute-start(bf16[2,32,512]{2,1,0:T(8,128)(2,1)S(1)} %maximum_select_fusion.refs_7_), channel_id=1, source_target_pairs={{0,16},{1,65},{2,18},{3,67},{4,20},{5,69},{6,22},{7,71},{8,24},{9,... | collective-permute-start | bytes 196616 | tf_op jit(solution)/shard_map/ppermute | solution.py:62
  97.1 6.5 %collective-permute-start.8 = (bf16[2,32,512]{2,1,0:T(8,128)(2,1)S(1)}, bf16[2,32,512]{2,1,0:T(8,128)(2,1)S(1)}, u32[]{:S(2)}, u32[]{:S(2)}) collective-permute-start(bf16[2,32,512]{2,1,0:T(8,128)(2,1)S(1)} %maximum_select_fusion.refs_7_), channel_id=1, source_target_pairs={{0,48},{1,193},{2,50},{3,195},{4,52},{5,197},{6,54},{7,199},{8,56}... | collective-permute-start | bytes 196616 | tf_op jit(solution)/shard_map/ppermute | solution.py:62
  99.8 7.3 %collective-permute-start.9 = (bf16[2,32,512]{2,1,0:T(8,128)(2,1)S(1)}, bf16[2,32,512]{2,1,0:T(8,128)(2,1)S(1)}, u32[]{:S(2)}, u32[]{:S(2)}) collective-permute-start(bf16[2,32,512]{2,1,0:T(8,128)(2,1)S(1)} %maximum_select_fusion.refs_7_), channel_id=1, source_target_pairs={{0,4},{1,13},{2,6},{3,15},{4,0},{5,9},{6,2},{7,11},{8,12},{9,5},{1... | collective-permute-start | bytes 196616 | tf_op jit(solution)/shard_map/ppermute | solution.py:62
  99.8 11.4 %collective-permute-start.10 = (bf16[2,32,512]{2,1,0:T(8,128)(2,1)S(1)}, bf16[2,32,512]{2,1,0:T(8,128)(2,1)S(1)}, u32[]{:S(2)}, u32[]{:S(2)}) collective-permute-start(bf16[2,32,512]{2,1,0:T(8,128)(2,1)S(1)} %maximum_select_fusion.refs_7_), channel_id=1, source_target_pairs={{0,32},{1,129},{2,34},{3,131},{4,36},{5,133},{6,38},{7,135},{8,40}... | collective-permute-start | bytes 196616 | tf_op jit(solution)/shard_map/ppermute | solution.py:62
  101.4 13.9 %copy-start.6 = (bf16[2,32,512]{2,1,0:T(8,128)(2,1)}, bf16[2,32,512]{2,1,0:T(8,128)(2,1)S(1)}, u32[]{:S(2)}) copy-start(bf16[2,32,512]{2,1,0:T(8,128)(2,1)S(1)} %collective-permute-done.7.refs_0_) | copy-start | bytes 196612
  101.4 9.7 %collective-permute-start.11 = (bf16[2,32,512]{2,1,0:T(8,128)(2,1)S(1)}, bf16[2,32,512]{2,1,0:T(8,128)(2,1)S(1)}, u32[]{:S(2)}, u32[]{:S(2)}) collective-permute-start(bf16[2,32,512]{2,1,0:T(8,128)(2,1)S(1)} %maximum_select_fusion.refs_7_), channel_id=1, source_target_pairs={{0,20},{1,77},{2,22},{3,79},{4,16},{5,73},{6,18},{7,75},{8,28},{9,... | collective-permute-start | bytes 196616 | tf_op jit(solution)/shard_map/ppermute | solution.py:62
  103.6 11.7 %copy-start.7 = (bf16[2,32,512]{2,1,0:T(8,128)(2,1)}, bf16[2,32,512]{2,1,0:T(8,128)(2,1)S(1)}, u32[]{:S(2)}) copy-start(bf16[2,32,512]{2,1,0:T(8,128)(2,1)S(1)} %collective-permute-done.8.refs_1_) | copy-start | bytes 196612
  103.6 7.5 %collective-permute-start.12 = (bf16[2,32,512]{2,1,0:T(8,128)(2,1)S(1)}, bf16[2,32,512]{2,1,0:T(8,128)(2,1)S(1)}, u32[]{:S(2)}, u32[]{:S(2)}) collective-permute-start(bf16[2,32,512]{2,1,0:T(8,128)(2,1)S(1)} %maximum_select_fusion.refs_7_), channel_id=1, source_target_pairs={{0,52},{1,205},{2,54},{3,207},{4,48},{5,201},{6,50},{7,203},{8,60}... | collective-permute-start | bytes 196616 | tf_op jit(solution)/shard_map/ppermute | solution.py:62
  107.1 8.2 %copy-start.8 = (bf16[2,32,512]{2,1,0:T(8,128)(2,1)}, bf16[2,32,512]{2,1,0:T(8,128)(2,1)S(1)}, u32[]{:S(2)}) copy-start(bf16[2,32,512]{2,1,0:T(8,128)(2,1)S(1)} %collective-permute-done.9.refs_2_) | copy-start | bytes 196612
  107.1 8.2 %collective-permute-start.13 = (bf16[2,32,512]{2,1,0:T(8,128)(2,1)S(1)}, bf16[2,32,512]{2,1,0:T(8,128)(2,1)S(1)}, u32[]{:S(2)}, u32[]{:S(2)}) collective-permute-start(bf16[2,32,512]{2,1,0:T(8,128)(2,1)S(1)} %maximum_select_fusion.refs_7_), channel_id=1, source_target_pairs={{0,36},{1,141},{2,38},{3,143},{4,32},{5,137},{6,34},{7,139},{8,44}... | collective-permute-start | bytes 196616 | tf_op jit(solution)/shard_map/ppermute | solution.py:62
  111.2 4.2 %copy-start.10 = (bf16[2,32,512]{2,1,0:T(8,128)(2,1)}, bf16[2,32,512]{2,1,0:T(8,128)(2,1)S(1)}, u32[]{:S(2)}) copy-start(bf16[2,32,512]{2,1,0:T(8,128)(2,1)S(1)} %collective-permute-done.11.refs_4_) | copy-start | bytes 196612
  117.9 21.0 %collective-permute-start.14 = (bf16[16,32,512]{2,1,0:T(8,128)(2,1)}, bf16[16,32,512]{2,1,0:T(8,128)(2,1)S(1)}, u32[]{:S(2)}, u32[]{:S(2)}) collective-permute-start(bf16[16,32,512]{2,1,0:T(8,128)(2,1)} %bitcast.26), channel_id=1, source_target_pairs={{0,64},{1,17},{2,66},{3,19},{4,68},{5,21},{6,70},{7,23},{8,72},{9,... | collective-permute-start | bytes 1572872 | tf_op jit(solution)/shard_map/ppermute | solution.py:62
  117.9 21.0 %collective-permute-start.15 = (bf16[16,32,512]{2,1,0:T(8,128)(2,1)}, bf16[16,32,512]{2,1,0:T(8,128)(2,1)S(1)}, u32[]{:S(2)}, u32[]{:S(2)}) collective-permute-start(bf16[16,32,512]{2,1,0:T(8,128)(2,1)} %bitcast.27), channel_id=1, source_target_pairs={{0,192},{1,49},{2,194},{3,51},{4,196},{5,53},{6,198},{7,55},{8,200... | collective-permute-start | bytes 1572872 | tf_op jit(solution)/shard_map/ppermute | solution.py:62
  120.6 18.5 %collective-permute-start.16 = (bf16[16,32,512]{2,1,0:T(8,128)(2,1)}, bf16[16,32,512]{2,1,0:T(8,128)(2,1)S(1)}, u32[]{:S(2)}, u32[]{:S(2)}) collective-permute-start(bf16[16,32,512]{2,1,0:T(8,128)(2,1)} %bitcast.28), channel_id=1, source_target_pairs={{0,2},{1,15},{2,0},{3,5},{4,6},{5,3},{6,4},{7,9},{8,10},{9,7},{10,... | collective-permute-start | bytes 1572872 | tf_op jit(solution)/shard_map/ppermute | solution.py:62
  121.5 17.6 %collective-permute-start.17 = (bf16[16,32,512]{2,1,0:T(8,128)(2,1)}, bf16[16,32,512]{2,1,0:T(8,128)(2,1)S(1)}, u32[]{:S(2)}, u32[]{:S(2)}) collective-permute-start(bf16[16,32,512]{2,1,0:T(8,128)(2,1)} %bitcast.29), channel_id=1, source_target_pairs={{0,128},{1,33},{2,130},{3,35},{4,132},{5,37},{6,134},{7,39},{8,136... | collective-permute-start | bytes 1572872 | tf_op jit(solution)/shard_map/ppermute | solution.py:62
  122.6 16.5 %collective-permute-start.18 = (bf16[16,32,512]{2,1,0:T(8,128)(2,1)}, bf16[16,32,512]{2,1,0:T(8,128)(2,1)S(1)}, u32[]{:S(2)}, u32[]{:S(2)}) collective-permute-start(bf16[16,32,512]{2,1,0:T(8,128)(2,1)} %bitcast.30), channel_id=1, source_target_pairs={{0,66},{1,31},{2,64},{3,21},{4,70},{5,19},{6,68},{7,25},{8,74},{9,... | collective-permute-start | bytes 1572872 | tf_op jit(solution)/shard_map/ppermute | solution.py:62
  138.9 10.8 %collective-permute-start.19 = (bf16[16,32,512]{2,1,0:T(8,128)(2,1)}, bf16[16,32,512]{2,1,0:T(8,128)(2,1)S(1)}, u32[]{:S(2)}, u32[]{:S(2)}) collective-permute-start(bf16[16,32,512]{2,1,0:T(8,128)(2,1)} %bitcast.31), channel_id=1, source_target_pairs={{0,194},{1,63},{2,192},{3,53},{4,198},{5,51},{6,196},{7,57},{8,202... | collective-permute-start | bytes 1572872 | tf_op jit(solution)/shard_map/ppermute | solution.py:62
  138.9 14.8 %collective-permute-start.20 = (bf16[16,32,512]{2,1,0:T(8,128)(2,1)}, bf16[16,32,512]{2,1,0:T(8,128)(2,1)}, u32[]{:S(2)}, u32[]{:S(2)}) collective-permute-start(bf16[16,32,512]{2,1,0:T(8,128)(2,1)} %bitcast.32), channel_id=1, source_target_pairs={{0,130},{1,47},{2,128},{3,37},{4,134},{5,35},{6,132},{7,41},{8,138... | collective-permute-start | bytes 1572872 | tf_op jit(solution)/shard_map/ppermute | solution.py:62
  163.3 1.6 collective-permute-start.21
  (4 other events, 10.0 us)

commit v2 on v0

v2 whole, which is shorter than its diff:
```python
import functools

import jax
import jax.numpy as jnp
from jax import lax
from jax.experimental import pallas as pl
from jax.experimental.pallas import tpu as pltpu
from jax.sharding import PartitionSpec as P

AXES = ("grp", "intra")
DEVICES = 256
SIZES = (4, 4, 8)
ORDER = ((0, 1, 2), (1, 2, 0), (2, 0, 1))
LANES = 128
VMEM_LIMIT = 24 * 1024 * 1024
FIRST_LIMIT = 48 * 1024 * 1024


def coordinates(d):
    return d // 64, d // 16 % 4, d // 2 % 8, d % 2


def flat(x, y, z, c):
    return x * 64 + y * 16 + z * 2 + c


def neighbour(d, axis):
    at, c = list(coordinates(d)[:3]), d % 2
    at[axis] = (at[axis] + (1 if at[axis] % 2 == c else -1)) % SIZES[axis]
    return flat(*at, c)


def permute(value, target):
    return lax.ppermute(value, AXES, [(d, target(d)) for d in range(DEVICES)])


def groups():
    seen = {}
    for d in range(DEVICES):
        x, y, z, c = coordinates(d)
        seen.setdefault((x % 2, y % 2, z % 2, c), []).append(d)
    return list(seen.values())


def part_rows(f):
    tiles = f // 16
    first = (tiles + 2) // 3 * 16
    return (first, first, f - 2 * first)


def place_in(part, rel, x1, y1):
    a, b, c = (rel[axis] for axis in ORDER[part])
    return a, (b * 2 + c) * 4 + x1 * 2 + y1


def sort_kernel(at_ref, in_ref, my_ref, other_ref, chunks, sems):
    c, x0, y0, z0 = (at_ref[i] for i in range(4))
    wide = chunks.shape[2]
    copies = []
    for i in range(4):
        start = pl.multiple_of((2 * (i % 2) + (x0 ^ (i // 2))) * wide, wide)
        copies.append(pltpu.make_async_copy(in_ref.at[:, pl.ds(start, wide)], chunks.at[i], sems.at[i]))
        copies[-1].start()
    n = 4 * LANES
    source = lax.broadcasted_iota(jnp.int32, (n, n), 0)
    goal = lax.broadcasted_iota(jnp.int32, (n, n), 1)
    q, r, row = goal // 128, goal // 32 % 4, goal % 32
    wanted = r * 128 + (((q % 2) ^ z0) * 2 + ((q // 2) ^ c)) * 32 + row
    move = jnp.where(source == wanted, 1.0, 0.0).astype(my_ref.dtype)
    for i in range(4):
        copies[i].wait()
        for y in range(4):
            turned = jnp.dot(chunks[i, :, y * n : (y + 1) * n], move, preferred_element_type=jnp.float32)
            turned = turned.astype(my_ref.dtype)
            where = (y0 ^ (y % 2)) * 4 + (y // 2) * 2
            for rz in range(2):
                my_ref[i, where + rz] = turned[:, rz * LANES : (rz + 1) * LANES]
                other_ref[i, where + rz] = turned[:, (2 + rz) * LANES : (3 + rz) * LANES]


def sort_columns(at, tokens, limit):
    t, d = tokens.shape
    space = pl.BlockSpec(memory_space=pltpu.VMEM)
    return pl.pallas_call(
        sort_kernel,
        in_specs=[pl.BlockSpec(memory_space=pltpu.SMEM), pl.BlockSpec(memory_space=pl.ANY)],
        out_specs=[space, space],
        out_shape=[jax.ShapeDtypeStruct((4, 8, t, LANES), tokens.dtype)] * 2,
        scratch_shapes=[pltpu.VMEM((4, t, d // 4), tokens.dtype), pltpu.SemaphoreType.DMA((4,))],
        compiler_params=pltpu.CompilerParams(vmem_limit_bytes=limit),
        cost_estimate=pl.CostEstimate(flops=8 * LANES * t * d, bytes_accessed=4 * t * d, transcendentals=0),
        name="sort_columns",
    )(at, tokens)


def gradient_kernel(parts, mine_ref, theirs_ref, my_cot_ref, their_cot_ref, *out_refs):
    cot = jnp.concatenate([my_cot_ref[...].T, their_cot_ref[...].T], axis=1)
    starts = [sum(parts[:p]) for p in range(3)]
    for rx in range(2):
        for x1 in range(2):
            for ry in range(2):
                blocks = [
                    jnp.concatenate([mine_ref[rx * 2 + x1, ry * 4 + i], theirs_ref[rx * 2 + x1, ry * 4 + i]], axis=0)
                    for i in range(4)
                ]
                total = jnp.dot(cot, jnp.concatenate(blocks, axis=1), preferred_element_type=jnp.float32)
                total = total.astype(jnp.bfloat16)
                for y1 in range(2):
                    for rz in range(2):
                        i = y1 * 2 + rz
                        for p in range(3):
                            half, at = place_in(p, (rx, ry, rz), x1, y1)
                            out_refs[2 * p + half][:, at * LANES : (at + 1) * LANES] = total[
                                starts[p] : starts[p] + parts[p], i * LANES : (i + 1) * LANES
                            ]


def vmem_call(kernel, outs, name, flops, *operands):
    size = sum(a.size * a.dtype.itemsize for a in operands) + sum(o.size * o.dtype.itemsize for o in outs)
    space = pl.BlockSpec(memory_space=pltpu.VMEM)
    return pl.pallas_call(
        kernel,
        in_specs=[space] * len(operands),
        out_specs=[space] * len(outs),
        out_shape=outs,
        compiler_params=pltpu.CompilerParams(vmem_limit_bytes=VMEM_LIMIT),
        cost_estimate=pl.CostEstimate(flops=flops, bytes_accessed=size, transcendentals=0),
        name=name,
    )(*operands)


def rows_kernel(*refs):
    kept, came, out_ref = refs[0:6:2], refs[1:6:2], refs[6]
    sums = [k[...].astype(jnp.float32) + r[...].astype(jnp.float32) for k, r in zip(kept, came)]
    out_ref[...] = jnp.concatenate(sums, axis=0).T.astype(out_ref.dtype)


def columns_kernel(parts, in_ref, *out_refs):
    turned = in_ref[...].astype(jnp.float32).T.astype(in_ref.dtype)
    for p, out in enumerate(out_refs):
        start = sum(parts[:p])
        out[...] = turned[start : start + parts[p]]


def half_product(part, half, token_refs, weight_ref):
    tokens = [None] * 16
    for rx in range(2):
        for ry in range(2):
            for rz in range(2):
                for x1 in range(2):
                    for y1 in range(2):
                        side, at = place_in(part, (rx, ry, rz), x1, y1)
                        if side == half:
                            block = [ref[rx * 2 + x1, ry * 4 + y1 * 2 + rz] for ref in token_refs]
                            tokens[at] = jnp.concatenate(block, axis=0)
    return lax.dot_general(
        jnp.concatenate(tokens, axis=1), weight_ref[...], (((1,), (1,)), ((), ())), preferred_element_type=jnp.float32
    )


def forward_own_kernel(mine_ref, theirs_ref, *refs):
    for p in range(3):
        refs[3 + p][...] = half_product(p, 0, (mine_ref, theirs_ref), refs[p])


def forward_kernel(first, tokens_ref, *refs):
    t = tokens_ref.shape[2]
    weights, before, out_ref = refs[:3], refs[3:6], refs[6]
    total = [before[p][first : first + t] + half_product(p, 1, (tokens_ref,), weights[p]) for p in range(3)]
    out_ref[...] = jnp.concatenate(total, axis=1).astype(out_ref.dtype)


def update_kernel(scale, partial_ref, master_ref, one_ref, two_ref, new_master, new_one, new_two, copies):
    gradient = partial_ref[...].astype(jnp.float32).sum(axis=0) * scale
    one = 0.9 * one_ref[...] + 0.1 * gradient
    two = 0.999 * two_ref[...] + 0.001 * gradient * gradient
    first = one / (1.0 - 0.9**10)
    second = two / (1.0 - 0.999**10)
    master = master_ref[...]
    master = master - 0.01 * (first / (jnp.sqrt(second) + 1e-08) + 0.1 * master)
    new_one[...] = one
    new_two[...] = two
    new_master[...] = master
    copies[...] = jnp.broadcast_to(master.astype(copies.dtype)[None], copies.shape)


def halved(value):
    n = value.shape[1] // 2
    return value[:, :n], value[:, n:]


def on_device(tokens, cotangent, next_tokens, master, moment_one, moment_two):
    rows, f = master.shape
    t, d = tokens.shape
    half = d // 2
    parts = part_rows(f)
    me = lax.axis_index("grp") * 32 + lax.axis_index("intra")
    x, y, z, c = coordinates(me)
    at = jnp.stack([c, x % 2, y % 2, z % 2]).astype(jnp.int32)
    bf16 = lambda *shape: jax.ShapeDtypeStruct(shape, jnp.bfloat16)
    f32 = lambda *shape: jax.ShapeDtypeStruct(shape, jnp.float32)
    other_core = lambda v: permute(v, lambda d: d ^ 1)
    flops = 4 * t * half * f

    their_cot = other_core(cotangent)
    mine, sent = sort_columns(at, tokens, FIRST_LIMIT)
    theirs = other_core(sent)
    halves = vmem_call(
        functools.partial(gradient_kernel, parts),
        [bf16(p, half // 2) for p in parts for _ in range(2)],
        "gradient",
        flops,
        mine,
        theirs,
        cotangent,
        their_cot,
    )
    last = []
    for p in range(3):
        kept, sent = halves[2 * p : 2 * p + 2]
        for i, axis in enumerate(ORDER[p]):
            came = permute(sent.astype(jnp.bfloat16), lambda d: neighbour(d, axis))
            if i < 2:
                kept, sent = halved(kept.astype(jnp.float32) + came.astype(jnp.float32))
        last += [kept, came]
    (partial,) = vmem_call(rows_kernel, [bf16(16 * rows, f)], "rows", 0, *last)
    partial = partial.reshape(16, rows, f)
    partial = lax.all_to_all(partial, AXES, 0, 0, tiled=True, axis_index_groups=groups())
    new_master, new_moment_one, new_moment_two, copies = vmem_call(
        functools.partial(update_kernel, 1.0 / (t * DEVICES)),
        [f32(rows, f)] * 3 + [bf16(16, rows, f)],
        "update",
        0,
        partial,
        master,
        moment_one,
        moment_two,
    )

    next_mine, next_sent = sort_columns(at, next_tokens, VMEM_LIMIT)
    next_theirs = other_core(next_sent)
    copies = lax.all_to_all(copies, AXES, 0, 0, tiled=True, axis_index_groups=groups())
    held = vmem_call(
        functools.partial(columns_kernel, parts),
        [bf16(p, 16 * rows) for p in parts],
        "columns",
        0,
        copies.reshape(16 * rows, f),
    )
    owns, cames = [], []
    for p in range(3):
        own = held[p]
        for i, axis in enumerate(ORDER[p][::-1]):
            came = permute(own, lambda d: neighbour(d, axis))
            if i < 2:
                own = jnp.concatenate([own, came], axis=1)
        owns.append(own)
        cames.append(came)
    before = vmem_call(
        forward_own_kernel, [f32(2 * t, p) for p in parts], "forward_own", flops // 2, next_mine, next_theirs, *owns
    )
    (their_out,) = vmem_call(
        functools.partial(forward_kernel, t), [bf16(t, f)], "forward_theirs", flops // 4, next_theirs, *cames, *before
    )
    their_out = other_core(their_out)
    (my_out,) = vmem_call(
        functools.partial(forward_kernel, 0), [f32(t, f)], "forward_mine", flops // 4, next_mine, *cames, *before
    )
    result = my_out + their_out.astype(jnp.float32)
    return (new_master, new_moment_one, new_moment_two, result.astype(jnp.bfloat16))


def solution(mesh):
    spec = P(AXES, None)
    return jax.shard_map(on_device, mesh=mesh, in_specs=(spec,) * 6, out_specs=(spec,) * 4, check_vma=False)
```

time: 1440 us -> 134 us (0.09)
  waiting for transfers between devices: 1370 us -> 30.3 us
  starting transfers between devices: 0.08 us -> 51.4 us
  Pallas kernels: 0 us -> 21 us
  matrix products: 17.2 us -> 0 us
    reduce_scatter x1 -> x0, waiting for transfers between devices: 1290 us -> none  [on_device(): lax.psum_scatter(lax.dot_general(tokens, cotangent, (((0,), (0,)), ((), (...]
    all_gather x1 -> x0, waiting for transfers between devices: 77.8 us -> none  [on_device(): lax.all_gather(copies, 'intra', axis=1, tiled=True)]
    ppermute x0 -> x22, starting transfers between devices: none -> 47.2 us  [permute(): return lax.ppermute(value, AXES, [(d, target(d)) for d in range(DEVICES)])]
    all_gather x1 -> x0, blocking collectives: 30 us -> none  [on_device(): copies = lax.all_gather(weights[None], 'grp', axis=0, tiled=True)]
    all_to_all x0 -> x1, blocking collectives: none -> 25.2 us  [on_device(): lax.all_to_all(partial, AXES, 0, 0, tiled=True, axis_index_groups=groups())]
    ppermute x0 -> x22, waiting for transfers between devices: none -> 21.8 us  [permute(): return lax.ppermute(value, AXES, [(d, target(d)) for d in range(DEVICES)])]
    pallas_call x0 -> x9, Pallas kernels: none -> 21 us  [the longest x7 11 us: vmem_call(): pl.pallas_call(kernel, in_specs=[space] * len(operands), out_specs=[space...]
    dot_general x2 -> x0, matrix products: 17.2 us -> none  [the longest x1 10.3 us: on_device(): lax.dot_general(tokens, cotangent, (((0,), (0,)), ((), ())), preferred_el...]
  transfers between devices with their start and end apart: 2 -> 23, of which waited for: 2 -> 12; matrix products, arithmetic and copies ran while one was open for 0% -> 1% of each run, Pallas kernels for 0% -> 8%
where the time goes in v2:
time: 134 us; the launch traced here: 133 us
  starting transfers between devices  51.4 us (38%)
  waiting for transfers between devices  30.3 us (23%)
  blocking collectives  25.2 us (19%)
  Pallas kernels  21 us (16%)
  local copies, waits for them, and re-layouts  2.64 us (2%)
  other arithmetic  1.67 us (1%)
    ppermute x22, starting transfers between devices, permute(): return lax.ppermute(value, AXES, [(d, target(d)) for d in range(DEVICES)])  47.2 us
    all_to_all x1, blocking collectives, on_device(): lax.all_to_all(partial, AXES, 0, 0, tiled=True, axis_index_groups=groups())  25.2 us
    ppermute x22, waiting for transfers between devices, permute(): return lax.ppermute(value, AXES, [(d, target(d)) for d in range(DEVICES)])  21.8 us
    pallas_call x7, Pallas kernels, vmem_call(): pl.pallas_call(kernel, in_specs=[space] * len(operands), out_specs=[space...  11 us
    pallas_call x2, Pallas kernels, sort_columns(): pl.pallas_call(sort_kernel, in_specs=[pl.BlockSpec(memory_space=pltpu.SME...  10 us
    all_to_all x1, waiting for transfers between devices, on_device(): lax.all_to_all(copies, AXES, 0, 0, tiled=True, axis_index_groups=groups())  8.55 us
    all_to_all x1, starting transfers between devices, on_device(): lax.all_to_all(copies, AXES, 0, 0, tiled=True, axis_index_groups=groups())  4.29 us
  transfers between devices with their start and end apart: 23, of which 12 were waited for; matrix products, arithmetic and copies ran while one was open for 1% of the time, Pallas kernels for 8%

profile of v2, /device:TPU:1, one launch (start us, length us, event | category | flops | bytes accessed | tf_op | source)
XLA Modules:
  0.0 133.4 jit_solution(1517969324589185427)
XLA Ops:
  0.8 4.6 %sort_columns.2 = (bf16[4,8,256,128]{3,2,1,0:T(8,128)(2,1)S(1)}, bf16[4,8,256,128]{3,2,1,0:T(8,128)(2,1)S(1)}) custom-call(s32[4]{0:T(128)S(1)} %pad_add_fusion.at_ref, bf16[256,8192]{1,0:T(8,128)(2,1)} %in_ref.2), custom_call_target="tpu_custom_call" | custom-call | flops 2147483648 | bytes 8388608 | tf_op jit(solution)/shard_map/sort_columns/pallas_call | solution.py:84
  5.5 3.3 %collective-permute-start = (bf16[4,8,256,128]{3,2,1,0:T(8,128)(2,1)S(1)}, bf16[4,8,256,128]{3,2,1,0:T(8,128)(2,1)S(1)}, u32[]{:S(2)}, u32[]{:S(2)}) collective-permute-start(bf16[4,8,256,128]{3,2,1,0:T(8,128)(2,1)S(1)} %get-tuple-element.25), channel_id=1, source_target_pairs={{0,1},{1,0},{2,3},{3,2},{4,5},{5,4},{6,7},{7,6},{8,9},{9,8},{10,11... | collective-permute-start | bytes 6291464 | tf_op jit(solution)/shard_map/ppermute | solution.py:34
  8.9 4.1 %collective-permute-done.1.their_cot_ref = bf16[256,512]{1,0:T(8,128)(2,1)S(1)} collective-permute-done((bf16[256,512]{1,0:T(8,128)(2,1)S(1)}, bf16[256,512]{1,0:T(8,128)(2,1)S(1)}, u32[]{:S(2)}, u32[]{:S(2)}) %collective-permute-start.1) | collective-permute-done | bytes 262176 | tf_op jit(solution)/shard_map/ppermute | solution.py:34
  13.0 2.4 %gradient.1 = (bf16[176,2048]{1,0:T(8,128)(2,1)S(1)}, bf16[176,2048]{1,0:T(8,128)(2,1)S(1)}, bf16[176,2048]{1,0:T(8,128)(2,1)S(1)}, bf16[176,2048]{1,0:T(8,128)(...) custom-call(bf16[4,8,256,128]{3,2,1,0:T(8,128)(2,1)S(1)} %get-tuple-element.24.mine_ref, ...), custom_call_target="tpu_custom_call" | custom-call | flops 2147483648 | bytes 8912896 | tf_op jit(solution)/shard_map/gradient/pallas_call | solution.py:121
  16.4 2.5 %collective-permute-start.2 = (bf16[176,2048]{1,0:T(8,128)(2,1)S(1)}, bf16[176,2048]{1,0:T(8,128)(2,1)S(1)}, u32[]{:S(2)}, u32[]{:S(2)}) collective-permute-start(bf16[176,2048]{1,0:T(8,128)(2,1)S(1)} %get-tuple-element.27), channel_id=1, source_target_pairs={{0,64},{1,193},{2,66},{3,195},{4,68},{5,197},{6,70},{7,199},{8,72}... | collective-permute-start | bytes 2162696 | tf_op jit(solution)/shard_map/ppermute | solution.py:34
  18.9 5.6 %collective-permute-start.8 = (bf16[160,2048]{1,0:T(8,128)(2,1)S(1)}, bf16[160,2048]{1,0:T(8,128)(2,1)S(1)}, u32[]{:S(2)}, u32[]{:S(2)}) collective-permute-start(bf16[160,2048]{1,0:T(8,128)(2,1)S(1)} %get-tuple-element.31), channel_id=1, source_target_pairs={{0,2},{1,15},{2,0},{3,5},{4,6},{5,3},{6,4},{7,9},{8,10},{9,7},{10,... | collective-permute-start | bytes 1966088 | tf_op jit(solution)/shard_map/ppermute | solution.py:34
  24.5 2.3 %collective-permute-done.5 = bf16[176,2048]{1,0:T(8,128)(2,1)S(1)} collective-permute-done((bf16[176,2048]{1,0:T(8,128)(2,1)S(1)}, bf16[176,2048]{1,0:T(8,128)(2,1)S(1)}, u32[]{:S(2)}, u32[]{:S(2)}) %collective-permute-start.5) | collective-permute-done | bytes 720928 | tf_op jit(solution)/shard_map/ppermute | solution.py:34
  27.0 4.0 %collective-permute-start.6 = (bf16[176,1024]{1,0:T(8,128)(2,1)S(1)}, bf16[176,1024]{1,0:T(8,128)(2,1)S(1)}, u32[]{:S(2)}, u32[]{:S(2)}) collective-permute-start(bf16[176,1024]{1,0:T(8,128)(2,1)S(1)} %slice.75), channel_id=1, source_target_pairs={{0,2},{1,15},{2,0},{3,5},{4,6},{5,3},{6,4},{7,9},{8,10},{9,7},{10,... | collective-permute-start | bytes 1081352 | tf_op jit(solution)/shard_map/ppermute | solution.py:34
  31.3 2.8 %collective-permute-start.3 = (bf16[176,1024]{1,0:T(8,128)(2,1)S(1)}, bf16[176,1024]{1,0:T(8,128)(2,1)S(1)}, u32[]{:S(2)}, u32[]{:S(2)}) collective-permute-start(bf16[176,1024]{1,0:T(8,128)(2,1)S(1)} %slice.76), channel_id=1, source_target_pairs={{0,16},{1,49},{2,18},{3,51},{4,20},{5,53},{6,22},{7,55},{8,24},{9,... | collective-permute-start | bytes 1081352 | tf_op jit(solution)/shard_map/ppermute | solution.py:34
  34.2 2.6 %collective-permute-start.9 = (bf16[160,1024]{1,0:T(8,128)(2,1)S(1)}, bf16[160,1024]{1,0:T(8,128)(2,1)S(1)}, u32[]{:S(2)}, u32[]{:S(2)}) collective-permute-start(bf16[160,1024]{1,0:T(8,128)(2,1)S(1)} %slice.77), channel_id=1, source_target_pairs={{0,64},{1,193},{2,66},{3,195},{4,68},{5,197},{6,70},{7,199},{8,72}... | collective-permute-start | bytes 983048 | tf_op jit(solution)/shard_map/ppermute | solution.py:34
  36.9 1.6 %collective-permute-start.7 = (bf16[176,512]{1,0:T(8,128)(2,1)S(1)}, bf16[176,512]{1,0:T(8,128)(2,1)S(1)}, u32[]{:S(2)}, u32[]{:S(2)}) collective-permute-start(bf16[176,512]{1,0:T(8,128)(2,1)S(1)} %slice.78), channel_id=1, source_target_pairs={{0,64},{1,193},{2,66},{3,195},{4,68},{5,197},{6,70},{7,199},{8,72}... | collective-permute-start | bytes 540680 | tf_op jit(solution)/shard_map/ppermute | solution.py:34
  39.0 2.4 %collective-permute-start.4 = (bf16[176,512]{1,0:T(8,128)(2,1)S(1)}, bf16[176,512]{1,0:T(8,128)(2,1)S(1)}, u32[]{:S(2)}, u32[]{:S(2)}) collective-permute-start(bf16[176,512]{1,0:T(8,128)(2,1)S(1)} %slice.79), channel_id=1, source_target_pairs={{0,2},{1,15},{2,0},{3,5},{4,6},{5,3},{6,4},{7,9},{8,10},{9,7},{10,... | collective-permute-start | bytes 540680 | tf_op jit(solution)/shard_map/ppermute | solution.py:34
  41.6 2.7 %collective-permute-start.10 = (bf16[160,512]{1,0:T(8,128)(2,1)S(1)}, bf16[160,512]{1,0:T(8,128)(2,1)S(1)}, u32[]{:S(2)}, u32[]{:S(2)}) collective-permute-start(bf16[160,512]{1,0:T(8,128)(2,1)S(1)} %slice.80), channel_id=1, source_target_pairs={{0,16},{1,49},{2,18},{3,51},{4,20},{5,53},{6,22},{7,55},{8,24},{9,... | collective-permute-start | bytes 491528 | tf_op jit(solution)/shard_map/ppermute | solution.py:34
  44.4 2.6 %collective-permute-done.10.refs_5_ = bf16[160,512]{1,0:T(8,128)(2,1)S(1)} collective-permute-done((bf16[160,512]{1,0:T(8,128)(2,1)S(1)}, bf16[160,512]{1,0:T(8,128)(2,1)S(1)}, u32[]{:S(2)}, u32[]{:S(2)}) %collective-permute-start.10) | collective-permute-done | bytes 163872 | tf_op jit(solution)/shard_map/ppermute | solution.py:34
  47.3 25.2 %all_to_all.10.partial_ref = bf16[16,32,512]{2,1,0:T(8,128)(2,1)S(1)} all-to-all(bf16[16,32,512]{2,1,0:T(8,128)(2,1)S(1)} %bitcast.7), channel_id=1, replica_groups={{0,4,8,12,32,36,40,44,128,132,136,140,160,164,168,172},{1,5,9,13,33,37,..., dimensions={0} | all-to-all | bytes 1048576 | tf_op jit(solution)/shard_map/all_to_all | solution.py:228
  73.5 4.3 %all-to-all-start.1 = ((bf16[16,32,512]{2,1,0:T(8,128)(2,1)}), bf16[16,32,512]{2,1,0:T(8,128)(2,1)S(1)}, u32[]{:S(2)}, u32[]{:S(2)}) async-start(bf16[16,32,512]{2,1,0:T(8,128)(2,1)} %get-tuple-element.36), calls=%async_computation.1 | async-start | bytes 1048576 | tf_op jit(solution)/shard_map/all_to_all | solution.py:242
  77.8 2.2 %copy-done.3 = bf16[256,8192]{1,0:T(8,128)(2,1)S(1)} copy-done((bf16[256,8192]{1,0:T(8,128)(2,1)S(1)}, bf16[256,8192]{1,0:T(8,128)(2,1)}, u32[]{:S(2)}) %copy-start.3) | copy-done | bytes 4194328
  80.0 5.4 %sort_columns.3 = (bf16[4,8,256,128]{3,2,1,0:T(8,128)(2,1)S(1)}, bf16[4,8,256,128]{3,2,1,0:T(8,128)(2,1)}) custom-call(s32[4]{0:T(128)S(1)} %pad_add_fusion.at_ref, bf16[256,8192]{1,0:T(8,128)(2,1)S(1)} %copy-done.3), custom_call_target="tpu_custom_call" | custom-call | flops 2147483648 | bytes 8388608 | tf_op jit(solution)/shard_map/sort_columns/pallas_call | solution.py:84
  85.3 1.8 %collective-permute-start.20 = (bf16[4,8,256,128]{3,2,1,0:T(8,128)(2,1)}, bf16[4,8,256,128]{3,2,1,0:T(8,128)(2,1)}, u32[]{:S(2)}, u32[]{:S(2)}) collective-permute-start(bf16[4,8,256,128]{3,2,1,0:T(8,128)(2,1)} %get-tuple-element.40), channel_id=1, source_target_pairs={{0,1},{1,0},{2,3},{3,2},{4,5},{5,4},{6,7},{7,6},{8,9},{9,8},{10,11... | collective-permute-start | bytes 6291464 | tf_op jit(solution)/shard_map/ppermute | solution.py:34
  87.1 8.6 %all-to-all-done.1 = bf16[16,32,512]{2,1,0:T(8,128)(2,1)S(1)} async-done(((bf16[16,32,512]{2,1,0:T(8,128)(2,1)}), bf16[16,32,512]{2,1,0:T(8,128)(2,1)S(1)}, u32[]{:S(2)}, u32[]{:S(2)}) %all-to-all-start.1) | async-done | bytes 524320 | tf_op jit(solution)/shard_map/all_to_all | solution.py:242
  95.9 3.2 %collective-permute-start.17 = (bf16[160,512]{1,0:T(8,128)(2,1)S(1)}, bf16[160,512]{1,0:T(8,128)(2,1)S(1)}, u32[]{:S(2)}, u32[]{:S(2)}) collective-permute-start(bf16[160,512]{1,0:T(8,128)(2,1)S(1)} %get-tuple-element.39), channel_id=1, source_target_pairs={{0,16},{1,49},{2,18},{3,51},{4,20},{5,53},{6,22},{7,55},{8,24},{9,... | collective-permute-start | bytes 491528 | tf_op jit(solution)/shard_map/ppermute | solution.py:34
  99.1 2.9 %collective-permute-start.14 = (bf16[176,512]{1,0:T(8,128)(2,1)S(1)}, bf16[176,512]{1,0:T(8,128)(2,1)S(1)}, u32[]{:S(2)}, u32[]{:S(2)}) collective-permute-start(bf16[176,512]{1,0:T(8,128)(2,1)S(1)} %get-tuple-element.38), channel_id=1, source_target_pairs={{0,64},{1,193},{2,66},{3,195},{4,68},{5,197},{6,70},{7,199},{8,72}... | collective-permute-start | bytes 540680 | tf_op jit(solution)/shard_map/ppermute | solution.py:34
  102.2 2.6 %collective-permute-start.18 = (bf16[160,1024]{1,0:T(8,128)(2,1)S(1)}, bf16[160,1024]{1,0:T(8,128)(2,1)S(1)}, u32[]{:S(2)}, u32[]{:S(2)}) collective-permute-start(bf16[160,1024]{1,0:T(8,128)(2,1)S(1)} %pad_maximum_fusion.2), channel_id=1, source_target_pairs={{0,64},{1,193},{2,66},{3,195},{4,68},{5,197},{6,70},{7,199},{8,72}... | collective-permute-start | bytes 983048 | tf_op jit(solution)/shard_map/ppermute | solution.py:34
  105.1 2.6 %collective-permute-done.11 = bf16[176,512]{1,0:T(8,128)(2,1)S(1)} collective-permute-done((bf16[176,512]{1,0:T(8,128)(2,1)S(1)}, bf16[176,512]{1,0:T(8,128)(2,1)S(1)}, u32[]{:S(2)}, u32[]{:S(2)}) %collective-permute-start.11) | collective-permute-done | bytes 180256 | tf_op jit(solution)/shard_map/ppermute | solution.py:34
  108.0 4.5 %collective-permute-done.15 = bf16[176,1024]{1,0:T(8,128)(2,1)S(1)} collective-permute-done((bf16[176,1024]{1,0:T(8,128)(2,1)S(1)}, bf16[176,1024]{1,0:T(8,128)(2,1)S(1)}, u32[]{:S(2)}, u32[]{:S(2)}) %collective-permute-start.15) | collective-permute-done | bytes 360480 | tf_op jit(solution)/shard_map/ppermute | solution.py:34
  112.5 2.7 %collective-permute-start.16 = (bf16[176,2048]{1,0:T(8,128)(2,1)S(1)}, bf16[176,2048]{1,0:T(8,128)(2,1)S(1)}, u32[]{:S(2)}, u32[]{:S(2)}) collective-permute-start(bf16[176,2048]{1,0:T(8,128)(2,1)S(1)} %constant_dynamic-update-slice_fusion.3.refs_1_), channel_id=1, source_target_pairs={{0,16},{1,49},{2,18},{3,51},{4,20},{5,53},{6,22},{7,55},{8,24},{9,... | collective-permute-start | bytes 2162696 | tf_op jit(solution)/shard_map/ppermute | solution.py:34
  115.5 2.7 %collective-permute-start.19 = (bf16[160,2048]{1,0:T(8,128)(2,1)S(1)}, bf16[160,2048]{1,0:T(8,128)(2,1)S(1)}, u32[]{:S(2)}, u32[]{:S(2)}) collective-permute-start(bf16[160,2048]{1,0:T(8,128)(2,1)S(1)} %constant_dynamic-update-slice_fusion.6.refs_2_), channel_id=1, source_target_pairs={{0,2},{1,15},{2,0},{3,5},{4,6},{5,3},{6,4},{7,9},{8,10},{9,7},{10,... | collective-permute-start | bytes 1966088 | tf_op jit(solution)/shard_map/ppermute | solution.py:34
  118.2 3.4 %forward_own.1 = (f32[512,176]{1,0:T(8,128)S(1)}, f32[512,176]{1,0:T(8,128)S(1)}, f32[512,160]{1,0:T(8,128)S(1)}) custom-call(bf16[4,8,256,128]{3,2,1,0:T(8,128)(2,1)S(1)} %get-tuple-element.35.mine_ref.tokens_ref, bf16[4,8,256,128]{3,2,1,0:T(8,128)(2,1)} %collective-permute-done.20.theirs_ref.tokens_ref, ...), custom_call_target="tpu_custom_call" | custom-call | flops 1073741824 | bytes 7340032 | tf_op jit(solution)/shard_map/forward_own/pallas_call | solution.py:121
  121.6 4.7 %collective-permute-done.19.refs_2_ = bf16[160,2048]{1,0:T(8,128)(2,1)S(1)} collective-permute-done((bf16[160,2048]{1,0:T(8,128)(2,1)S(1)}, bf16[160,2048]{1,0:T(8,128)(2,1)S(1)}, u32[]{:S(2)}, u32[]{:S(2)}) %collective-permute-start.19) | collective-permute-done | bytes 655392 | tf_op jit(solution)/shard_map/ppermute | solution.py:34
  126.7 2.6 %forward_theirs.1 = bf16[256,512]{1,0:T(8,128)(2,1)S(1)} custom-call(bf16[4,8,256,128]{3,2,1,0:T(8,128)(2,1)} %collective-permute-done.20.theirs_ref.tokens_ref, bf16[176,2048]{1,0:T(8,128)(2,1)S(1)} %collective-permute-done.13.refs_0_, bf16[176,2048]{1,0:T(8,128)(2,1)S(1)} %collective-permute-done.16.refs_1_, ...), custom_call_target="tpu_custom_call" | custom-call | flops 536870912 | bytes 5505024 | tf_op jit(solution)/shard_map/forward_theirs/pallas_call | solution.py:121
  129.4 2.0 %collective-permute-start.21 = (bf16[256,512]{1,0:T(8,128)(2,1)S(1)}, bf16[256,512]{1,0:T(8,128)(2,1)S(1)}, u32[]{:S(2)}, u32[]{:S(2)}) collective-permute-start(bf16[256,512]{1,0:T(8,128)(2,1)S(1)} %forward_theirs.1), channel_id=1, source_target_pairs={{0,1},{1,0},{2,3},{3,2},{4,5},{5,4},{6,7},{7,6},{8,9},{9,8},{10,11... | collective-permute-start | bytes 786440 | tf_op jit(solution)/shard_map/ppermute | solution.py:34
  131.4 1.1 forward_mine.1
  (62 shorter events, 6.4 us)
Async XLA Ops:
  0.8 8.0 %copy-start.4 = (bf16[256,512]{1,0:T(8,128)(2,1)S(1)}, bf16[256,512]{1,0:T(8,128)(2,1)}, u32[]{:S(2)}) copy-start(bf16[256,512]{1,0:T(8,128)(2,1)} %my_cot_ref.1) | copy-start | bytes 786436
  5.5 7.5 %collective-permute-start = (bf16[4,8,256,128]{3,2,1,0:T(8,128)(2,1)S(1)}, bf16[4,8,256,128]{3,2,1,0:T(8,128)(2,1)S(1)}, u32[]{:S(2)}, u32[]{:S(2)}) collective-permute-start(bf16[4,8,256,128]{3,2,1,0:T(8,128)(2,1)S(1)} %get-tuple-element.25), channel_id=1, source_target_pairs={{0,1},{1,0},{2,3},{3,2},{4,5},{5,4},{6,7},{7,6},{8,9},{9,8},{10,11... | collective-permute-start | bytes 6291464 | tf_op jit(solution)/shard_map/ppermute | solution.py:34
  8.8 4.2 %collective-permute-start.1 = (bf16[256,512]{1,0:T(8,128)(2,1)S(1)}, bf16[256,512]{1,0:T(8,128)(2,1)S(1)}, u32[]{:S(2)}, u32[]{:S(2)}) collective-permute-start(bf16[256,512]{1,0:T(8,128)(2,1)S(1)} %copy-done.4), channel_id=1, source_target_pairs={{0,1},{1,0},{2,3},{3,2},{4,5},{5,4},{6,7},{7,6},{8,9},{9,8},{10,11... | collective-permute-start | bytes 786440 | tf_op jit(solution)/shard_map/ppermute | solution.py:34
  15.3 11.4 %collective-permute-start.5 = (bf16[176,2048]{1,0:T(8,128)(2,1)S(1)}, bf16[176,2048]{1,0:T(8,128)(2,1)S(1)}, u32[]{:S(2)}, u32[]{:S(2)}) collective-permute-start(bf16[176,2048]{1,0:T(8,128)(2,1)S(1)} %get-tuple-element.29), channel_id=1, source_target_pairs={{0,16},{1,49},{2,18},{3,51},{4,20},{5,53},{6,22},{7,55},{8,24},{9,... | collective-permute-start | bytes 2162696 | tf_op jit(solution)/shard_map/ppermute | solution.py:34
  16.4 14.6 %collective-permute-start.2 = (bf16[176,2048]{1,0:T(8,128)(2,1)S(1)}, bf16[176,2048]{1,0:T(8,128)(2,1)S(1)}, u32[]{:S(2)}, u32[]{:S(2)}) collective-permute-start(bf16[176,2048]{1,0:T(8,128)(2,1)S(1)} %get-tuple-element.27), channel_id=1, source_target_pairs={{0,64},{1,193},{2,66},{3,195},{4,68},{5,197},{6,70},{7,199},{8,72}... | collective-permute-start | bytes 2162696 | tf_op jit(solution)/shard_map/ppermute | solution.py:34
  18.9 15.1 %collective-permute-start.8 = (bf16[160,2048]{1,0:T(8,128)(2,1)S(1)}, bf16[160,2048]{1,0:T(8,128)(2,1)S(1)}, u32[]{:S(2)}, u32[]{:S(2)}) collective-permute-start(bf16[160,2048]{1,0:T(8,128)(2,1)S(1)} %get-tuple-element.31), channel_id=1, source_target_pairs={{0,2},{1,15},{2,0},{3,5},{4,6},{5,3},{6,4},{7,9},{8,10},{9,7},{10,... | collective-permute-start | bytes 1966088 | tf_op jit(solution)/shard_map/ppermute | solution.py:34
  27.0 9.8 %collective-permute-start.6 = (bf16[176,1024]{1,0:T(8,128)(2,1)S(1)}, bf16[176,1024]{1,0:T(8,128)(2,1)S(1)}, u32[]{:S(2)}, u32[]{:S(2)}) collective-permute-start(bf16[176,1024]{1,0:T(8,128)(2,1)S(1)} %slice.75), channel_id=1, source_target_pairs={{0,2},{1,15},{2,0},{3,5},{4,6},{5,3},{6,4},{7,9},{8,10},{9,7},{10,... | collective-permute-start | bytes 1081352 | tf_op jit(solution)/shard_map/ppermute | solution.py:34
  31.3 7.6 %collective-permute-start.3 = (bf16[176,1024]{1,0:T(8,128)(2,1)S(1)}, bf16[176,1024]{1,0:T(8,128)(2,1)S(1)}, u32[]{:S(2)}, u32[]{:S(2)}) collective-permute-start(bf16[176,1024]{1,0:T(8,128)(2,1)S(1)} %slice.76), channel_id=1, source_target_pairs={{0,16},{1,49},{2,18},{3,51},{4,20},{5,53},{6,22},{7,55},{8,24},{9,... | collective-permute-start | bytes 1081352 | tf_op jit(solution)/shard_map/ppermute | solution.py:34
  34.2 7.2 %collective-permute-start.9 = (bf16[160,1024]{1,0:T(8,128)(2,1)S(1)}, bf16[160,1024]{1,0:T(8,128)(2,1)S(1)}, u32[]{:S(2)}, u32[]{:S(2)}) collective-permute-start(bf16[160,1024]{1,0:T(8,128)(2,1)S(1)} %slice.77), channel_id=1, source_target_pairs={{0,64},{1,193},{2,66},{3,195},{4,68},{5,197},{6,70},{7,199},{8,72}... | collective-permute-start | bytes 983048 | tf_op jit(solution)/shard_map/ppermute | solution.py:34
  36.9 10.1 %collective-permute-start.7 = (bf16[176,512]{1,0:T(8,128)(2,1)S(1)}, bf16[176,512]{1,0:T(8,128)(2,1)S(1)}, u32[]{:S(2)}, u32[]{:S(2)}) collective-permute-start(bf16[176,512]{1,0:T(8,128)(2,1)S(1)} %slice.78), channel_id=1, source_target_pairs={{0,64},{1,193},{2,66},{3,195},{4,68},{5,197},{6,70},{7,199},{8,72}... | collective-permute-start | bytes 540680 | tf_op jit(solution)/shard_map/ppermute | solution.py:34
  39.0 8.1 %collective-permute-start.4 = (bf16[176,512]{1,0:T(8,128)(2,1)S(1)}, bf16[176,512]{1,0:T(8,128)(2,1)S(1)}, u32[]{:S(2)}, u32[]{:S(2)}) collective-permute-start(bf16[176,512]{1,0:T(8,128)(2,1)S(1)} %slice.79), channel_id=1, source_target_pairs={{0,2},{1,15},{2,0},{3,5},{4,6},{5,3},{6,4},{7,9},{8,10},{9,7},{10,... | collective-permute-start | bytes 540680 | tf_op jit(solution)/shard_map/ppermute | solution.py:34
  41.6 5.5 %collective-permute-start.10 = (bf16[160,512]{1,0:T(8,128)(2,1)S(1)}, bf16[160,512]{1,0:T(8,128)(2,1)S(1)}, u32[]{:S(2)}, u32[]{:S(2)}) collective-permute-start(bf16[160,512]{1,0:T(8,128)(2,1)S(1)} %slice.80), channel_id=1, source_target_pairs={{0,16},{1,49},{2,18},{3,51},{4,20},{5,53},{6,22},{7,55},{8,24},{9,... | collective-permute-start | bytes 491528 | tf_op jit(solution)/shard_map/ppermute | solution.py:34
  44.4 28.1 %copy-start = (f32[32,512]{1,0:T(8,128)S(1)}, f32[32,512]{1,0:T(8,128)}, u32[]{:S(2)}) copy-start(f32[32,512]{1,0:T(8,128)} %master_ref.1) | copy-start | bytes 196612
  44.4 28.1 %copy-start.1 = (f32[32,512]{1,0:T(8,128)S(1)}, f32[32,512]{1,0:T(8,128)}, u32[]{:S(2)}) copy-start(f32[32,512]{1,0:T(8,128)} %one_ref.1) | copy-start | bytes 196612
  44.4 28.1 %copy-start.2 = (f32[32,512]{1,0:T(8,128)S(1)}, f32[32,512]{1,0:T(8,128)}, u32[]{:S(2)}) copy-start(f32[32,512]{1,0:T(8,128)} %two_ref.1) | copy-start | bytes 196612
  73.5 22.2 %all-to-all-start.1 = ((bf16[16,32,512]{2,1,0:T(8,128)(2,1)}), bf16[16,32,512]{2,1,0:T(8,128)(2,1)S(1)}, u32[]{:S(2)}, u32[]{:S(2)}) async-start(bf16[16,32,512]{2,1,0:T(8,128)(2,1)} %get-tuple-element.36), calls=%async_computation.1 | async-start | bytes 1048576 | tf_op jit(solution)/shard_map/all_to_all | solution.py:242
  77.8 2.2 %copy-start.3 = (bf16[256,8192]{1,0:T(8,128)(2,1)S(1)}, bf16[256,8192]{1,0:T(8,128)(2,1)}, u32[]{:S(2)}) copy-start(bf16[256,8192]{1,0:T(8,128)(2,1)} %in_ref.3) | copy-start | bytes 12582916
  85.3 32.9 %collective-permute-start.20 = (bf16[4,8,256,128]{3,2,1,0:T(8,128)(2,1)}, bf16[4,8,256,128]{3,2,1,0:T(8,128)(2,1)}, u32[]{:S(2)}, u32[]{:S(2)}) collective-permute-start(bf16[4,8,256,128]{3,2,1,0:T(8,128)(2,1)} %get-tuple-element.40), channel_id=1, source_target_pairs={{0,1},{1,0},{2,3},{3,2},{4,5},{5,4},{6,7},{7,6},{8,9},{9,8},{10,11... | collective-permute-start | bytes 6291464 | tf_op jit(solution)/shard_map/ppermute | solution.py:34
  95.9 6.2 %collective-permute-start.17 = (bf16[160,512]{1,0:T(8,128)(2,1)S(1)}, bf16[160,512]{1,0:T(8,128)(2,1)S(1)}, u32[]{:S(2)}, u32[]{:S(2)}) collective-permute-start(bf16[160,512]{1,0:T(8,128)(2,1)S(1)} %get-tuple-element.39), channel_id=1, source_target_pairs={{0,16},{1,49},{2,18},{3,51},{4,20},{5,53},{6,22},{7,55},{8,24},{9,... | collective-permute-start | bytes 491528 | tf_op jit(solution)/shard_map/ppermute | solution.py:34
  99.1 5.8 %collective-permute-start.14 = (bf16[176,512]{1,0:T(8,128)(2,1)S(1)}, bf16[176,512]{1,0:T(8,128)(2,1)S(1)}, u32[]{:S(2)}, u32[]{:S(2)}) collective-permute-start(bf16[176,512]{1,0:T(8,128)(2,1)S(1)} %get-tuple-element.38), channel_id=1, source_target_pairs={{0,64},{1,193},{2,66},{3,195},{4,68},{5,197},{6,70},{7,199},{8,72}... | collective-permute-start | bytes 540680 | tf_op jit(solution)/shard_map/ppermute | solution.py:34
  102.0 5.6 %collective-permute-start.11 = (bf16[176,512]{1,0:T(8,128)(2,1)S(1)}, bf16[176,512]{1,0:T(8,128)(2,1)S(1)}, u32[]{:S(2)}, u32[]{:S(2)}) collective-permute-start(bf16[176,512]{1,0:T(8,128)(2,1)S(1)} %get-tuple-element.37), channel_id=1, source_target_pairs={{0,2},{1,15},{2,0},{3,5},{4,6},{5,3},{6,4},{7,9},{8,10},{9,7},{10,... | collective-permute-start | bytes 540680 | tf_op jit(solution)/shard_map/ppermute | solution.py:34
  102.2 13.3 %collective-permute-start.18 = (bf16[160,1024]{1,0:T(8,128)(2,1)S(1)}, bf16[160,1024]{1,0:T(8,128)(2,1)S(1)}, u32[]{:S(2)}, u32[]{:S(2)}) collective-permute-start(bf16[160,1024]{1,0:T(8,128)(2,1)S(1)} %pad_maximum_fusion.2), channel_id=1, source_target_pairs={{0,64},{1,193},{2,66},{3,195},{4,68},{5,197},{6,70},{7,199},{8,72}... | collective-permute-start | bytes 983048 | tf_op jit(solution)/shard_map/ppermute | solution.py:34
  104.9 7.6 %collective-permute-start.15 = (bf16[176,1024]{1,0:T(8,128)(2,1)S(1)}, bf16[176,1024]{1,0:T(8,128)(2,1)S(1)}, u32[]{:S(2)}, u32[]{:S(2)}) collective-permute-start(bf16[176,1024]{1,0:T(8,128)(2,1)S(1)} %pad_maximum_fusion.1), channel_id=1, source_target_pairs={{0,2},{1,15},{2,0},{3,5},{4,6},{5,3},{6,4},{7,9},{8,10},{9,7},{10,... | collective-permute-start | bytes 1081352 | tf_op jit(solution)/shard_map/ppermute | solution.py:34
  107.7 7.6 %collective-permute-start.12 = (bf16[176,1024]{1,0:T(8,128)(2,1)S(1)}, bf16[176,1024]{1,0:T(8,128)(2,1)S(1)}, u32[]{:S(2)}, u32[]{:S(2)}) collective-permute-start(bf16[176,1024]{1,0:T(8,128)(2,1)S(1)} %pad_maximum_fusion), channel_id=1, source_target_pairs={{0,16},{1,49},{2,18},{3,51},{4,20},{5,53},{6,22},{7,55},{8,24},{9,... | collective-permute-start | bytes 1081352 | tf_op jit(solution)/shard_map/ppermute | solution.py:34
  112.5 13.7 %collective-permute-start.16 = (bf16[176,2048]{1,0:T(8,128)(2,1)S(1)}, bf16[176,2048]{1,0:T(8,128)(2,1)S(1)}, u32[]{:S(2)}, u32[]{:S(2)}) collective-permute-start(bf16[176,2048]{1,0:T(8,128)(2,1)S(1)} %constant_dynamic-update-slice_fusion.3.refs_1_), channel_id=1, source_target_pairs={{0,16},{1,49},{2,18},{3,51},{4,20},{5,53},{6,22},{7,55},{8,24},{9,... | collective-permute-start | bytes 2162696 | tf_op jit(solution)/shard_map/ppermute | solution.py:34
  115.3 11.4 %collective-permute-start.13 = (bf16[176,2048]{1,0:T(8,128)(2,1)S(1)}, bf16[176,2048]{1,0:T(8,128)(2,1)S(1)}, u32[]{:S(2)}, u32[]{:S(2)}) collective-permute-start(bf16[176,2048]{1,0:T(8,128)(2,1)S(1)} %constant_dynamic-update-slice_fusion.refs_0_), channel_id=1, source_target_pairs={{0,64},{1,193},{2,66},{3,195},{4,68},{5,197},{6,70},{7,199},{8,72}... | collective-permute-start | bytes 2162696 | tf_op jit(solution)/shard_map/ppermute | solution.py:34
  115.5 10.7 %collective-permute-start.19 = (bf16[160,2048]{1,0:T(8,128)(2,1)S(1)}, bf16[160,2048]{1,0:T(8,128)(2,1)S(1)}, u32[]{:S(2)}, u32[]{:S(2)}) collective-permute-start(bf16[160,2048]{1,0:T(8,128)(2,1)S(1)} %constant_dynamic-update-slice_fusion.6.refs_2_), channel_id=1, source_target_pairs={{0,2},{1,15},{2,0},{3,5},{4,6},{5,3},{6,4},{7,9},{8,10},{9,7},{10,... | collective-permute-start | bytes 1966088 | tf_op jit(solution)/shard_map/ppermute | solution.py:34
  129.4 3.2 %collective-permute-start.21 = (bf16[256,512]{1,0:T(8,128)(2,1)S(1)}, bf16[256,512]{1,0:T(8,128)(2,1)S(1)}, u32[]{:S(2)}, u32[]{:S(2)}) collective-permute-start(bf16[256,512]{1,0:T(8,128)(2,1)S(1)} %forward_theirs.1), channel_id=1, source_target_pairs={{0,1},{1,0},{2,3},{3,2},{4,5},{5,4},{6,7},{7,6},{8,9},{9,8},{10,11... | collective-permute-start | bytes 786440 | tf_op jit(solution)/shard_map/ppermute | solution.py:34

commit v3 on v2

--- a/solution.py
+++ b/solution.py
@@ -53,12 +53,12 @@
     return a, (b * 2 + c) * 4 + x1 * 2 + y1
 
 
-def sort_kernel(at_ref, in_ref, my_ref, other_ref, chunks, sems):
+def sort_kernel(sides, at_ref, in_ref, my_ref, other_ref, chunks, sems):
     c, x0, y0, z0 = (at_ref[i] for i in range(4))
     wide = chunks.shape[2]
     copies = []
-    for i in range(4):
-        start = pl.multiple_of((2 * (i % 2) + (x0 ^ (i // 2))) * wide, wide)
+    for i in range(2 * len(sides)):
+        start = pl.multiple_of((2 * (i % 2) + (x0 ^ sides[i // 2])) * wide, wide)
         copies.append(pltpu.make_async_copy(in_ref.at[:, pl.ds(start, wide)], chunks.at[i], sems.at[i]))
         copies[-1].start()
     n = 4 * LANES
@@ -67,7 +67,7 @@
     q, r, row = goal // 128, goal // 32 % 4, goal % 32
     wanted = r * 128 + (((q % 2) ^ z0) * 2 + ((q // 2) ^ c)) * 32 + row
     move = jnp.where(source == wanted, 1.0, 0.0).astype(my_ref.dtype)
-    for i in range(4):
+    for i in range(2 * len(sides)):
         copies[i].wait()
         for y in range(4):
             turned = jnp.dot(chunks[i, :, y * n : (y + 1) * n], move, preferred_element_type=jnp.float32)
@@ -78,41 +78,65 @@
                 other_ref[i, where + rz] = turned[:, (2 + rz) * LANES : (3 + rz) * LANES]
 
 
-def sort_columns(at, tokens, limit):
+def sort_columns(at, tokens, sides, limit):
     t, d = tokens.shape
+    n = 2 * len(sides)
     space = pl.BlockSpec(memory_space=pltpu.VMEM)
     return pl.pallas_call(
-        sort_kernel,
+        functools.partial(sort_kernel, sides),
         in_specs=[pl.BlockSpec(memory_space=pltpu.SMEM), pl.BlockSpec(memory_space=pl.ANY)],
         out_specs=[space, space],
-        out_shape=[jax.ShapeDtypeStruct((4, 8, t, LANES), tokens.dtype)] * 2,
-        scratch_shapes=[pltpu.VMEM((4, t, d // 4), tokens.dtype), pltpu.SemaphoreType.DMA((4,))],
+        out_shape=[jax.ShapeDtypeStruct((n, 8, t, LANES), tokens.dtype)] * 2,
+        scratch_shapes=[pltpu.VMEM((n, t, d // 4), tokens.dtype), pltpu.SemaphoreType.DMA((n,))],
         compiler_params=pltpu.CompilerParams(vmem_limit_bytes=limit),
-        cost_estimate=pl.CostEstimate(flops=8 * LANES * t * d, bytes_accessed=4 * t * d, transcendentals=0),
+        cost_estimate=pl.CostEstimate(
+            flops=2 * n * LANES * t * d, bytes_accessed=n * t * d, transcendentals=0
+        ),
         name="sort_columns",
     )(at, tokens)
 
 
-def gradient_kernel(parts, mine_ref, theirs_ref, my_cot_ref, their_cot_ref, *out_refs):
+def gradient_blocks(mine_ref, theirs_ref, my_cot_ref, their_cot_ref):
     cot = jnp.concatenate([my_cot_ref[...].T, their_cot_ref[...].T], axis=1)
+    for x1 in range(2):
+        for ry in range(2):
+            blocks = [
+                jnp.concatenate([mine_ref[x1, ry * 4 + i], theirs_ref[x1, ry * 4 + i]], axis=0) for i in range(4)
+            ]
+            total = jnp.dot(cot, jnp.concatenate(blocks, axis=1), preferred_element_type=jnp.float32)
+            yield x1, ry, total.astype(jnp.bfloat16)
+
+
+def lanes(at):
+    return slice(at * LANES, (at + 1) * LANES)
+
+
+def gradient_far_kernel(parts, mine_ref, theirs_ref, my_cot_ref, their_cot_ref, sent_ref, *held_refs):
     starts = [sum(parts[:p]) for p in range(3)]
-    for rx in range(2):
-        for x1 in range(2):
-            for ry in range(2):
-                blocks = [
-                    jnp.concatenate([mine_ref[rx * 2 + x1, ry * 4 + i], theirs_ref[rx * 2 + x1, ry * 4 + i]], axis=0)
-                    for i in range(4)
-                ]
-                total = jnp.dot(cot, jnp.concatenate(blocks, axis=1), preferred_element_type=jnp.float32)
-                total = total.astype(jnp.bfloat16)
-                for y1 in range(2):
-                    for rz in range(2):
-                        i = y1 * 2 + rz
-                        for p in range(3):
-                            half, at = place_in(p, (rx, ry, rz), x1, y1)
-                            out_refs[2 * p + half][:, at * LANES : (at + 1) * LANES] = total[
-                                starts[p] : starts[p] + parts[p], i * LANES : (i + 1) * LANES
-                            ]
+    for x1, ry, total in gradient_blocks(mine_ref, theirs_ref, my_cot_ref, their_cot_ref):
+        for i in range(4):
+            y1, rz = i // 2, i % 2
+            _, at = place_in(0, (1, ry, rz), x1, y1)
+            sent_ref[:, lanes(at)] = total[: parts[0], lanes(i)]
+        for p in (1, 2):
+            at = (ry * 2 + x1) * 4 * LANES
+            held_refs[p - 1][:, at : at + 4 * LANES] = total[starts[p] : starts[p] + parts[p]]
+
+
+def gradient_near_kernel(parts, mine_ref, theirs_ref, my_cot_ref, their_cot_ref, *refs):
+    held_refs, out_refs = (None,) + refs[:2], refs[2:]
+    starts = [sum(parts[:p]) for p in range(3)]
+    for x1, ry, total in gradient_blocks(mine_ref, theirs_ref, my_cot_ref, their_cot_ref):
+        for i in range(4):
+            y1, rz = i // 2, i % 2
+            for p in range(3):
+                half, at = place_in(p, (0, ry, rz), x1, y1)
+                out = out_refs[2 * p + half - (p > 0)]
+                out[:, lanes(at)] = total[starts[p] : starts[p] + parts[p], lanes(i)]
+                if p:
+                    half, at = place_in(p, (1, ry, rz), x1, y1)
+                    out = out_refs[2 * p + half - 1]
+                    out[:, lanes(at)] = held_refs[p][:, lanes((ry * 2 + x1) * 4 + i)]
 
 
 def vmem_call(kernel, outs, name, flops, *operands):
@@ -161,6 +185,7 @@
 def forward_own_kernel(mine_ref, theirs_ref, *refs):
     for p in range(3):
         refs[3 + p][...] = half_product(p, 0, (mine_ref, theirs_ref), refs[p])
+    refs[6][...] = theirs_ref[...]
 
 
 def forward_kernel(first, tokens_ref, *refs):
@@ -203,18 +228,32 @@
     flops = 4 * t * half * f
 
     their_cot = other_core(cotangent)
-    mine, sent = sort_columns(at, tokens, FIRST_LIMIT)
-    theirs = other_core(sent)
-    halves = vmem_call(
-        functools.partial(gradient_kernel, parts),
-        [bf16(p, half // 2) for p in parts for _ in range(2)],
-        "gradient",
-        flops,
-        mine,
-        theirs,
+    mine_far, sent = sort_columns(at, tokens, (1,), FIRST_LIMIT)
+    theirs_far = other_core(sent)
+    mine_near, sent = sort_columns(at, tokens, (0,), FIRST_LIMIT)
+    theirs_near = other_core(sent)
+    sent_0, *held = vmem_call(
+        functools.partial(gradient_far_kernel, parts),
+        [bf16(p, half // 2) for p in parts],
+        "gradient_far",
+        flops // 2,
+        mine_far,
+        theirs_far,
         cotangent,
         their_cot,
     )
+    kept_0, *halves = vmem_call(
+        functools.partial(gradient_near_kernel, parts),
+        [bf16(parts[0], half // 2)] + [bf16(p, half // 2) for p in parts[1:] for _ in range(2)],
+        "gradient_near",
+        flops // 2,
+        mine_near,
+        theirs_near,
+        cotangent,
+        their_cot,
+        *held,
+    )
+    halves = [kept_0, sent_0] + halves
     last = []
     for p in range(3):
         kept, sent = halves[2 * p : 2 * p + 2]
@@ -237,7 +276,7 @@
         moment_two,
     )
 
-    next_mine, next_sent = sort_columns(at, next_tokens, VMEM_LIMIT)
+    next_mine, next_sent = sort_columns(at, next_tokens, (0, 1), VMEM_LIMIT)
     next_theirs = other_core(next_sent)
     copies = lax.all_to_all(copies, AXES, 0, 0, tiled=True, axis_index_groups=groups())
     held = vmem_call(
@@ -256,8 +295,14 @@
                 own = jnp.concatenate([own, came], axis=1)
         owns.append(own)
         cames.append(came)
-    before = vmem_call(
-        forward_own_kernel, [f32(2 * t, p) for p in parts], "forward_own", flops // 2, next_mine, next_theirs, *owns
+    *before, next_theirs = vmem_call(
+        forward_own_kernel,
+        [f32(2 * t, p) for p in parts] + [bf16(*next_theirs.shape)],
+        "forward_own",
+        flops // 2,
+        next_mine,
+        next_theirs,
+        *owns,
     )
     (their_out,) = vmem_call(
         functools.partial(forward_kernel, t), [bf16(t, f)], "forward_theirs", flops // 4, next_theirs, *cames, *before

time: 134 us -> 134 us (level)
    pallas_call x2 -> x3, Pallas kernels: 10 us -> 11.8 us  [sort_columns(): pl.pallas_call(functools.partial(sort_kernel, sides), in_specs=[pl.BlockS...]
    ppermute x22 -> x23, waiting for transfers between devices: 21.8 us -> 20.2 us  [permute(): return lax.ppermute(value, AXES, [(d, target(d)) for d in range(DEVICES)])]
    pallas_call x7 -> x8, Pallas kernels: 11 us -> 9.84 us  [vmem_call(): pl.pallas_call(kernel, in_specs=[space] * len(operands), out_specs=[space...]
    ppermute x22 -> x23, starting transfers between devices: 47.2 us -> 47.7 us  [permute(): return lax.ppermute(value, AXES, [(d, target(d)) for d in range(DEVICES)])]
  transfers between devices with their start and end apart: 23 -> 24, of which waited for: 12 -> 12; matrix products, arithmetic and copies ran while one was open for 1% -> 1% of each run, Pallas kernels for 8% -> 11%
where the time goes in v3:
time: 134 us; the launch traced here: 133 us
  starting transfers between devices  52 us (39%)
  waiting for transfers between devices  29 us (22%)
  blocking collectives  25.2 us (19%)
  Pallas kernels  21.6 us (16%)
  local copies, waits for them, and re-layouts  2.65 us (2%)
  other arithmetic  1.7 us (1%)
    ppermute x23, starting transfers between devices, permute(): return lax.ppermute(value, AXES, [(d, target(d)) for d in range(DEVICES)])  47.7 us
    all_to_all x1, blocking collectives, on_device(): lax.all_to_all(partial, AXES, 0, 0, tiled=True, axis_index_groups=groups())  25.2 us
    ppermute x23, waiting for transfers between devices, permute(): return lax.ppermute(value, AXES, [(d, target(d)) for d in range(DEVICES)])  20.2 us
    pallas_call x3, Pallas kernels, sort_columns(): pl.pallas_call(functools.partial(sort_kernel, sides), in_specs=[pl.BlockS...  11.8 us
    pallas_call x8, Pallas kernels, vmem_call(): pl.pallas_call(kernel, in_specs=[space] * len(operands), out_specs=[space...  9.84 us
    all_to_all x1, waiting for transfers between devices, on_device(): lax.all_to_all(copies, AXES, 0, 0, tiled=True, axis_index_groups=groups())  8.89 us
    all_to_all x1, starting transfers between devices, on_device(): lax.all_to_all(copies, AXES, 0, 0, tiled=True, axis_index_groups=groups())  4.23 us
  transfers between devices with their start and end apart: 24, of which 12 were waited for; matrix products, arithmetic and copies ran while one was open for 1% of the time, Pallas kernels for 11%

profile of v3, /device:TPU:1, one launch (start us, length us, event | category | flops | bytes accessed | tf_op | source)
XLA Modules:
  0.0 133.3 jit_solution(10127713785483668932)
XLA Ops:
  0.8 3.2 %sort_columns.4 = (bf16[2,8,256,128]{3,2,1,0:T(8,128)(2,1)S(1)}, bf16[2,8,256,128]{3,2,1,0:T(8,128)(2,1)S(1)}) custom-call(s32[4]{0:T(128)S(1)} %pad_add_fusion.at_ref, bf16[256,8192]{1,0:T(8,128)(2,1)} %in_ref.4), custom_call_target="tpu_custom_call" | custom-call | flops 1073741824 | bytes 4194304 | tf_op jit(solution)/shard_map/sort_columns/pallas_call | solution.py:85
  4.0 3.3 %collective-permute-start.2 = (bf16[2,8,256,128]{3,2,1,0:T(8,128)(2,1)S(1)}, bf16[2,8,256,128]{3,2,1,0:T(8,128)(2,1)S(1)}, u32[]{:S(2)}, u32[]{:S(2)}) collective-permute-start(bf16[2,8,256,128]{3,2,1,0:T(8,128)(2,1)S(1)} %get-tuple-element.32), channel_id=1, source_target_pairs={{0,1},{1,0},{2,3},{3,2},{4,5},{5,4},{6,7},{7,6},{8,9},{9,8},{10,11... | collective-permute-start | bytes 3145736 | tf_op jit(solution)/shard_map/ppermute | solution.py:34
  7.4 3.2 %sort_columns.3 = (bf16[2,8,256,128]{3,2,1,0:T(8,128)(2,1)S(1)}, bf16[2,8,256,128]{3,2,1,0:T(8,128)(2,1)S(1)}) custom-call(s32[4]{0:T(128)S(1)} %pad_add_fusion.at_ref, bf16[256,8192]{1,0:T(8,128)(2,1)} %in_ref.4), custom_call_target="tpu_custom_call" | custom-call | flops 1073741824 | bytes 4194304 | tf_op jit(solution)/shard_map/sort_columns/pallas_call | solution.py:85
  11.2 2.5 %collective-permute-done.1.their_cot_ref = bf16[256,512]{1,0:T(8,128)(2,1)S(1)} collective-permute-done((bf16[256,512]{1,0:T(8,128)(2,1)S(1)}, bf16[256,512]{1,0:T(8,128)(2,1)S(1)}, u32[]{:S(2)}, u32[]{:S(2)}) %collective-permute-start.1) | collective-permute-done | bytes 262176 | tf_op jit(solution)/shard_map/ppermute | solution.py:34
  13.7 1.3 gradient_far.1
  15.0 1.5 %gradient_near.1 = (bf16[176,2048]{1,0:T(8,128)(2,1)S(1)}, bf16[176,2048]{1,0:T(8,128)(2,1)S(1)}, bf16[176,2048]{1,0:T(8,128)(2,1)S(1)}, bf16[160,2048]{1,0:T(8,128)(2,1)S(1)}, bf16[160,2048]{1,0:T(8,128)(2,1)S(1)}) custom-call(bf16[2,8,256,128]{3,2,1,0:T(8,128)(2,1)S(1)} %get-tuple-element.29.mine_ref, ...), custom_call_target="tpu_custom_call" | custom-call | flops 1073741824 | bytes 7471104 | tf_op jit(solution)/shard_map/gradient_near/pallas_call | solution.py:145
  17.5 2.5 %collective-permute-start.3 = (bf16[176,2048]{1,0:T(8,128)(2,1)S(1)}, bf16[176,2048]{1,0:T(8,128)(2,1)S(1)}, u32[]{:S(2)}, u32[]{:S(2)}) collective-permute-start(bf16[176,2048]{1,0:T(8,128)(2,1)S(1)} %get-tuple-element.36), channel_id=1, source_target_pairs={{0,64},{1,193},{2,66},{3,195},{4,68},{5,197},{6,70},{7,199},{8,72}... | collective-permute-start | bytes 2162696 | tf_op jit(solution)/shard_map/ppermute | solution.py:34
  20.0 5.6 %collective-permute-start.9 = (bf16[160,2048]{1,0:T(8,128)(2,1)S(1)}, bf16[160,2048]{1,0:T(8,128)(2,1)S(1)}, u32[]{:S(2)}, u32[]{:S(2)}) collective-permute-start(bf16[160,2048]{1,0:T(8,128)(2,1)S(1)} %get-tuple-element.40), channel_id=1, source_target_pairs={{0,2},{1,15},{2,0},{3,5},{4,6},{5,3},{6,4},{7,9},{8,10},{9,7},{10,... | collective-permute-start | bytes 1966088 | tf_op jit(solution)/shard_map/ppermute | solution.py:34
  25.6 2.3 %collective-permute-done.6 = bf16[176,2048]{1,0:T(8,128)(2,1)S(1)} collective-permute-done((bf16[176,2048]{1,0:T(8,128)(2,1)S(1)}, bf16[176,2048]{1,0:T(8,128)(2,1)S(1)}, u32[]{:S(2)}, u32[]{:S(2)}) %collective-permute-start.6) | collective-permute-done | bytes 720928 | tf_op jit(solution)/shard_map/ppermute | solution.py:34
  28.1 4.0 %collective-permute-start.7 = (bf16[176,1024]{1,0:T(8,128)(2,1)S(1)}, bf16[176,1024]{1,0:T(8,128)(2,1)S(1)}, u32[]{:S(2)}, u32[]{:S(2)}) collective-permute-start(bf16[176,1024]{1,0:T(8,128)(2,1)S(1)} %slice.75), channel_id=1, source_target_pairs={{0,2},{1,15},{2,0},{3,5},{4,6},{5,3},{6,4},{7,9},{8,10},{9,7},{10,... | collective-permute-start | bytes 1081352 | tf_op jit(solution)/shard_map/ppermute | solution.py:34
  32.4 2.8 %collective-permute-start.4 = (bf16[176,1024]{1,0:T(8,128)(2,1)S(1)}, bf16[176,1024]{1,0:T(8,128)(2,1)S(1)}, u32[]{:S(2)}, u32[]{:S(2)}) collective-permute-start(bf16[176,1024]{1,0:T(8,128)(2,1)S(1)} %slice.76), channel_id=1, source_target_pairs={{0,16},{1,49},{2,18},{3,51},{4,20},{5,53},{6,22},{7,55},{8,24},{9,... | collective-permute-start | bytes 1081352 | tf_op jit(solution)/shard_map/ppermute | solution.py:34
  35.3 2.6 %collective-permute-start.10 = (bf16[160,1024]{1,0:T(8,128)(2,1)S(1)}, bf16[160,1024]{1,0:T(8,128)(2,1)S(1)}, u32[]{:S(2)}, u32[]{:S(2)}) collective-permute-start(bf16[160,1024]{1,0:T(8,128)(2,1)S(1)} %slice.77), channel_id=1, source_target_pairs={{0,64},{1,193},{2,66},{3,195},{4,68},{5,197},{6,70},{7,199},{8,72}... | collective-permute-start | bytes 983048 | tf_op jit(solution)/shard_map/ppermute | solution.py:34
  38.0 1.6 %collective-permute-start.8 = (bf16[176,512]{1,0:T(8,128)(2,1)S(1)}, bf16[176,512]{1,0:T(8,128)(2,1)S(1)}, u32[]{:S(2)}, u32[]{:S(2)}) collective-permute-start(bf16[176,512]{1,0:T(8,128)(2,1)S(1)} %slice.78), channel_id=1, source_target_pairs={{0,64},{1,193},{2,66},{3,195},{4,68},{5,197},{6,70},{7,199},{8,72}... | collective-permute-start | bytes 540680 | tf_op jit(solution)/shard_map/ppermute | solution.py:34
  40.1 2.4 %collective-permute-start.5 = (bf16[176,512]{1,0:T(8,128)(2,1)S(1)}, bf16[176,512]{1,0:T(8,128)(2,1)S(1)}, u32[]{:S(2)}, u32[]{:S(2)}) collective-permute-start(bf16[176,512]{1,0:T(8,128)(2,1)S(1)} %slice.79), channel_id=1, source_target_pairs={{0,2},{1,15},{2,0},{3,5},{4,6},{5,3},{6,4},{7,9},{8,10},{9,7},{10,... | collective-permute-start | bytes 540680 | tf_op jit(solution)/shard_map/ppermute | solution.py:34
  42.7 2.9 %collective-permute-start.11 = (bf16[160,512]{1,0:T(8,128)(2,1)S(1)}, bf16[160,512]{1,0:T(8,128)(2,1)S(1)}, u32[]{:S(2)}, u32[]{:S(2)}) collective-permute-start(bf16[160,512]{1,0:T(8,128)(2,1)S(1)} %slice.80), channel_id=1, source_target_pairs={{0,16},{1,49},{2,18},{3,51},{4,20},{5,53},{6,22},{7,55},{8,24},{9,... | collective-permute-start | bytes 491528 | tf_op jit(solution)/shard_map/ppermute | solution.py:34
  45.7 2.6 %collective-permute-done.11.refs_5_ = bf16[160,512]{1,0:T(8,128)(2,1)S(1)} collective-permute-done((bf16[160,512]{1,0:T(8,128)(2,1)S(1)}, bf16[160,512]{1,0:T(8,128)(2,1)S(1)}, u32[]{:S(2)}, u32[]{:S(2)}) %collective-permute-start.11) | collective-permute-done | bytes 163872 | tf_op jit(solution)/shard_map/ppermute | solution.py:34
  48.6 25.2 %all_to_all.10.partial_ref = bf16[16,32,512]{2,1,0:T(8,128)(2,1)S(1)} all-to-all(bf16[16,32,512]{2,1,0:T(8,128)(2,1)S(1)} %bitcast.7), channel_id=1, replica_groups={{0,4,8,12,32,36,40,44,128,132,136,140,160,164,168,172},{1,5,9,13,33,37,..., dimensions={0} | all-to-all | bytes 1048576 | tf_op jit(solution)/shard_map/all_to_all | solution.py:267
  74.8 4.2 %all-to-all-start.1 = ((bf16[16,32,512]{2,1,0:T(8,128)(2,1)}), bf16[16,32,512]{2,1,0:T(8,128)(2,1)S(1)}, u32[]{:S(2)}, u32[]{:S(2)}) async-start(bf16[16,32,512]{2,1,0:T(8,128)(2,1)} %get-tuple-element.45), calls=%async_computation.1 | async-start | bytes 1048576 | tf_op jit(solution)/shard_map/all_to_all | solution.py:281
  79.0 2.2 %copy-done.4 = bf16[256,8192]{1,0:T(8,128)(2,1)S(1)} copy-done((bf16[256,8192]{1,0:T(8,128)(2,1)S(1)}, bf16[256,8192]{1,0:T(8,128)(2,1)}, u32[]{:S(2)}) %copy-start.4) | copy-done | bytes 4194328
  81.2 5.4 %sort_columns.5 = (bf16[4,8,256,128]{3,2,1,0:T(8,128)(2,1)S(1)}, bf16[4,8,256,128]{3,2,1,0:T(8,128)(2,1)}) custom-call(s32[4]{0:T(128)S(1)} %pad_add_fusion.at_ref, bf16[256,8192]{1,0:T(8,128)(2,1)S(1)} %copy-done.4), custom_call_target="tpu_custom_call" | custom-call | flops 2147483648 | bytes 8388608 | tf_op jit(solution)/shard_map/sort_columns/pallas_call | solution.py:85
  86.6 1.6 %collective-permute-start.21 = (bf16[4,8,256,128]{3,2,1,0:T(8,128)(2,1)}, bf16[4,8,256,128]{3,2,1,0:T(8,128)(2,1)}, u32[]{:S(2)}, u32[]{:S(2)}) collective-permute-start(bf16[4,8,256,128]{3,2,1,0:T(8,128)(2,1)} %get-tuple-element.49), channel_id=1, source_target_pairs={{0,1},{1,0},{2,3},{3,2},{4,5},{5,4},{6,7},{7,6},{8,9},{9,8},{10,11... | collective-permute-start | bytes 6291464 | tf_op jit(solution)/shard_map/ppermute | solution.py:34
  88.2 8.9 %all-to-all-done.1 = bf16[16,32,512]{2,1,0:T(8,128)(2,1)S(1)} async-done(((bf16[16,32,512]{2,1,0:T(8,128)(2,1)}), bf16[16,32,512]{2,1,0:T(8,128)(2,1)S(1)}, u32[]{:S(2)}, u32[]{:S(2)}) %all-to-all-start.1) | async-done | bytes 524320 | tf_op jit(solution)/shard_map/all_to_all | solution.py:281
  97.3 3.2 %collective-permute-start.18 = (bf16[160,512]{1,0:T(8,128)(2,1)S(1)}, bf16[160,512]{1,0:T(8,128)(2,1)S(1)}, u32[]{:S(2)}, u32[]{:S(2)}) collective-permute-start(bf16[160,512]{1,0:T(8,128)(2,1)S(1)} %get-tuple-element.48), channel_id=1, source_target_pairs={{0,16},{1,49},{2,18},{3,51},{4,20},{5,53},{6,22},{7,55},{8,24},{9,... | collective-permute-start | bytes 491528 | tf_op jit(solution)/shard_map/ppermute | solution.py:34
  100.5 3.2 %collective-permute-start.15 = (bf16[176,512]{1,0:T(8,128)(2,1)S(1)}, bf16[176,512]{1,0:T(8,128)(2,1)S(1)}, u32[]{:S(2)}, u32[]{:S(2)}) collective-permute-start(bf16[176,512]{1,0:T(8,128)(2,1)S(1)} %get-tuple-element.47), channel_id=1, source_target_pairs={{0,64},{1,193},{2,66},{3,195},{4,68},{5,197},{6,70},{7,199},{8,72}... | collective-permute-start | bytes 540680 | tf_op jit(solution)/shard_map/ppermute | solution.py:34
  103.9 2.6 %collective-permute-start.19 = (bf16[160,1024]{1,0:T(8,128)(2,1)S(1)}, bf16[160,1024]{1,0:T(8,128)(2,1)S(1)}, u32[]{:S(2)}, u32[]{:S(2)}) collective-permute-start(bf16[160,1024]{1,0:T(8,128)(2,1)S(1)} %pad_maximum_fusion.2), channel_id=1, source_target_pairs={{0,64},{1,193},{2,66},{3,195},{4,68},{5,197},{6,70},{7,199},{8,72}... | collective-permute-start | bytes 983048 | tf_op jit(solution)/shard_map/ppermute | solution.py:34
  106.8 2.6 %collective-permute-done.12 = bf16[176,512]{1,0:T(8,128)(2,1)S(1)} collective-permute-done((bf16[176,512]{1,0:T(8,128)(2,1)S(1)}, bf16[176,512]{1,0:T(8,128)(2,1)S(1)}, u32[]{:S(2)}, u32[]{:S(2)}) %collective-permute-start.12) | collective-permute-done | bytes 180256 | tf_op jit(solution)/shard_map/ppermute | solution.py:34
  109.6 4.5 %collective-permute-done.16 = bf16[176,1024]{1,0:T(8,128)(2,1)S(1)} collective-permute-done((bf16[176,1024]{1,0:T(8,128)(2,1)S(1)}, bf16[176,1024]{1,0:T(8,128)(2,1)S(1)}, u32[]{:S(2)}, u32[]{:S(2)}) %collective-permute-start.16) | collective-permute-done | bytes 360480 | tf_op jit(solution)/shard_map/ppermute | solution.py:34
  114.2 2.7 %collective-permute-start.17 = (bf16[176,2048]{1,0:T(8,128)(2,1)S(1)}, bf16[176,2048]{1,0:T(8,128)(2,1)S(1)}, u32[]{:S(2)}, u32[]{:S(2)}) collective-permute-start(bf16[176,2048]{1,0:T(8,128)(2,1)S(1)} %constant_dynamic-update-slice_fusion.3.refs_1_), channel_id=1, source_target_pairs={{0,16},{1,49},{2,18},{3,51},{4,20},{5,53},{6,22},{7,55},{8,24},{9,... | collective-permute-start | bytes 2162696 | tf_op jit(solution)/shard_map/ppermute | solution.py:34
  117.2 2.7 %collective-permute-start.20 = (bf16[160,2048]{1,0:T(8,128)(2,1)S(1)}, bf16[160,2048]{1,0:T(8,128)(2,1)S(1)}, u32[]{:S(2)}, u32[]{:S(2)}) collective-permute-start(bf16[160,2048]{1,0:T(8,128)(2,1)S(1)} %constant_dynamic-update-slice_fusion.6.refs_2_), channel_id=1, source_target_pairs={{0,2},{1,15},{2,0},{3,5},{4,6},{5,3},{6,4},{7,9},{8,10},{9,7},{10,... | collective-permute-start | bytes 1966088 | tf_op jit(solution)/shard_map/ppermute | solution.py:34
  119.9 3.5 %forward_own.1 = (f32[512,176]{1,0:T(8,128)S(1)}, f32[512,176]{1,0:T(8,128)S(1)}, f32[512,160]{1,0:T(8,128)S(1)}, bf16[4,8,256,128]{3,2,1,0:T(8,128)(2,1)S(1)}) custom-call(bf16[4,8,256,128]{3,2,1,0:T(8,128)(2,1)S(1)} %get-tuple-element.44.mine_ref.tokens_ref, bf16[4,8,256,128]{3,2,1,0:T(8,128)(2,1)} %collective-permute-done.21.theirs_ref, ...), custom_call_target="tpu_custom_call" | custom-call | flops 1073741824 | bytes 9437184 | tf_op jit(solution)/shard_map/forward_own/pallas_call | solution.py:145
  123.4 4.5 %collective-permute-done.20.refs_2_ = bf16[160,2048]{1,0:T(8,128)(2,1)S(1)} collective-permute-done((bf16[160,2048]{1,0:T(8,128)(2,1)S(1)}, bf16[160,2048]{1,0:T(8,128)(2,1)S(1)}, u32[]{:S(2)}, u32[]{:S(2)}) %collective-permute-start.20) | collective-permute-done | bytes 655392 | tf_op jit(solution)/shard_map/ppermute | solution.py:34
  129.5 1.8 %collective-permute-start.22 = (bf16[256,512]{1,0:T(8,128)(2,1)S(1)}, bf16[256,512]{1,0:T(8,128)(2,1)S(1)}, u32[]{:S(2)}, u32[]{:S(2)}) collective-permute-start(bf16[256,512]{1,0:T(8,128)(2,1)S(1)} %forward_theirs.1), channel_id=1, source_target_pairs={{0,1},{1,0},{2,3},{3,2},{4,5},{5,4},{6,7},{7,6},{8,9},{9,8},{10,11... | collective-permute-start | bytes 786440 | tf_op jit(solution)/shard_map/ppermute | solution.py:34
  (66 shorter events, 9.1 us)
Async XLA Ops:
  4.0 6.6 %copy-start = (bf16[256,512]{1,0:T(8,128)(2,1)S(1)}, bf16[256,512]{1,0:T(8,128)(2,1)}, u32[]{:S(2)}) copy-start(bf16[256,512]{1,0:T(8,128)(2,1)} %my_cot_ref.3) | copy-start | bytes 786436
  4.0 9.7 %collective-permute-start.2 = (bf16[2,8,256,128]{3,2,1,0:T(8,128)(2,1)S(1)}, bf16[2,8,256,128]{3,2,1,0:T(8,128)(2,1)S(1)}, u32[]{:S(2)}, u32[]{:S(2)}) collective-permute-start(bf16[2,8,256,128]{3,2,1,0:T(8,128)(2,1)S(1)} %get-tuple-element.32), channel_id=1, source_target_pairs={{0,1},{1,0},{2,3},{3,2},{4,5},{5,4},{6,7},{7,6},{8,9},{9,8},{10,11... | collective-permute-start | bytes 3145736 | tf_op jit(solution)/shard_map/ppermute | solution.py:34
  10.6 4.4 %collective-permute-start = (bf16[2,8,256,128]{3,2,1,0:T(8,128)(2,1)S(1)}, bf16[2,8,256,128]{3,2,1,0:T(8,128)(2,1)S(1)}, u32[]{:S(2)}, u32[]{:S(2)}) collective-permute-start(bf16[2,8,256,128]{3,2,1,0:T(8,128)(2,1)S(1)} %get-tuple-element.30), channel_id=1, source_target_pairs={{0,1},{1,0},{2,3},{3,2},{4,5},{5,4},{6,7},{7,6},{8,9},{9,8},{10,11... | collective-permute-start | bytes 3145736 | tf_op jit(solution)/shard_map/ppermute | solution.py:34
  10.7 3.0 %collective-permute-start.1 = (bf16[256,512]{1,0:T(8,128)(2,1)S(1)}, bf16[256,512]{1,0:T(8,128)(2,1)S(1)}, u32[]{:S(2)}, u32[]{:S(2)}) collective-permute-start(bf16[256,512]{1,0:T(8,128)(2,1)S(1)} %copy-done), channel_id=1, source_target_pairs={{0,1},{1,0},{2,3},{3,2},{4,5},{5,4},{6,7},{7,6},{8,9},{9,8},{10,11... | collective-permute-start | bytes 786440 | tf_op jit(solution)/shard_map/ppermute | solution.py:34
  16.4 11.4 %collective-permute-start.6 = (bf16[176,2048]{1,0:T(8,128)(2,1)S(1)}, bf16[176,2048]{1,0:T(8,128)(2,1)S(1)}, u32[]{:S(2)}, u32[]{:S(2)}) collective-permute-start(bf16[176,2048]{1,0:T(8,128)(2,1)S(1)} %get-tuple-element.38), channel_id=1, source_target_pairs={{0,16},{1,49},{2,18},{3,51},{4,20},{5,53},{6,22},{7,55},{8,24},{9,... | collective-permute-start | bytes 2162696 | tf_op jit(solution)/shard_map/ppermute | solution.py:34
  17.5 14.6 %collective-permute-start.3 = (bf16[176,2048]{1,0:T(8,128)(2,1)S(1)}, bf16[176,2048]{1,0:T(8,128)(2,1)S(1)}, u32[]{:S(2)}, u32[]{:S(2)}) collective-permute-start(bf16[176,2048]{1,0:T(8,128)(2,1)S(1)} %get-tuple-element.36), channel_id=1, source_target_pairs={{0,64},{1,193},{2,66},{3,195},{4,68},{5,197},{6,70},{7,199},{8,72}... | collective-permute-start | bytes 2162696 | tf_op jit(solution)/shard_map/ppermute | solution.py:34
  20.0 15.1 %collective-permute-start.9 = (bf16[160,2048]{1,0:T(8,128)(2,1)S(1)}, bf16[160,2048]{1,0:T(8,128)(2,1)S(1)}, u32[]{:S(2)}, u32[]{:S(2)}) collective-permute-start(bf16[160,2048]{1,0:T(8,128)(2,1)S(1)} %get-tuple-element.40), channel_id=1, source_target_pairs={{0,2},{1,15},{2,0},{3,5},{4,6},{5,3},{6,4},{7,9},{8,10},{9,7},{10,... | collective-permute-start | bytes 1966088 | tf_op jit(solution)/shard_map/ppermute | solution.py:34
  28.1 9.8 %collective-permute-start.7 = (bf16[176,1024]{1,0:T(8,128)(2,1)S(1)}, bf16[176,1024]{1,0:T(8,128)(2,1)S(1)}, u32[]{:S(2)}, u32[]{:S(2)}) collective-permute-start(bf16[176,1024]{1,0:T(8,128)(2,1)S(1)} %slice.75), channel_id=1, source_target_pairs={{0,2},{1,15},{2,0},{3,5},{4,6},{5,3},{6,4},{7,9},{8,10},{9,7},{10,... | collective-permute-start | bytes 1081352 | tf_op jit(solution)/shard_map/ppermute | solution.py:34
  32.4 7.6 %collective-permute-start.4 = (bf16[176,1024]{1,0:T(8,128)(2,1)S(1)}, bf16[176,1024]{1,0:T(8,128)(2,1)S(1)}, u32[]{:S(2)}, u32[]{:S(2)}) collective-permute-start(bf16[176,1024]{1,0:T(8,128)(2,1)S(1)} %slice.76), channel_id=1, source_target_pairs={{0,16},{1,49},{2,18},{3,51},{4,20},{5,53},{6,22},{7,55},{8,24},{9,... | collective-permute-start | bytes 1081352 | tf_op jit(solution)/shard_map/ppermute | solution.py:34
  35.3 7.2 %collective-permute-start.10 = (bf16[160,1024]{1,0:T(8,128)(2,1)S(1)}, bf16[160,1024]{1,0:T(8,128)(2,1)S(1)}, u32[]{:S(2)}, u32[]{:S(2)}) collective-permute-start(bf16[160,1024]{1,0:T(8,128)(2,1)S(1)} %slice.77), channel_id=1, source_target_pairs={{0,64},{1,193},{2,66},{3,195},{4,68},{5,197},{6,70},{7,199},{8,72}... | collective-permute-start | bytes 983048 | tf_op jit(solution)/shard_map/ppermute | solution.py:34
  38.0 10.3 %collective-permute-start.8 = (bf16[176,512]{1,0:T(8,128)(2,1)S(1)}, bf16[176,512]{1,0:T(8,128)(2,1)S(1)}, u32[]{:S(2)}, u32[]{:S(2)}) collective-permute-start(bf16[176,512]{1,0:T(8,128)(2,1)S(1)} %slice.78), channel_id=1, source_target_pairs={{0,64},{1,193},{2,66},{3,195},{4,68},{5,197},{6,70},{7,199},{8,72}... | collective-permute-start | bytes 540680 | tf_op jit(solution)/shard_map/ppermute | solution.py:34
  40.1 8.3 %collective-permute-start.5 = (bf16[176,512]{1,0:T(8,128)(2,1)S(1)}, bf16[176,512]{1,0:T(8,128)(2,1)S(1)}, u32[]{:S(2)}, u32[]{:S(2)}) collective-permute-start(bf16[176,512]{1,0:T(8,128)(2,1)S(1)} %slice.79), channel_id=1, source_target_pairs={{0,2},{1,15},{2,0},{3,5},{4,6},{5,3},{6,4},{7,9},{8,10},{9,7},{10,... | collective-permute-start | bytes 540680 | tf_op jit(solution)/shard_map/ppermute | solution.py:34
  42.7 5.6 %collective-permute-start.11 = (bf16[160,512]{1,0:T(8,128)(2,1)S(1)}, bf16[160,512]{1,0:T(8,128)(2,1)S(1)}, u32[]{:S(2)}, u32[]{:S(2)}) collective-permute-start(bf16[160,512]{1,0:T(8,128)(2,1)S(1)} %slice.80), channel_id=1, source_target_pairs={{0,16},{1,49},{2,18},{3,51},{4,20},{5,53},{6,22},{7,55},{8,24},{9,... | collective-permute-start | bytes 491528 | tf_op jit(solution)/shard_map/ppermute | solution.py:34
  45.7 28.1 %copy-start.1 = (f32[32,512]{1,0:T(8,128)S(1)}, f32[32,512]{1,0:T(8,128)}, u32[]{:S(2)}) copy-start(f32[32,512]{1,0:T(8,128)} %master_ref.1) | copy-start | bytes 196612
  45.7 28.1 %copy-start.2 = (f32[32,512]{1,0:T(8,128)S(1)}, f32[32,512]{1,0:T(8,128)}, u32[]{:S(2)}) copy-start(f32[32,512]{1,0:T(8,128)} %one_ref.1) | copy-start | bytes 196612
  45.7 28.1 %copy-start.3 = (f32[32,512]{1,0:T(8,128)S(1)}, f32[32,512]{1,0:T(8,128)}, u32[]{:S(2)}) copy-start(f32[32,512]{1,0:T(8,128)} %two_ref.1) | copy-start | bytes 196612
  74.8 22.3 %all-to-all-start.1 = ((bf16[16,32,512]{2,1,0:T(8,128)(2,1)}), bf16[16,32,512]{2,1,0:T(8,128)(2,1)S(1)}, u32[]{:S(2)}, u32[]{:S(2)}) async-start(bf16[16,32,512]{2,1,0:T(8,128)(2,1)} %get-tuple-element.45), calls=%async_computation.1 | async-start | bytes 1048576 | tf_op jit(solution)/shard_map/all_to_all | solution.py:281
  79.0 2.2 %copy-start.4 = (bf16[256,8192]{1,0:T(8,128)(2,1)S(1)}, bf16[256,8192]{1,0:T(8,128)(2,1)}, u32[]{:S(2)}) copy-start(bf16[256,8192]{1,0:T(8,128)(2,1)} %in_ref.5) | copy-start | bytes 12582916
  86.6 33.3 %collective-permute-start.21 = (bf16[4,8,256,128]{3,2,1,0:T(8,128)(2,1)}, bf16[4,8,256,128]{3,2,1,0:T(8,128)(2,1)}, u32[]{:S(2)}, u32[]{:S(2)}) collective-permute-start(bf16[4,8,256,128]{3,2,1,0:T(8,128)(2,1)} %get-tuple-element.49), channel_id=1, source_target_pairs={{0,1},{1,0},{2,3},{3,2},{4,5},{5,4},{6,7},{7,6},{8,9},{9,8},{10,11... | collective-permute-start | bytes 6291464 | tf_op jit(solution)/shard_map/ppermute | solution.py:34
  97.3 6.5 %collective-permute-start.18 = (bf16[160,512]{1,0:T(8,128)(2,1)S(1)}, bf16[160,512]{1,0:T(8,128)(2,1)S(1)}, u32[]{:S(2)}, u32[]{:S(2)}) collective-permute-start(bf16[160,512]{1,0:T(8,128)(2,1)S(1)} %get-tuple-element.48), channel_id=1, source_target_pairs={{0,16},{1,49},{2,18},{3,51},{4,20},{5,53},{6,22},{7,55},{8,24},{9,... | collective-permute-start | bytes 491528 | tf_op jit(solution)/shard_map/ppermute | solution.py:34
  100.5 6.1 %collective-permute-start.15 = (bf16[176,512]{1,0:T(8,128)(2,1)S(1)}, bf16[176,512]{1,0:T(8,128)(2,1)S(1)}, u32[]{:S(2)}, u32[]{:S(2)}) collective-permute-start(bf16[176,512]{1,0:T(8,128)(2,1)S(1)} %get-tuple-element.47), channel_id=1, source_target_pairs={{0,64},{1,193},{2,66},{3,195},{4,68},{5,197},{6,70},{7,199},{8,72}... | collective-permute-start | bytes 540680 | tf_op jit(solution)/shard_map/ppermute | solution.py:34
  103.7 5.6 %collective-permute-start.12 = (bf16[176,512]{1,0:T(8,128)(2,1)S(1)}, bf16[176,512]{1,0:T(8,128)(2,1)S(1)}, u32[]{:S(2)}, u32[]{:S(2)}) collective-permute-start(bf16[176,512]{1,0:T(8,128)(2,1)S(1)} %get-tuple-element.46), channel_id=1, source_target_pairs={{0,2},{1,15},{2,0},{3,5},{4,6},{5,3},{6,4},{7,9},{8,10},{9,7},{10,... | collective-permute-start | bytes 540680 | tf_op jit(solution)/shard_map/ppermute | solution.py:34
  103.9 13.3 %collective-permute-start.19 = (bf16[160,1024]{1,0:T(8,128)(2,1)S(1)}, bf16[160,1024]{1,0:T(8,128)(2,1)S(1)}, u32[]{:S(2)}, u32[]{:S(2)}) collective-permute-start(bf16[160,1024]{1,0:T(8,128)(2,1)S(1)} %pad_maximum_fusion.2), channel_id=1, source_target_pairs={{0,64},{1,193},{2,66},{3,195},{4,68},{5,197},{6,70},{7,199},{8,72}... | collective-permute-start | bytes 983048 | tf_op jit(solution)/shard_map/ppermute | solution.py:34
  106.6 7.6 %collective-permute-start.16 = (bf16[176,1024]{1,0:T(8,128)(2,1)S(1)}, bf16[176,1024]{1,0:T(8,128)(2,1)S(1)}, u32[]{:S(2)}, u32[]{:S(2)}) collective-permute-start(bf16[176,1024]{1,0:T(8,128)(2,1)S(1)} %pad_maximum_fusion.1), channel_id=1, source_target_pairs={{0,2},{1,15},{2,0},{3,5},{4,6},{5,3},{6,4},{7,9},{8,10},{9,7},{10,... | collective-permute-start | bytes 1081352 | tf_op jit(solution)/shard_map/ppermute | solution.py:34
  109.4 7.6 %collective-permute-start.13 = (bf16[176,1024]{1,0:T(8,128)(2,1)S(1)}, bf16[176,1024]{1,0:T(8,128)(2,1)S(1)}, u32[]{:S(2)}, u32[]{:S(2)}) collective-permute-start(bf16[176,1024]{1,0:T(8,128)(2,1)S(1)} %pad_maximum_fusion), channel_id=1, source_target_pairs={{0,16},{1,49},{2,18},{3,51},{4,20},{5,53},{6,22},{7,55},{8,24},{9,... | collective-permute-start | bytes 1081352 | tf_op jit(solution)/shard_map/ppermute | solution.py:34
  114.2 13.7 %collective-permute-start.17 = (bf16[176,2048]{1,0:T(8,128)(2,1)S(1)}, bf16[176,2048]{1,0:T(8,128)(2,1)S(1)}, u32[]{:S(2)}, u32[]{:S(2)}) collective-permute-start(bf16[176,2048]{1,0:T(8,128)(2,1)S(1)} %constant_dynamic-update-slice_fusion.3.refs_1_), channel_id=1, source_target_pairs={{0,16},{1,49},{2,18},{3,51},{4,20},{5,53},{6,22},{7,55},{8,24},{9,... | collective-permute-start | bytes 2162696 | tf_op jit(solution)/shard_map/ppermute | solution.py:34
  117.0 11.4 %collective-permute-start.14 = (bf16[176,2048]{1,0:T(8,128)(2,1)S(1)}, bf16[176,2048]{1,0:T(8,128)(2,1)S(1)}, u32[]{:S(2)}, u32[]{:S(2)}) collective-permute-start(bf16[176,2048]{1,0:T(8,128)(2,1)S(1)} %constant_dynamic-update-slice_fusion.refs_0_), channel_id=1, source_target_pairs={{0,64},{1,193},{2,66},{3,195},{4,68},{5,197},{6,70},{7,199},{8,72}... | collective-permute-start | bytes 2162696 | tf_op jit(solution)/shard_map/ppermute | solution.py:34
  117.2 10.7 %collective-permute-start.20 = (bf16[160,2048]{1,0:T(8,128)(2,1)S(1)}, bf16[160,2048]{1,0:T(8,128)(2,1)S(1)}, u32[]{:S(2)}, u32[]{:S(2)}) collective-permute-start(bf16[160,2048]{1,0:T(8,128)(2,1)S(1)} %constant_dynamic-update-slice_fusion.6.refs_2_), channel_id=1, source_target_pairs={{0,2},{1,15},{2,0},{3,5},{4,6},{5,3},{6,4},{7,9},{8,10},{9,7},{10,... | collective-permute-start | bytes 1966088 | tf_op jit(solution)/shard_map/ppermute | solution.py:34
  129.5 3.0 %collective-permute-start.22 = (bf16[256,512]{1,0:T(8,128)(2,1)S(1)}, bf16[256,512]{1,0:T(8,128)(2,1)S(1)}, u32[]{:S(2)}, u32[]{:S(2)}) collective-permute-start(bf16[256,512]{1,0:T(8,128)(2,1)S(1)} %forward_theirs.1), channel_id=1, source_target_pairs={{0,1},{1,0},{2,3},{3,2},{4,5},{5,4},{6,7},{7,6},{8,9},{9,8},{10,11... | collective-permute-start | bytes 786440 | tf_op jit(solution)/shard_map/ppermute | solution.py:34

commit v4 on v2

--- a/solution.py
+++ b/solution.py
@@ -34,11 +34,16 @@
     return lax.ppermute(value, AXES, [(d, target(d)) for d in range(DEVICES)])
 
 
+def twin(d):
+    x, y, z, c = coordinates(d)
+    return flat(x, y, z ^ 4, c)
+
+
 def groups():
     seen = {}
     for d in range(DEVICES):
         x, y, z, c = coordinates(d)
-        seen.setdefault((x % 2, y % 2, z % 2, c), []).append(d)
+        seen.setdefault((x % 2, y % 2, z % 2, z // 4, c), []).append(d)
     return list(seen.values())
 
 
@@ -64,8 +69,8 @@
     n = 4 * LANES
     source = lax.broadcasted_iota(jnp.int32, (n, n), 0)
     goal = lax.broadcasted_iota(jnp.int32, (n, n), 1)
-    q, r, row = goal // 128, goal // 32 % 4, goal % 32
-    wanted = r * 128 + (((q % 2) ^ z0) * 2 + ((q // 2) ^ c)) * 32 + row
+    q, z1, z2, row = goal // 128, goal // 64 % 2, goal // 32 % 2, goal % 32
+    wanted = (z2 * 2 + z1) * 128 + (((q % 2) ^ z0) * 2 + ((q // 2) ^ c)) * 32 + row
     move = jnp.where(source == wanted, 1.0, 0.0).astype(my_ref.dtype)
     for i in range(4):
         copies[i].wait()
@@ -115,18 +120,18 @@
                             ]
 
 
-def vmem_call(kernel, outs, name, flops, *operands):
+def vmem_call(kernel, outs, name, flops, *operands, scalars=()):
     size = sum(a.size * a.dtype.itemsize for a in operands) + sum(o.size * o.dtype.itemsize for o in outs)
     space = pl.BlockSpec(memory_space=pltpu.VMEM)
     return pl.pallas_call(
         kernel,
-        in_specs=[space] * len(operands),
+        in_specs=[pl.BlockSpec(memory_space=pltpu.SMEM)] * len(scalars) + [space] * len(operands),
         out_specs=[space] * len(outs),
         out_shape=outs,
         compiler_params=pltpu.CompilerParams(vmem_limit_bytes=VMEM_LIMIT),
         cost_estimate=pl.CostEstimate(flops=flops, bytes_accessed=size, transcendentals=0),
         name=name,
-    )(*operands)
+    )(*scalars, *operands)
 
 
 def rows_kernel(*refs):
@@ -161,6 +166,7 @@
 def forward_own_kernel(mine_ref, theirs_ref, *refs):
     for p in range(3):
         refs[3 + p][...] = half_product(p, 0, (mine_ref, theirs_ref), refs[p])
+    refs[6][...] = theirs_ref[...]
 
 
 def forward_kernel(first, tokens_ref, *refs):
@@ -170,8 +176,14 @@
     out_ref[...] = jnp.concatenate(total, axis=1).astype(out_ref.dtype)
 
 
-def update_kernel(scale, partial_ref, master_ref, one_ref, two_ref, new_master, new_one, new_two, copies):
-    gradient = partial_ref[...].astype(jnp.float32).sum(axis=0) * scale
+def split_kernel(at_ref, partial_ref, own_ref, other_ref):
+    z2 = at_ref[4]
+    own_ref[...] = partial_ref[:, z2].astype(jnp.float32).sum(axis=0)
+    other_ref[...] = partial_ref[:, 1 - z2].astype(jnp.float32).sum(axis=0).astype(other_ref.dtype)
+
+
+def update_kernel(scale, own_ref, came_ref, master_ref, one_ref, two_ref, new_master, new_one, new_two, weights):
+    gradient = (own_ref[...] + came_ref[...].astype(jnp.float32)) * scale
     one = 0.9 * one_ref[...] + 0.1 * gradient
     two = 0.999 * two_ref[...] + 0.001 * gradient * gradient
     first = one / (1.0 - 0.9**10)
@@ -181,7 +193,14 @@
     new_one[...] = one
     new_two[...] = two
     new_master[...] = master
-    copies[...] = jnp.broadcast_to(master.astype(copies.dtype)[None], copies.shape)
+    weights[...] = master.astype(weights.dtype)
+
+
+def copies_kernel(at_ref, own_ref, came_ref, out_ref):
+    z2 = at_ref[4]
+    for i in range(out_ref.shape[0]):
+        out_ref[i, z2] = own_ref[...]
+        out_ref[i, 1 - z2] = came_ref[...]
 
 
 def halved(value):
@@ -196,7 +215,7 @@
     parts = part_rows(f)
     me = lax.axis_index("grp") * 32 + lax.axis_index("intra")
     x, y, z, c = coordinates(me)
-    at = jnp.stack([c, x % 2, y % 2, z % 2]).astype(jnp.int32)
+    at = jnp.stack([c, x % 2, y % 2, z % 2, z // 4]).astype(jnp.int32)
     bf16 = lambda *shape: jax.ShapeDtypeStruct(shape, jnp.bfloat16)
     f32 = lambda *shape: jax.ShapeDtypeStruct(shape, jnp.float32)
     other_core = lambda v: permute(v, lambda d: d ^ 1)
@@ -215,29 +234,36 @@
         cotangent,
         their_cot,
     )
+    later, *halves = lax.optimization_barrier((at, *halves))
+    next_mine, next_sent = sort_columns(later, next_tokens, VMEM_LIMIT)
     last = []
     for p in range(3):
         kept, sent = halves[2 * p : 2 * p + 2]
         for i, axis in enumerate(ORDER[p]):
             came = permute(sent.astype(jnp.bfloat16), lambda d: neighbour(d, axis))
+            if p == 0 and i == 0:
+                came, next_sent = lax.optimization_barrier((came, next_sent))
             if i < 2:
                 kept, sent = halved(kept.astype(jnp.float32) + came.astype(jnp.float32))
         last += [kept, came]
     (partial,) = vmem_call(rows_kernel, [bf16(16 * rows, f)], "rows", 0, *last)
-    partial = partial.reshape(16, rows, f)
-    partial = lax.all_to_all(partial, AXES, 0, 0, tiled=True, axis_index_groups=groups())
-    new_master, new_moment_one, new_moment_two, copies = vmem_call(
+    partial = lax.all_to_all(partial.reshape(8, 2, rows, f), AXES, 0, 0, tiled=True, axis_index_groups=groups())
+    own, other = vmem_call(split_kernel, [f32(rows, f), bf16(rows, f)], "split", 0, partial, scalars=[at])
+    new_master, new_moment_one, new_moment_two, weights = vmem_call(
         functools.partial(update_kernel, 1.0 / (t * DEVICES)),
-        [f32(rows, f)] * 3 + [bf16(16, rows, f)],
+        [f32(rows, f)] * 3 + [bf16(rows, f)],
         "update",
         0,
-        partial,
+        own,
+        permute(other, twin),
         master,
         moment_one,
         moment_two,
     )
-
-    next_mine, next_sent = sort_columns(at, next_tokens, VMEM_LIMIT)
+    (copies,) = vmem_call(
+        copies_kernel, [bf16(8, 2, rows, f)], "copies", 0, weights, permute(weights, twin), scalars=[at]
+    )
+
     next_theirs = other_core(next_sent)
     copies = lax.all_to_all(copies, AXES, 0, 0, tiled=True, axis_index_groups=groups())
     held = vmem_call(
@@ -256,8 +282,14 @@
                 own = jnp.concatenate([own, came], axis=1)
         owns.append(own)
         cames.append(came)
-    before = vmem_call(
-        forward_own_kernel, [f32(2 * t, p) for p in parts], "forward_own", flops // 2, next_mine, next_theirs, *owns
+    *before, next_theirs = vmem_call(
+        forward_own_kernel,
+        [f32(2 * t, p) for p in parts] + [bf16(*next_theirs.shape)],
+        "forward_own",
+        flops // 2,
+        next_mine,
+        next_theirs,
+        *owns,
     )
     (their_out,) = vmem_call(
         functools.partial(forward_kernel, t), [bf16(t, f)], "forward_theirs", flops // 4, next_theirs, *cames, *before

time: 134 us -> 141 us (1.052)
  waiting for transfers between devices: 30.3 us -> 44.3 us
  blocking collectives: 25.2 us -> 21.1 us
    ppermute x22 -> x24, waiting for transfers between devices: 21.8 us -> 30.4 us  [permute(): return lax.ppermute(value, AXES, [(d, target(d)) for d in range(DEVICES)])]
    all_to_all x1, waiting for transfers between devices: 8.55 us -> 13.8 us  [on_device(): lax.all_to_all(copies, AXES, 0, 0, tiled=True, axis_index_groups=groups())]
    all_to_all x1, blocking collectives: 25.2 us -> 21.1 us  [on_device(): lax.all_to_all(partial.reshape(8, 2, rows, f), AXES, 0, 0, tiled=True, ax...]
    ppermute x22 -> x24, starting transfers between devices: 47.2 us -> 47.5 us  [permute(): return lax.ppermute(value, AXES, [(d, target(d)) for d in range(DEVICES)])]
    pallas_call x7 -> x9, Pallas kernels: 11 us -> 11.2 us  [vmem_call(): pl.pallas_call(kernel, in_specs=[pl.BlockSpec(memory_space=pltpu.SMEM)] *...]
  transfers between devices with their start and end apart: 23 -> 25, of which waited for: 12 -> 15; matrix products, arithmetic and copies ran while one was open for 1% -> 1% of each run, Pallas kernels for 8% -> 6%
where the time goes in v4:
time: 141 us
  starting transfers between devices  51 us (36%)
  waiting for transfers between devices  44.3 us (31%)
  blocking collectives  21.1 us (15%)
  Pallas kernels  19.9 us (14%)
  local copies, waits for them, and re-layouts  1.7 us (1%)
  other arithmetic  1.66 us (1%)
    ppermute x24, starting transfers between devices, permute(): return lax.ppermute(value, AXES, [(d, target(d)) for d in range(DEVICES)])  47.5 us
    ppermute x24, waiting for transfers between devices, permute(): return lax.ppermute(value, AXES, [(d, target(d)) for d in range(DEVICES)])  30.4 us
    all_to_all x1, blocking collectives, on_device(): lax.all_to_all(partial.reshape(8, 2, rows, f), AXES, 0, 0, tiled=True, ax...  21.1 us
    all_to_all x1, waiting for transfers between devices, on_device(): lax.all_to_all(copies, AXES, 0, 0, tiled=True, axis_index_groups=groups())  13.8 us
    pallas_call x9, Pallas kernels, vmem_call(): pl.pallas_call(kernel, in_specs=[pl.BlockSpec(memory_space=pltpu.SMEM)] *...  11.2 us
    pallas_call x2, Pallas kernels, sort_columns(): pl.pallas_call(sort_kernel, in_specs=[pl.BlockSpec(memory_space=pltpu.SME...  8.67 us
    all_to_all x1, starting transfers between devices, on_device(): lax.all_to_all(copies, AXES, 0, 0, tiled=True, axis_index_groups=groups())  3.49 us
  transfers between devices with their start and end apart: 25, of which 15 were waited for; matrix products, arithmetic and copies ran while one was open for 1% of the time, Pallas kernels for 6%

profile of v4, /device:TPU:1, one launch (start us, length us, event | category | flops | bytes accessed | tf_op | source)
XLA Modules:
  0.0 140.7 jit_solution(2645259096134800910)
XLA Ops:
  0.8 4.6 %sort_columns.2 = (bf16[4,8,256,128]{3,2,1,0:T(8,128)(2,1)S(1)}, bf16[4,8,256,128]{3,2,1,0:T(8,128)(2,1)S(1)}) custom-call(s32[5]{0:T(128)S(1)} %stack.23.at_ref, bf16[256,8192]{1,0:T(8,128)(2,1)} %in_ref.2), custom_call_target="tpu_custom_call" | custom-call | flops 2147483648 | bytes 8388608 | tf_op jit(solution)/shard_map/sort_columns/pallas_call | solution.py:89
  5.5 3.3 %collective-permute-start = (bf16[4,8,256,128]{3,2,1,0:T(8,128)(2,1)S(1)}, bf16[4,8,256,128]{3,2,1,0:T(8,128)(2,1)S(1)}, u32[]{:S(2)}, u32[]{:S(2)}) collective-permute-start(bf16[4,8,256,128]{3,2,1,0:T(8,128)(2,1)S(1)} %get-tuple-element.37), channel_id=1, source_target_pairs={{0,1},{1,0},{2,3},{3,2},{4,5},{5,4},{6,7},{7,6},{8,9},{9,8},{10,11... | collective-permute-start | bytes 6291464 | tf_op jit(solution)/shard_map/ppermute | solution.py:34
  8.9 4.1 %collective-permute-done.1.their_cot_ref = bf16[256,512]{1,0:T(8,128)(2,1)S(1)} collective-permute-done((bf16[256,512]{1,0:T(8,128)(2,1)S(1)}, bf16[256,512]{1,0:T(8,128)(2,1)S(1)}, u32[]{:S(2)}, u32[]{:S(2)}) %collective-permute-start.1) | collective-permute-done | bytes 262176 | tf_op jit(solution)/shard_map/ppermute | solution.py:34
  13.0 2.4 %gradient.1 = (bf16[176,2048]{1,0:T(8,128)(2,1)S(1)}, bf16[176,2048]{1,0:T(8,128)(2,1)S(1)}, bf16[176,2048]{1,0:T(8,128)(2,1)S(1)}, bf16[176,2048]{1,0:T(8,128)(...) custom-call(bf16[4,8,256,128]{3,2,1,0:T(8,128)(2,1)S(1)} %get-tuple-element.36.mine_ref, ...), custom_call_target="tpu_custom_call" | custom-call | flops 2147483648 | bytes 8912896 | tf_op jit(solution)/shard_map/gradient/pallas_call | solution.py:126
  16.5 5.6 %collective-permute-start.8 = (bf16[160,2048]{1,0:T(8,128)(2,1)S(1)}, bf16[160,2048]{1,0:T(8,128)(2,1)S(1)}, u32[]{:S(2)}, u32[]{:S(2)}) collective-permute-start(bf16[160,2048]{1,0:T(8,128)(2,1)S(1)} %get-tuple-element.52), channel_id=1, source_target_pairs={{0,2},{1,15},{2,0},{3,5},{4,6},{5,3},{6,4},{7,9},{8,10},{9,7},{10,... | collective-permute-start | bytes 1966088 | tf_op jit(solution)/shard_map/ppermute | solution.py:34
  22.0 2.5 %collective-permute-start.2 = (bf16[176,2048]{1,0:T(8,128)(2,1)S(1)}, bf16[176,2048]{1,0:T(8,128)(2,1)S(1)}, u32[]{:S(2)}, u32[]{:S(2)}) collective-permute-start(bf16[176,2048]{1,0:T(8,128)(2,1)S(1)} %get-tuple-element.45), channel_id=1, source_target_pairs={{0,64},{1,193},{2,66},{3,195},{4,68},{5,197},{6,70},{7,199},{8,72}... | collective-permute-start | bytes 2162696 | tf_op jit(solution)/shard_map/ppermute | solution.py:34
  24.5 4.0 %sort_columns.3 = (bf16[4,8,256,128]{3,2,1,0:T(8,128)(2,1)S(1)}, bf16[4,8,256,128]{3,2,1,0:T(8,128)(2,1)S(1)}) custom-call(s32[5]{0:T(128)S(1)} %stack.23.at_ref, bf16[256,8192]{1,0:T(8,128)(2,1)S(1)} %copy-done.3), custom_call_target="tpu_custom_call" | custom-call | flops 2147483648 | bytes 8388608 | tf_op jit(solution)/shard_map/sort_columns/pallas_call | solution.py:89
  28.8 1.1 copy-done.4
  31.0 2.3 %collective-permute-done.2 = bf16[176,2048]{1,0:T(8,128)(2,1)S(1)} collective-permute-done((bf16[176,2048]{1,0:T(8,128)(2,1)S(1)}, bf16[176,2048]{1,0:T(8,128)(2,1)S(1)}, u32[]{:S(2)}, u32[]{:S(2)}) %collective-permute-start.2) | collective-permute-done | bytes 720928 | tf_op jit(solution)/shard_map/ppermute | solution.py:34
  34.3 2.6 %collective-permute-start.9 = (bf16[160,1024]{1,0:T(8,128)(2,1)S(1)}, bf16[160,1024]{1,0:T(8,128)(2,1)S(1)}, u32[]{:S(2)}, u32[]{:S(2)}) collective-permute-start(bf16[160,1024]{1,0:T(8,128)(2,1)S(1)} %slice.77), channel_id=1, source_target_pairs={{0,64},{1,193},{2,66},{3,195},{4,68},{5,197},{6,70},{7,199},{8,72}... | collective-permute-start | bytes 983048 | tf_op jit(solution)/shard_map/ppermute | solution.py:34
  38.8 2.4 %collective-permute-done.3 = bf16[176,1024]{1,0:T(8,128)(2,1)S(1)} collective-permute-done((bf16[176,1024]{1,0:T(8,128)(2,1)S(1)}, bf16[176,1024]{1,0:T(8,128)(2,1)S(1)}, u32[]{:S(2)}, u32[]{:S(2)}) %collective-permute-start.3) | collective-permute-done | bytes 360480 | tf_op jit(solution)/shard_map/ppermute | solution.py:34
  41.8 2.8 %collective-permute-start.10 = (bf16[160,512]{1,0:T(8,128)(2,1)S(1)}, bf16[160,512]{1,0:T(8,128)(2,1)S(1)}, u32[]{:S(2)}, u32[]{:S(2)}) collective-permute-start(bf16[160,512]{1,0:T(8,128)(2,1)S(1)} %slice.80), channel_id=1, source_target_pairs={{0,16},{1,49},{2,18},{3,51},{4,20},{5,53},{6,22},{7,55},{8,24},{9,... | collective-permute-start | bytes 491528 | tf_op jit(solution)/shard_map/ppermute | solution.py:34
  44.7 2.6 %collective-permute-done.10.refs_5_ = bf16[160,512]{1,0:T(8,128)(2,1)S(1)} collective-permute-done((bf16[160,512]{1,0:T(8,128)(2,1)S(1)}, bf16[160,512]{1,0:T(8,128)(2,1)S(1)}, u32[]{:S(2)}, u32[]{:S(2)}) %collective-permute-start.10) | collective-permute-done | bytes 163872 | tf_op jit(solution)/shard_map/ppermute | solution.py:34
  47.5 21.1 %all_to_all.10.partial_ref = bf16[8,2,32,512]{3,2,1,0:T(8,128)(2,1)S(1)} all-to-all(bf16[8,2,32,512]{3,2,1,0:T(8,128)(2,1)S(1)} %bitcast.8), channel_id=1, replica_groups={{0,4,32,36,128,132,160,164},{1,5,33,37,129,133,161,165},{2,6,34,38,130,..., dimensions={0} | all-to-all | bytes 1048576 | tf_op jit(solution)/shard_map/all_to_all | solution.py:250
  69.2 4.0 %collective-permute-start.11 = (bf16[32,512]{1,0:T(8,128)(2,1)S(1)}, bf16[32,512]{1,0:T(8,128)(2,1)S(1)}, u32[]{:S(2)}, u32[]{:S(2)}) collective-permute-start(bf16[32,512]{1,0:T(8,128)(2,1)S(1)} %get-tuple-element.54), channel_id=1, source_target_pairs={{0,8},{1,9},{2,10},{3,11},{4,12},{5,13},{6,14},{7,15},{8,0},{9,1},... | collective-permute-start | bytes 98312 | tf_op jit(solution)/shard_map/ppermute | solution.py:34
  73.2 2.8 %collective-permute-done.11.came_ref = bf16[32,512]{1,0:T(8,128)(2,1)S(1)} collective-permute-done((bf16[32,512]{1,0:T(8,128)(2,1)S(1)}, bf16[32,512]{1,0:T(8,128)(2,1)S(1)}, u32[]{:S(2)}, u32[]{:S(2)}) %collective-permute-start.11) | collective-permute-done | bytes 32800 | tf_op jit(solution)/shard_map/ppermute | solution.py:34
  76.8 3.9 %collective-permute-start.12 = (bf16[32,512]{1,0:T(8,128)(2,1)S(1)}, bf16[32,512]{1,0:T(8,128)(2,1)S(1)}, u32[]{:S(2)}, u32[]{:S(2)}) collective-permute-start(bf16[32,512]{1,0:T(8,128)(2,1)S(1)} %get-tuple-element.59.own_ref), channel_id=1, source_target_pairs={{0,8},{1,9},{2,10},{3,11},{4,12},{5,13},{6,14},{7,15},{8,0},{9,1},... | collective-permute-start | bytes 98312 | tf_op jit(solution)/shard_map/ppermute | solution.py:34
  80.7 2.7 %collective-permute-done.12.came_ref = bf16[32,512]{1,0:T(8,128)(2,1)S(1)} collective-permute-done((bf16[32,512]{1,0:T(8,128)(2,1)S(1)}, bf16[32,512]{1,0:T(8,128)(2,1)S(1)}, u32[]{:S(2)}, u32[]{:S(2)}) %collective-permute-start.12) | collective-permute-done | bytes 32800 | tf_op jit(solution)/shard_map/ppermute | solution.py:34
  83.4 1.4 copies.1
  84.8 3.5 %all-to-all-start.1 = ((bf16[8,2,32,512]{3,2,1,0:T(8,128)(2,1)}), bf16[8,2,32,512]{3,2,1,0:T(8,128)(2,1)S(1)}, u32[]{:S(2)}, u32[]{:S(2)}) async-start(bf16[8,2,32,512]{3,2,1,0:T(8,128)(2,1)} %copies.1), calls=%async_computation.1 | async-start | bytes 1048576 | tf_op jit(solution)/shard_map/all_to_all | solution.py:268
  88.3 4.2 %collective-permute-start.22 = (bf16[4,8,256,128]{3,2,1,0:T(8,128)(2,1)}, bf16[4,8,256,128]{3,2,1,0:T(8,128)(2,1)}, u32[]{:S(2)}, u32[]{:S(2)}) collective-permute-start(bf16[4,8,256,128]{3,2,1,0:T(8,128)(2,1)} %copy-done.4), channel_id=1, source_target_pairs={{0,1},{1,0},{2,3},{3,2},{4,5},{5,4},{6,7},{7,6},{8,9},{9,8},{10,11... | collective-permute-start | bytes 6291464 | tf_op jit(solution)/shard_map/ppermute | solution.py:34
  92.5 13.8 %all-to-all-done.1 = bf16[8,2,32,512]{3,2,1,0:T(8,128)(2,1)S(1)} async-done(((bf16[8,2,32,512]{3,2,1,0:T(8,128)(2,1)}), bf16[8,2,32,512]{3,2,1,0:T(8,128)(2,1)S(1)}, u32[]{:S(2)}, u32[]{:S(2)}) %all-to-all-start.1) | async-done | bytes 524320 | tf_op jit(solution)/shard_map/all_to_all | solution.py:268
  107.3 4.0 %collective-permute-start.16 = (bf16[176,512]{1,0:T(8,128)(2,1)S(1)}, bf16[176,512]{1,0:T(8,128)(2,1)S(1)}, u32[]{:S(2)}, u32[]{:S(2)}) collective-permute-start(bf16[176,512]{1,0:T(8,128)(2,1)S(1)} %get-tuple-element.61), channel_id=1, source_target_pairs={{0,64},{1,193},{2,66},{3,195},{4,68},{5,197},{6,70},{7,199},{8,72}... | collective-permute-start | bytes 540680 | tf_op jit(solution)/shard_map/ppermute | solution.py:34
  112.0 2.1 %collective-permute-start.20 = (bf16[160,1024]{1,0:T(8,128)(2,1)S(1)}, bf16[160,1024]{1,0:T(8,128)(2,1)S(1)}, u32[]{:S(2)}, u32[]{:S(2)}) collective-permute-start(bf16[160,1024]{1,0:T(8,128)(2,1)S(1)} %pad_maximum_fusion.2), channel_id=1, source_target_pairs={{0,64},{1,193},{2,66},{3,195},{4,68},{5,197},{6,70},{7,199},{8,72}... | collective-permute-start | bytes 983048 | tf_op jit(solution)/shard_map/ppermute | solution.py:34
  114.5 2.5 %collective-permute-done.13 = bf16[176,512]{1,0:T(8,128)(2,1)S(1)} collective-permute-done((bf16[176,512]{1,0:T(8,128)(2,1)S(1)}, bf16[176,512]{1,0:T(8,128)(2,1)S(1)}, u32[]{:S(2)}, u32[]{:S(2)}) %collective-permute-start.13) | collective-permute-done | bytes 180256 | tf_op jit(solution)/shard_map/ppermute | solution.py:34
  117.3 4.5 %collective-permute-done.17 = bf16[176,1024]{1,0:T(8,128)(2,1)S(1)} collective-permute-done((bf16[176,1024]{1,0:T(8,128)(2,1)S(1)}, bf16[176,1024]{1,0:T(8,128)(2,1)S(1)}, u32[]{:S(2)}, u32[]{:S(2)}) %collective-permute-start.17) | collective-permute-done | bytes 360480 | tf_op jit(solution)/shard_map/ppermute | solution.py:34
  121.9 2.7 %collective-permute-start.18 = (bf16[176,2048]{1,0:T(8,128)(2,1)S(1)}, bf16[176,2048]{1,0:T(8,128)(2,1)S(1)}, u32[]{:S(2)}, u32[]{:S(2)}) collective-permute-start(bf16[176,2048]{1,0:T(8,128)(2,1)S(1)} %constant_dynamic-update-slice_fusion.3.refs_1_), channel_id=1, source_target_pairs={{0,16},{1,49},{2,18},{3,51},{4,20},{5,53},{6,22},{7,55},{8,24},{9,... | collective-permute-start | bytes 2162696 | tf_op jit(solution)/shard_map/ppermute | solution.py:34
  124.9 2.7 %collective-permute-start.21 = (bf16[160,2048]{1,0:T(8,128)(2,1)S(1)}, bf16[160,2048]{1,0:T(8,128)(2,1)S(1)}, u32[]{:S(2)}, u32[]{:S(2)}) collective-permute-start(bf16[160,2048]{1,0:T(8,128)(2,1)S(1)} %constant_dynamic-update-slice_fusion.6.refs_2_), channel_id=1, source_target_pairs={{0,2},{1,15},{2,0},{3,5},{4,6},{5,3},{6,4},{7,9},{8,10},{9,7},{10,... | collective-permute-start | bytes 1966088 | tf_op jit(solution)/shard_map/ppermute | solution.py:34
  127.6 3.5 %forward_own.1 = (f32[512,176]{1,0:T(8,128)S(1)}, f32[512,176]{1,0:T(8,128)S(1)}, f32[512,160]{1,0:T(8,128)S(1)}, bf16[4,8,256,128]{3,2,1,0:T(8,128)(2,1)S(1)}) custom-call(bf16[4,8,256,128]{3,2,1,0:T(8,128)(2,1)S(1)} %get-tuple-element.58.mine_ref.tokens_ref, bf16[4,8,256,128]{3,2,1,0:T(8,128)(2,1)} %collective-permute-done.22.theirs_ref, ...), custom_call_target="tpu_custom_call" | custom-call | flops 1073741824 | bytes 9437184 | tf_op jit(solution)/shard_map/forward_own/pallas_call | solution.py:126
  131.1 4.5 %collective-permute-done.21.refs_2_ = bf16[160,2048]{1,0:T(8,128)(2,1)S(1)} collective-permute-done((bf16[160,2048]{1,0:T(8,128)(2,1)S(1)}, bf16[160,2048]{1,0:T(8,128)(2,1)S(1)}, u32[]{:S(2)}, u32[]{:S(2)}) %collective-permute-start.21) | collective-permute-done | bytes 655392 | tf_op jit(solution)/shard_map/ppermute | solution.py:34
  137.2 1.5 %collective-permute-start.23 = (bf16[256,512]{1,0:T(8,128)(2,1)S(1)}, bf16[256,512]{1,0:T(8,128)(2,1)S(1)}, u32[]{:S(2)}, u32[]{:S(2)}) collective-permute-start(bf16[256,512]{1,0:T(8,128)(2,1)S(1)} %forward_theirs.1), channel_id=1, source_target_pairs={{0,1},{1,0},{2,3},{3,2},{4,5},{5,4},{6,7},{7,6},{8,9},{9,8},{10,11... | collective-permute-start | bytes 786440 | tf_op jit(solution)/shard_map/ppermute | solution.py:34
  138.7 1.1 forward_mine.1
  (70 shorter events, 12.4 us)
Async XLA Ops:
  0.8 8.0 %copy-start.5 = (bf16[256,512]{1,0:T(8,128)(2,1)S(1)}, bf16[256,512]{1,0:T(8,128)(2,1)}, u32[]{:S(2)}) copy-start(bf16[256,512]{1,0:T(8,128)(2,1)} %my_cot_ref.1) | copy-start | bytes 786436
  5.5 7.5 %collective-permute-start = (bf16[4,8,256,128]{3,2,1,0:T(8,128)(2,1)S(1)}, bf16[4,8,256,128]{3,2,1,0:T(8,128)(2,1)S(1)}, u32[]{:S(2)}, u32[]{:S(2)}) collective-permute-start(bf16[4,8,256,128]{3,2,1,0:T(8,128)(2,1)S(1)} %get-tuple-element.37), channel_id=1, source_target_pairs={{0,1},{1,0},{2,3},{3,2},{4,5},{5,4},{6,7},{7,6},{8,9},{9,8},{10,11... | collective-permute-start | bytes 6291464 | tf_op jit(solution)/shard_map/ppermute | solution.py:34
  8.8 4.2 %collective-permute-start.1 = (bf16[256,512]{1,0:T(8,128)(2,1)S(1)}, bf16[256,512]{1,0:T(8,128)(2,1)S(1)}, u32[]{:S(2)}, u32[]{:S(2)}) collective-permute-start(bf16[256,512]{1,0:T(8,128)(2,1)S(1)} %copy-done.5), channel_id=1, source_target_pairs={{0,1},{1,0},{2,3},{3,2},{4,5},{5,4},{6,7},{7,6},{8,9},{9,8},{10,11... | collective-permute-start | bytes 786440 | tf_op jit(solution)/shard_map/ppermute | solution.py:34
  13.0 11.5 %copy-start.3 = (bf16[256,8192]{1,0:T(8,128)(2,1)S(1)}, bf16[256,8192]{1,0:T(8,128)(2,1)}, u32[]{:S(2)}) copy-start(bf16[256,8192]{1,0:T(8,128)(2,1)} %in_ref.3) | copy-start | bytes 12582916
  15.4 13.2 %collective-permute-start.5 = (bf16[176,2048]{1,0:T(8,128)(2,1)S(1)}, bf16[176,2048]{1,0:T(8,128)(2,1)S(1)}, u32[]{:S(2)}, u32[]{:S(2)}) collective-permute-start(bf16[176,2048]{1,0:T(8,128)(2,1)S(1)} %get-tuple-element.50), channel_id=1, source_target_pairs={{0,16},{1,49},{2,18},{3,51},{4,20},{5,53},{6,22},{7,55},{8,24},{9,... | collective-permute-start | bytes 2162696 | tf_op jit(solution)/shard_map/ppermute | solution.py:34
  16.5 17.6 %collective-permute-start.8 = (bf16[160,2048]{1,0:T(8,128)(2,1)S(1)}, bf16[160,2048]{1,0:T(8,128)(2,1)S(1)}, u32[]{:S(2)}, u32[]{:S(2)}) collective-permute-start(bf16[160,2048]{1,0:T(8,128)(2,1)S(1)} %get-tuple-element.52), channel_id=1, source_target_pairs={{0,2},{1,15},{2,0},{3,5},{4,6},{5,3},{6,4},{7,9},{8,10},{9,7},{10,... | collective-permute-start | bytes 1966088 | tf_op jit(solution)/shard_map/ppermute | solution.py:34
  22.0 11.3 %collective-permute-start.2 = (bf16[176,2048]{1,0:T(8,128)(2,1)S(1)}, bf16[176,2048]{1,0:T(8,128)(2,1)S(1)}, u32[]{:S(2)}, u32[]{:S(2)}) collective-permute-start(bf16[176,2048]{1,0:T(8,128)(2,1)S(1)} %get-tuple-element.45), channel_id=1, source_target_pairs={{0,64},{1,193},{2,66},{3,195},{4,68},{5,197},{6,70},{7,199},{8,72}... | collective-permute-start | bytes 2162696 | tf_op jit(solution)/shard_map/ppermute | solution.py:34
  28.6 1.4 copy-start.4
  30.0 7.6 %collective-permute-start.6 = (bf16[176,1024]{1,0:T(8,128)(2,1)S(1)}, bf16[176,1024]{1,0:T(8,128)(2,1)S(1)}, u32[]{:S(2)}, u32[]{:S(2)}) collective-permute-start(bf16[176,1024]{1,0:T(8,128)(2,1)S(1)} %slice.75), channel_id=1, source_target_pairs={{0,2},{1,15},{2,0},{3,5},{4,6},{5,3},{6,4},{7,9},{8,10},{9,7},{10,... | collective-permute-start | bytes 1081352 | tf_op jit(solution)/shard_map/ppermute | solution.py:34
  33.6 7.6 %collective-permute-start.3 = (bf16[176,1024]{1,0:T(8,128)(2,1)S(1)}, bf16[176,1024]{1,0:T(8,128)(2,1)S(1)}, u32[]{:S(2)}, u32[]{:S(2)}) collective-permute-start(bf16[176,1024]{1,0:T(8,128)(2,1)S(1)} %slice.76), channel_id=1, source_target_pairs={{0,16},{1,49},{2,18},{3,51},{4,20},{5,53},{6,22},{7,55},{8,24},{9,... | collective-permute-start | bytes 1081352 | tf_op jit(solution)/shard_map/ppermute | solution.py:34
  34.3 7.4 %collective-permute-start.9 = (bf16[160,1024]{1,0:T(8,128)(2,1)S(1)}, bf16[160,1024]{1,0:T(8,128)(2,1)S(1)}, u32[]{:S(2)}, u32[]{:S(2)}) collective-permute-start(bf16[160,1024]{1,0:T(8,128)(2,1)S(1)} %slice.77), channel_id=1, source_target_pairs={{0,64},{1,193},{2,66},{3,195},{4,68},{5,197},{6,70},{7,199},{8,72}... | collective-permute-start | bytes 983048 | tf_op jit(solution)/shard_map/ppermute | solution.py:34
  37.7 9.6 %collective-permute-start.7 = (bf16[176,512]{1,0:T(8,128)(2,1)S(1)}, bf16[176,512]{1,0:T(8,128)(2,1)S(1)}, u32[]{:S(2)}, u32[]{:S(2)}) collective-permute-start(bf16[176,512]{1,0:T(8,128)(2,1)S(1)} %slice.78), channel_id=1, source_target_pairs={{0,64},{1,193},{2,66},{3,195},{4,68},{5,197},{6,70},{7,199},{8,72}... | collective-permute-start | bytes 540680 | tf_op jit(solution)/shard_map/ppermute | solution.py:34
  41.3 5.9 %collective-permute-start.4 = (bf16[176,512]{1,0:T(8,128)(2,1)S(1)}, bf16[176,512]{1,0:T(8,128)(2,1)S(1)}, u32[]{:S(2)}, u32[]{:S(2)}) collective-permute-start(bf16[176,512]{1,0:T(8,128)(2,1)S(1)} %slice.79), channel_id=1, source_target_pairs={{0,2},{1,15},{2,0},{3,5},{4,6},{5,3},{6,4},{7,9},{8,10},{9,7},{10,... | collective-permute-start | bytes 540680 | tf_op jit(solution)/shard_map/ppermute | solution.py:34
  41.8 5.5 %collective-permute-start.10 = (bf16[160,512]{1,0:T(8,128)(2,1)S(1)}, bf16[160,512]{1,0:T(8,128)(2,1)S(1)}, u32[]{:S(2)}, u32[]{:S(2)}) collective-permute-start(bf16[160,512]{1,0:T(8,128)(2,1)S(1)} %slice.80), channel_id=1, source_target_pairs={{0,16},{1,49},{2,18},{3,51},{4,20},{5,53},{6,22},{7,55},{8,24},{9,... | collective-permute-start | bytes 491528 | tf_op jit(solution)/shard_map/ppermute | solution.py:34
  44.6 31.4 %copy-start = (f32[32,512]{1,0:T(8,128)S(1)}, f32[32,512]{1,0:T(8,128)}, u32[]{:S(2)}) copy-start(f32[32,512]{1,0:T(8,128)} %master_ref.1) | copy-start | bytes 196612
  44.6 31.4 %copy-start.1 = (f32[32,512]{1,0:T(8,128)S(1)}, f32[32,512]{1,0:T(8,128)}, u32[]{:S(2)}) copy-start(f32[32,512]{1,0:T(8,128)} %one_ref.1) | copy-start | bytes 196612
  44.6 31.4 %copy-start.2 = (f32[32,512]{1,0:T(8,128)S(1)}, f32[32,512]{1,0:T(8,128)}, u32[]{:S(2)}) copy-start(f32[32,512]{1,0:T(8,128)} %two_ref.1) | copy-start | bytes 196612
  69.2 6.9 %collective-permute-start.11 = (bf16[32,512]{1,0:T(8,128)(2,1)S(1)}, bf16[32,512]{1,0:T(8,128)(2,1)S(1)}, u32[]{:S(2)}, u32[]{:S(2)}) collective-permute-start(bf16[32,512]{1,0:T(8,128)(2,1)S(1)} %get-tuple-element.54), channel_id=1, source_target_pairs={{0,8},{1,9},{2,10},{3,11},{4,12},{5,13},{6,14},{7,15},{8,0},{9,1},... | collective-permute-start | bytes 98312 | tf_op jit(solution)/shard_map/ppermute | solution.py:34
  76.8 6.7 %collective-permute-start.12 = (bf16[32,512]{1,0:T(8,128)(2,1)S(1)}, bf16[32,512]{1,0:T(8,128)(2,1)S(1)}, u32[]{:S(2)}, u32[]{:S(2)}) collective-permute-start(bf16[32,512]{1,0:T(8,128)(2,1)S(1)} %get-tuple-element.59.own_ref), channel_id=1, source_target_pairs={{0,8},{1,9},{2,10},{3,11},{4,12},{5,13},{6,14},{7,15},{8,0},{9,1},... | collective-permute-start | bytes 98312 | tf_op jit(solution)/shard_map/ppermute | solution.py:34
  84.8 21.5 %all-to-all-start.1 = ((bf16[8,2,32,512]{3,2,1,0:T(8,128)(2,1)}), bf16[8,2,32,512]{3,2,1,0:T(8,128)(2,1)S(1)}, u32[]{:S(2)}, u32[]{:S(2)}) async-start(bf16[8,2,32,512]{3,2,1,0:T(8,128)(2,1)} %copies.1), calls=%async_computation.1 | async-start | bytes 1048576 | tf_op jit(solution)/shard_map/all_to_all | solution.py:268
  88.3 39.3 %collective-permute-start.22 = (bf16[4,8,256,128]{3,2,1,0:T(8,128)(2,1)}, bf16[4,8,256,128]{3,2,1,0:T(8,128)(2,1)}, u32[]{:S(2)}, u32[]{:S(2)}) collective-permute-start(bf16[4,8,256,128]{3,2,1,0:T(8,128)(2,1)} %copy-done.4), channel_id=1, source_target_pairs={{0,1},{1,0},{2,3},{3,2},{4,5},{5,4},{6,7},{7,6},{8,9},{9,8},{10,11... | collective-permute-start | bytes 6291464 | tf_op jit(solution)/shard_map/ppermute | solution.py:34
  106.5 5.5 %collective-permute-start.19 = (bf16[160,512]{1,0:T(8,128)(2,1)S(1)}, bf16[160,512]{1,0:T(8,128)(2,1)S(1)}, u32[]{:S(2)}, u32[]{:S(2)}) collective-permute-start(bf16[160,512]{1,0:T(8,128)(2,1)S(1)} %get-tuple-element.62), channel_id=1, source_target_pairs={{0,16},{1,49},{2,18},{3,51},{4,20},{5,53},{6,22},{7,55},{8,24},{9,... | collective-permute-start | bytes 491528 | tf_op jit(solution)/shard_map/ppermute | solution.py:34
  107.3 6.9 %collective-permute-start.16 = (bf16[176,512]{1,0:T(8,128)(2,1)S(1)}, bf16[176,512]{1,0:T(8,128)(2,1)S(1)}, u32[]{:S(2)}, u32[]{:S(2)}) collective-permute-start(bf16[176,512]{1,0:T(8,128)(2,1)S(1)} %get-tuple-element.61), channel_id=1, source_target_pairs={{0,64},{1,193},{2,66},{3,195},{4,68},{5,197},{6,70},{7,199},{8,72}... | collective-permute-start | bytes 540680 | tf_op jit(solution)/shard_map/ppermute | solution.py:34
  111.4 5.6 %collective-permute-start.13 = (bf16[176,512]{1,0:T(8,128)(2,1)S(1)}, bf16[176,512]{1,0:T(8,128)(2,1)S(1)}, u32[]{:S(2)}, u32[]{:S(2)}) collective-permute-start(bf16[176,512]{1,0:T(8,128)(2,1)S(1)} %get-tuple-element.60), channel_id=1, source_target_pairs={{0,2},{1,15},{2,0},{3,5},{4,6},{5,3},{6,4},{7,9},{8,10},{9,7},{10,... | collective-permute-start | bytes 540680 | tf_op jit(solution)/shard_map/ppermute | solution.py:34
  112.0 12.8 %collective-permute-start.20 = (bf16[160,1024]{1,0:T(8,128)(2,1)S(1)}, bf16[160,1024]{1,0:T(8,128)(2,1)S(1)}, u32[]{:S(2)}, u32[]{:S(2)}) collective-permute-start(bf16[160,1024]{1,0:T(8,128)(2,1)S(1)} %pad_maximum_fusion.2), channel_id=1, source_target_pairs={{0,64},{1,193},{2,66},{3,195},{4,68},{5,197},{6,70},{7,199},{8,72}... | collective-permute-start | bytes 983048 | tf_op jit(solution)/shard_map/ppermute | solution.py:34
  114.3 7.6 %collective-permute-start.17 = (bf16[176,1024]{1,0:T(8,128)(2,1)S(1)}, bf16[176,1024]{1,0:T(8,128)(2,1)S(1)}, u32[]{:S(2)}, u32[]{:S(2)}) collective-permute-start(bf16[176,1024]{1,0:T(8,128)(2,1)S(1)} %pad_maximum_fusion.1), channel_id=1, source_target_pairs={{0,2},{1,15},{2,0},{3,5},{4,6},{5,3},{6,4},{7,9},{8,10},{9,7},{10,... | collective-permute-start | bytes 1081352 | tf_op jit(solution)/shard_map/ppermute | solution.py:34
  117.1 7.6 %collective-permute-start.14 = (bf16[176,1024]{1,0:T(8,128)(2,1)S(1)}, bf16[176,1024]{1,0:T(8,128)(2,1)S(1)}, u32[]{:S(2)}, u32[]{:S(2)}) collective-permute-start(bf16[176,1024]{1,0:T(8,128)(2,1)S(1)} %pad_maximum_fusion), channel_id=1, source_target_pairs={{0,16},{1,49},{2,18},{3,51},{4,20},{5,53},{6,22},{7,55},{8,24},{9,... | collective-permute-start | bytes 1081352 | tf_op jit(solution)/shard_map/ppermute | solution.py:34
  121.9 13.8 %collective-permute-start.18 = (bf16[176,2048]{1,0:T(8,128)(2,1)S(1)}, bf16[176,2048]{1,0:T(8,128)(2,1)S(1)}, u32[]{:S(2)}, u32[]{:S(2)}) collective-permute-start(bf16[176,2048]{1,0:T(8,128)(2,1)S(1)} %constant_dynamic-update-slice_fusion.3.refs_1_), channel_id=1, source_target_pairs={{0,16},{1,49},{2,18},{3,51},{4,20},{5,53},{6,22},{7,55},{8,24},{9,... | collective-permute-start | bytes 2162696 | tf_op jit(solution)/shard_map/ppermute | solution.py:34
  124.7 11.4 %collective-permute-start.15 = (bf16[176,2048]{1,0:T(8,128)(2,1)S(1)}, bf16[176,2048]{1,0:T(8,128)(2,1)S(1)}, u32[]{:S(2)}, u32[]{:S(2)}) collective-permute-start(bf16[176,2048]{1,0:T(8,128)(2,1)S(1)} %constant_dynamic-update-slice_fusion.refs_0_), channel_id=1, source_target_pairs={{0,64},{1,193},{2,66},{3,195},{4,68},{5,197},{6,70},{7,199},{8,72}... | collective-permute-start | bytes 2162696 | tf_op jit(solution)/shard_map/ppermute | solution.py:34
  124.9 10.7 %collective-permute-start.21 = (bf16[160,2048]{1,0:T(8,128)(2,1)S(1)}, bf16[160,2048]{1,0:T(8,128)(2,1)S(1)}, u32[]{:S(2)}, u32[]{:S(2)}) collective-permute-start(bf16[160,2048]{1,0:T(8,128)(2,1)S(1)} %constant_dynamic-update-slice_fusion.6.refs_2_), channel_id=1, source_target_pairs={{0,2},{1,15},{2,0},{3,5},{4,6},{5,3},{6,4},{7,9},{8,10},{9,7},{10,... | collective-permute-start | bytes 1966088 | tf_op jit(solution)/shard_map/ppermute | solution.py:34
  137.2 2.7 %collective-permute-start.23 = (bf16[256,512]{1,0:T(8,128)(2,1)S(1)}, bf16[256,512]{1,0:T(8,128)(2,1)S(1)}, u32[]{:S(2)}, u32[]{:S(2)}) collective-permute-start(bf16[256,512]{1,0:T(8,128)(2,1)S(1)} %forward_theirs.1), channel_id=1, source_target_pairs={{0,1},{1,0},{2,3},{3,2},{4,5},{5,4},{6,7},{7,6},{8,9},{9,8},{10,11... | collective-permute-start | bytes 786440 | tf_op jit(solution)/shard_map/ppermute | solution.py:34

commit v5 on v2

--- a/solution.py
+++ b/solution.py
@@ -161,6 +161,7 @@
 def forward_own_kernel(mine_ref, theirs_ref, *refs):
     for p in range(3):
         refs[3 + p][...] = half_product(p, 0, (mine_ref, theirs_ref), refs[p])
+    refs[6][...] = theirs_ref[...]
 
 
 def forward_kernel(first, tokens_ref, *refs):
@@ -215,11 +216,15 @@
         cotangent,
         their_cot,
     )
+    later, *halves = lax.optimization_barrier((at, *halves))
+    next_mine, next_sent = sort_columns(later, next_tokens, VMEM_LIMIT)
     last = []
     for p in range(3):
         kept, sent = halves[2 * p : 2 * p + 2]
         for i, axis in enumerate(ORDER[p]):
             came = permute(sent.astype(jnp.bfloat16), lambda d: neighbour(d, axis))
+            if p == 0 and i == 0:
+                came, next_sent = lax.optimization_barrier((came, next_sent))
             if i < 2:
                 kept, sent = halved(kept.astype(jnp.float32) + came.astype(jnp.float32))
         last += [kept, came]
@@ -237,7 +242,6 @@
         moment_two,
     )
 
-    next_mine, next_sent = sort_columns(at, next_tokens, VMEM_LIMIT)
     next_theirs = other_core(next_sent)
     copies = lax.all_to_all(copies, AXES, 0, 0, tiled=True, axis_index_groups=groups())
     held = vmem_call(
@@ -256,8 +260,14 @@
                 own = jnp.concatenate([own, came], axis=1)
         owns.append(own)
         cames.append(came)
-    before = vmem_call(
-        forward_own_kernel, [f32(2 * t, p) for p in parts], "forward_own", flops // 2, next_mine, next_theirs, *owns
+    *before, next_theirs = vmem_call(
+        forward_own_kernel,
+        [f32(2 * t, p) for p in parts] + [bf16(*next_theirs.shape)],
+        "forward_own",
+        flops // 2,
+        next_mine,
+        next_theirs,
+        *owns,
     )
     (their_out,) = vmem_call(
         functools.partial(forward_kernel, t), [bf16(t, f)], "forward_theirs", flops // 4, next_theirs, *cames, *before

time: 134 us -> 133 us (level)
  waiting for transfers between devices: 30.3 us -> 39.3 us
  starting transfers between devices: 51.4 us -> 44.7 us
  Pallas kernels: 21 us -> 18.2 us
    all_to_all x1, waiting for transfers between devices: 8.55 us -> 16.5 us  [on_device(): lax.all_to_all(copies, AXES, 0, 0, tiled=True, axis_index_groups=groups())]
    ppermute x22, starting transfers between devices: 47.2 us -> 40.2 us  [permute(): return lax.ppermute(value, AXES, [(d, target(d)) for d in range(DEVICES)])]
    pallas_call x7, Pallas kernels: 11 us -> 9.51 us  [vmem_call(): pl.pallas_call(kernel, in_specs=[space] * len(operands), out_specs=[space...]
    pallas_call x2, Pallas kernels: 10 us -> 8.67 us  [sort_columns(): pl.pallas_call(sort_kernel, in_specs=[pl.BlockSpec(memory_space=pltpu.SME...]
  transfers between devices with their start and end apart: 23 -> 23, of which waited for: 12 -> 9; matrix products, arithmetic and copies ran while one was open for 1% -> 1% of each run, Pallas kernels for 8% -> 7%
where the time goes in v5:
time: 133 us
  starting transfers between devices  44.7 us (34%)
  waiting for transfers between devices  39.3 us (30%)
  blocking collectives  26 us (20%)
  Pallas kernels  18.2 us (14%)
  other arithmetic  1.77 us (1%)
  local copies, waits for them, and re-layouts  1.58 us (1%)
    ppermute x22, starting transfers between devices, permute(): return lax.ppermute(value, AXES, [(d, target(d)) for d in range(DEVICES)])  40.2 us
    all_to_all x1, blocking collectives, on_device(): lax.all_to_all(partial, AXES, 0, 0, tiled=True, axis_index_groups=groups())  26 us
    ppermute x22, waiting for transfers between devices, permute(): return lax.ppermute(value, AXES, [(d, target(d)) for d in range(DEVICES)])  22.8 us
    all_to_all x1, waiting for transfers between devices, on_device(): lax.all_to_all(copies, AXES, 0, 0, tiled=True, axis_index_groups=groups())  16.5 us
    pallas_call x7, Pallas kernels, vmem_call(): pl.pallas_call(kernel, in_specs=[space] * len(operands), out_specs=[space...  9.51 us
    pallas_call x2, Pallas kernels, sort_columns(): pl.pallas_call(sort_kernel, in_specs=[pl.BlockSpec(memory_space=pltpu.SME...  8.67 us
    all_to_all x1, starting transfers between devices, on_device(): lax.all_to_all(copies, AXES, 0, 0, tiled=True, axis_index_groups=groups())  4.46 us
  transfers between devices with their start and end apart: 23, of which 9 were waited for; matrix products, arithmetic and copies ran while one was open for 1% of the time, Pallas kernels for 7%

profile of v5, /device:TPU:1, one launch (start us, length us, event | category | flops | bytes accessed | tf_op | source)
XLA Modules:
  0.0 132.6 jit_solution(4736638987135462541)
XLA Ops:
  0.8 4.6 %sort_columns.2 = (bf16[4,8,256,128]{3,2,1,0:T(8,128)(2,1)S(1)}, bf16[4,8,256,128]{3,2,1,0:T(8,128)(2,1)S(1)}) custom-call(s32[4]{0:T(128)S(1)} %pad_add_fusion.at_ref, bf16[256,8192]{1,0:T(8,128)(2,1)} %in_ref.2), custom_call_target="tpu_custom_call" | custom-call | flops 2147483648 | bytes 8388608 | tf_op jit(solution)/shard_map/sort_columns/pallas_call | solution.py:84
  5.5 3.3 %collective-permute-start = (bf16[4,8,256,128]{3,2,1,0:T(8,128)(2,1)S(1)}, bf16[4,8,256,128]{3,2,1,0:T(8,128)(2,1)S(1)}, u32[]{:S(2)}, u32[]{:S(2)}) collective-permute-start(bf16[4,8,256,128]{3,2,1,0:T(8,128)(2,1)S(1)} %get-tuple-element.35), channel_id=1, source_target_pairs={{0,1},{1,0},{2,3},{3,2},{4,5},{5,4},{6,7},{7,6},{8,9},{9,8},{10,11... | collective-permute-start | bytes 6291464 | tf_op jit(solution)/shard_map/ppermute | solution.py:34
  8.9 4.1 %collective-permute-done.1.their_cot_ref = bf16[256,512]{1,0:T(8,128)(2,1)S(1)} collective-permute-done((bf16[256,512]{1,0:T(8,128)(2,1)S(1)}, bf16[256,512]{1,0:T(8,128)(2,1)S(1)}, u32[]{:S(2)}, u32[]{:S(2)}) %collective-permute-start.1) | collective-permute-done | bytes 262176 | tf_op jit(solution)/shard_map/ppermute | solution.py:34
  13.0 2.4 %gradient.1 = (bf16[176,2048]{1,0:T(8,128)(2,1)S(1)}, bf16[176,2048]{1,0:T(8,128)(2,1)S(1)}, bf16[176,2048]{1,0:T(8,128)(2,1)S(1)}, bf16[176,2048]{1,0:T(8,128)(...) custom-call(bf16[4,8,256,128]{3,2,1,0:T(8,128)(2,1)S(1)} %get-tuple-element.34.mine_ref, ...), custom_call_target="tpu_custom_call" | custom-call | flops 2147483648 | bytes 8912896 | tf_op jit(solution)/shard_map/gradient/pallas_call | solution.py:121
  15.4 1.1 collective-permute-start.5
  16.4 5.6 %collective-permute-start.8 = (bf16[160,2048]{1,0:T(8,128)(2,1)S(1)}, bf16[160,2048]{1,0:T(8,128)(2,1)S(1)}, u32[]{:S(2)}, u32[]{:S(2)}) collective-permute-start(bf16[160,2048]{1,0:T(8,128)(2,1)S(1)} %get-tuple-element.50), channel_id=1, source_target_pairs={{0,2},{1,15},{2,0},{3,5},{4,6},{5,3},{6,4},{7,9},{8,10},{9,7},{10,... | collective-permute-start | bytes 1966088 | tf_op jit(solution)/shard_map/ppermute | solution.py:34
  22.0 2.5 %collective-permute-start.2 = (bf16[176,2048]{1,0:T(8,128)(2,1)S(1)}, bf16[176,2048]{1,0:T(8,128)(2,1)S(1)}, u32[]{:S(2)}, u32[]{:S(2)}) collective-permute-start(bf16[176,2048]{1,0:T(8,128)(2,1)S(1)} %get-tuple-element.43), channel_id=1, source_target_pairs={{0,64},{1,193},{2,66},{3,195},{4,68},{5,197},{6,70},{7,199},{8,72}... | collective-permute-start | bytes 2162696 | tf_op jit(solution)/shard_map/ppermute | solution.py:34
  24.5 4.0 %sort_columns.3 = (bf16[4,8,256,128]{3,2,1,0:T(8,128)(2,1)S(1)}, bf16[4,8,256,128]{3,2,1,0:T(8,128)(2,1)S(1)}) custom-call(s32[4]{0:T(128)S(1)} %pad_add_fusion.at_ref, bf16[256,8192]{1,0:T(8,128)(2,1)S(1)} %copy-done.3), custom_call_target="tpu_custom_call" | custom-call | flops 2147483648 | bytes 8388608 | tf_op jit(solution)/shard_map/sort_columns/pallas_call | solution.py:84
  28.8 1.1 copy-done.4
  29.9 1.1 collective-permute-start.6
  31.0 2.3 %collective-permute-done.2 = bf16[176,2048]{1,0:T(8,128)(2,1)S(1)} collective-permute-done((bf16[176,2048]{1,0:T(8,128)(2,1)S(1)}, bf16[176,2048]{1,0:T(8,128)(2,1)S(1)}, u32[]{:S(2)}, u32[]{:S(2)}) %collective-permute-start.2) | collective-permute-done | bytes 720928 | tf_op jit(solution)/shard_map/ppermute | solution.py:34
  34.3 2.6 %collective-permute-start.9 = (bf16[160,1024]{1,0:T(8,128)(2,1)S(1)}, bf16[160,1024]{1,0:T(8,128)(2,1)S(1)}, u32[]{:S(2)}, u32[]{:S(2)}) collective-permute-start(bf16[160,1024]{1,0:T(8,128)(2,1)S(1)} %slice.77), channel_id=1, source_target_pairs={{0,64},{1,193},{2,66},{3,195},{4,68},{5,197},{6,70},{7,199},{8,72}... | collective-permute-start | bytes 983048 | tf_op jit(solution)/shard_map/ppermute | solution.py:34
  37.6 1.1 collective-permute-start.7
  38.7 2.4 %collective-permute-done.3 = bf16[176,1024]{1,0:T(8,128)(2,1)S(1)} collective-permute-done((bf16[176,1024]{1,0:T(8,128)(2,1)S(1)}, bf16[176,1024]{1,0:T(8,128)(2,1)S(1)}, u32[]{:S(2)}, u32[]{:S(2)}) %collective-permute-start.3) | collective-permute-done | bytes 360480 | tf_op jit(solution)/shard_map/ppermute | solution.py:34
  41.8 2.8 %collective-permute-start.10 = (bf16[160,512]{1,0:T(8,128)(2,1)S(1)}, bf16[160,512]{1,0:T(8,128)(2,1)S(1)}, u32[]{:S(2)}, u32[]{:S(2)}) collective-permute-start(bf16[160,512]{1,0:T(8,128)(2,1)S(1)} %slice.80), channel_id=1, source_target_pairs={{0,16},{1,49},{2,18},{3,51},{4,20},{5,53},{6,22},{7,55},{8,24},{9,... | collective-permute-start | bytes 491528 | tf_op jit(solution)/shard_map/ppermute | solution.py:34
  44.7 2.6 %collective-permute-done.10.refs_5_ = bf16[160,512]{1,0:T(8,128)(2,1)S(1)} collective-permute-done((bf16[160,512]{1,0:T(8,128)(2,1)S(1)}, bf16[160,512]{1,0:T(8,128)(2,1)S(1)}, u32[]{:S(2)}, u32[]{:S(2)}) %collective-permute-start.10) | collective-permute-done | bytes 163872 | tf_op jit(solution)/shard_map/ppermute | solution.py:34
  47.5 26.0 %all_to_all.10.partial_ref = bf16[16,32,512]{2,1,0:T(8,128)(2,1)S(1)} all-to-all(bf16[16,32,512]{2,1,0:T(8,128)(2,1)S(1)} %bitcast.7), channel_id=1, replica_groups={{0,4,8,12,32,36,40,44,128,132,136,140,160,164,168,172},{1,5,9,13,33,37,..., dimensions={0} | all-to-all | bytes 1048576 | tf_op jit(solution)/shard_map/all_to_all | solution.py:233
  74.5 4.5 %all-to-all-start.1 = ((bf16[16,32,512]{2,1,0:T(8,128)(2,1)}), bf16[16,32,512]{2,1,0:T(8,128)(2,1)S(1)}, u32[]{:S(2)}, u32[]{:S(2)}) async-start(bf16[16,32,512]{2,1,0:T(8,128)(2,1)} %get-tuple-element.55), calls=%async_computation.1 | async-start | bytes 1048576 | tf_op jit(solution)/shard_map/all_to_all | solution.py:246
  79.0 1.5 %collective-permute-start.20 = (bf16[4,8,256,128]{3,2,1,0:T(8,128)(2,1)}, bf16[4,8,256,128]{3,2,1,0:T(8,128)(2,1)}, u32[]{:S(2)}, u32[]{:S(2)}) collective-permute-start(bf16[4,8,256,128]{3,2,1,0:T(8,128)(2,1)} %copy-done.4), channel_id=1, source_target_pairs={{0,1},{1,0},{2,3},{3,2},{4,5},{5,4},{6,7},{7,6},{8,9},{9,8},{10,11... | collective-permute-start | bytes 6291464 | tf_op jit(solution)/shard_map/ppermute | solution.py:34
  80.5 16.5 %all-to-all-done.1 = bf16[16,32,512]{2,1,0:T(8,128)(2,1)S(1)} async-done(((bf16[16,32,512]{2,1,0:T(8,128)(2,1)}), bf16[16,32,512]{2,1,0:T(8,128)(2,1)S(1)}, u32[]{:S(2)}, u32[]{:S(2)}) %all-to-all-start.1) | async-done | bytes 524320 | tf_op jit(solution)/shard_map/all_to_all | solution.py:246
  97.3 2.1 %collective-permute-start.14 = (bf16[176,512]{1,0:T(8,128)(2,1)S(1)}, bf16[176,512]{1,0:T(8,128)(2,1)S(1)}, u32[]{:S(2)}, u32[]{:S(2)}) collective-permute-start(bf16[176,512]{1,0:T(8,128)(2,1)S(1)} %get-tuple-element.57), channel_id=1, source_target_pairs={{0,64},{1,193},{2,66},{3,195},{4,68},{5,197},{6,70},{7,199},{8,72}... | collective-permute-start | bytes 540680 | tf_op jit(solution)/shard_map/ppermute | solution.py:34
  99.5 3.7 %collective-permute-start.11 = (bf16[176,512]{1,0:T(8,128)(2,1)S(1)}, bf16[176,512]{1,0:T(8,128)(2,1)S(1)}, u32[]{:S(2)}, u32[]{:S(2)}) collective-permute-start(bf16[176,512]{1,0:T(8,128)(2,1)S(1)} %get-tuple-element.56), channel_id=1, source_target_pairs={{0,2},{1,15},{2,0},{3,5},{4,6},{5,3},{6,4},{7,9},{8,10},{9,7},{10,... | collective-permute-start | bytes 540680 | tf_op jit(solution)/shard_map/ppermute | solution.py:34
  103.2 1.6 %collective-permute-start.18 = (bf16[160,1024]{1,0:T(8,128)(2,1)S(1)}, bf16[160,1024]{1,0:T(8,128)(2,1)S(1)}, u32[]{:S(2)}, u32[]{:S(2)}) collective-permute-start(bf16[160,1024]{1,0:T(8,128)(2,1)S(1)} %pad_maximum_fusion.2), channel_id=1, source_target_pairs={{0,64},{1,193},{2,66},{3,195},{4,68},{5,197},{6,70},{7,199},{8,72}... | collective-permute-start | bytes 983048 | tf_op jit(solution)/shard_map/ppermute | solution.py:34
  104.9 1.2 collective-permute-start.15
  106.1 2.7 %collective-permute-start.12 = (bf16[176,1024]{1,0:T(8,128)(2,1)S(1)}, bf16[176,1024]{1,0:T(8,128)(2,1)S(1)}, u32[]{:S(2)}, u32[]{:S(2)}) collective-permute-start(bf16[176,1024]{1,0:T(8,128)(2,1)S(1)} %pad_maximum_fusion), channel_id=1, source_target_pairs={{0,16},{1,49},{2,18},{3,51},{4,20},{5,53},{6,22},{7,55},{8,24},{9,... | collective-permute-start | bytes 1081352 | tf_op jit(solution)/shard_map/ppermute | solution.py:34
  108.9 3.6 %collective-permute-done.15 = bf16[176,1024]{1,0:T(8,128)(2,1)S(1)} collective-permute-done((bf16[176,1024]{1,0:T(8,128)(2,1)S(1)}, bf16[176,1024]{1,0:T(8,128)(2,1)S(1)}, u32[]{:S(2)}, u32[]{:S(2)}) %collective-permute-start.15) | collective-permute-done | bytes 360480 | tf_op jit(solution)/shard_map/ppermute | solution.py:34
  112.5 1.1 collective-permute-start.16
  113.7 2.8 %collective-permute-start.13 = (bf16[176,2048]{1,0:T(8,128)(2,1)S(1)}, bf16[176,2048]{1,0:T(8,128)(2,1)S(1)}, u32[]{:S(2)}, u32[]{:S(2)}) collective-permute-start(bf16[176,2048]{1,0:T(8,128)(2,1)S(1)} %constant_dynamic-update-slice_fusion.refs_0_), channel_id=1, source_target_pairs={{0,64},{1,193},{2,66},{3,195},{4,68},{5,197},{6,70},{7,199},{8,72}... | collective-permute-start | bytes 2162696 | tf_op jit(solution)/shard_map/ppermute | solution.py:34
  116.7 3.5 %forward_own.1 = (f32[512,176]{1,0:T(8,128)S(1)}, f32[512,176]{1,0:T(8,128)S(1)}, f32[512,160]{1,0:T(8,128)S(1)}, bf16[4,8,256,128]{3,2,1,0:T(8,128)(2,1)S(1)}) custom-call(bf16[4,8,256,128]{3,2,1,0:T(8,128)(2,1)S(1)} %get-tuple-element.54.mine_ref.tokens_ref, bf16[4,8,256,128]{3,2,1,0:T(8,128)(2,1)} %collective-permute-done.20.theirs_ref, ...), custom_call_target="tpu_custom_call" | custom-call | flops 1073741824 | bytes 9437184 | tf_op jit(solution)/shard_map/forward_own/pallas_call | solution.py:121
  120.2 7.0 %collective-permute-done.19.refs_2_ = bf16[160,2048]{1,0:T(8,128)(2,1)S(1)} collective-permute-done((bf16[160,2048]{1,0:T(8,128)(2,1)S(1)}, bf16[160,2048]{1,0:T(8,128)(2,1)S(1)}, u32[]{:S(2)}, u32[]{:S(2)}) %collective-permute-start.19) | collective-permute-done | bytes 655392 | tf_op jit(solution)/shard_map/ppermute | solution.py:34
  128.3 2.4 %collective-permute-start.21 = (bf16[256,512]{1,0:T(8,128)(2,1)S(1)}, bf16[256,512]{1,0:T(8,128)(2,1)S(1)}, u32[]{:S(2)}, u32[]{:S(2)}) collective-permute-start(bf16[256,512]{1,0:T(8,128)(2,1)S(1)} %forward_theirs.1), channel_id=1, source_target_pairs={{0,1},{1,0},{2,3},{3,2},{4,5},{5,4},{6,7},{7,6},{8,9},{9,8},{10,11... | collective-permute-start | bytes 786440 | tf_op jit(solution)/shard_map/ppermute | solution.py:34
  130.7 1.1 forward_mine.1
  (64 shorter events, 6.6 us)
Async XLA Ops:
  0.8 8.0 %copy-start.5 = (bf16[256,512]{1,0:T(8,128)(2,1)S(1)}, bf16[256,512]{1,0:T(8,128)(2,1)}, u32[]{:S(2)}) copy-start(bf16[256,512]{1,0:T(8,128)(2,1)} %my_cot_ref.1) | copy-start | bytes 786436
  5.5 7.5 %collective-permute-start = (bf16[4,8,256,128]{3,2,1,0:T(8,128)(2,1)S(1)}, bf16[4,8,256,128]{3,2,1,0:T(8,128)(2,1)S(1)}, u32[]{:S(2)}, u32[]{:S(2)}) collective-permute-start(bf16[4,8,256,128]{3,2,1,0:T(8,128)(2,1)S(1)} %get-tuple-element.35), channel_id=1, source_target_pairs={{0,1},{1,0},{2,3},{3,2},{4,5},{5,4},{6,7},{7,6},{8,9},{9,8},{10,11... | collective-permute-start | bytes 6291464 | tf_op jit(solution)/shard_map/ppermute | solution.py:34
  8.8 4.2 %collective-permute-start.1 = (bf16[256,512]{1,0:T(8,128)(2,1)S(1)}, bf16[256,512]{1,0:T(8,128)(2,1)S(1)}, u32[]{:S(2)}, u32[]{:S(2)}) collective-permute-start(bf16[256,512]{1,0:T(8,128)(2,1)S(1)} %copy-done.5), channel_id=1, source_target_pairs={{0,1},{1,0},{2,3},{3,2},{4,5},{5,4},{6,7},{7,6},{8,9},{9,8},{10,11... | collective-permute-start | bytes 786440 | tf_op jit(solution)/shard_map/ppermute | solution.py:34
  13.0 11.5 %copy-start.3 = (bf16[256,8192]{1,0:T(8,128)(2,1)S(1)}, bf16[256,8192]{1,0:T(8,128)(2,1)}, u32[]{:S(2)}) copy-start(bf16[256,8192]{1,0:T(8,128)(2,1)} %in_ref.3) | copy-start | bytes 12582916
  15.4 13.2 %collective-permute-start.5 = (bf16[176,2048]{1,0:T(8,128)(2,1)S(1)}, bf16[176,2048]{1,0:T(8,128)(2,1)S(1)}, u32[]{:S(2)}, u32[]{:S(2)}) collective-permute-start(bf16[176,2048]{1,0:T(8,128)(2,1)S(1)} %get-tuple-element.48), channel_id=1, source_target_pairs={{0,16},{1,49},{2,18},{3,51},{4,20},{5,53},{6,22},{7,55},{8,24},{9,... | collective-permute-start | bytes 2162696 | tf_op jit(solution)/shard_map/ppermute | solution.py:34
  16.4 17.6 %collective-permute-start.8 = (bf16[160,2048]{1,0:T(8,128)(2,1)S(1)}, bf16[160,2048]{1,0:T(8,128)(2,1)S(1)}, u32[]{:S(2)}, u32[]{:S(2)}) collective-permute-start(bf16[160,2048]{1,0:T(8,128)(2,1)S(1)} %get-tuple-element.50), channel_id=1, source_target_pairs={{0,2},{1,15},{2,0},{3,5},{4,6},{5,3},{6,4},{7,9},{8,10},{9,7},{10,... | collective-permute-start | bytes 1966088 | tf_op jit(solution)/shard_map/ppermute | solution.py:34
  22.0 11.3 %collective-permute-start.2 = (bf16[176,2048]{1,0:T(8,128)(2,1)S(1)}, bf16[176,2048]{1,0:T(8,128)(2,1)S(1)}, u32[]{:S(2)}, u32[]{:S(2)}) collective-permute-start(bf16[176,2048]{1,0:T(8,128)(2,1)S(1)} %get-tuple-element.43), channel_id=1, source_target_pairs={{0,64},{1,193},{2,66},{3,195},{4,68},{5,197},{6,70},{7,199},{8,72}... | collective-permute-start | bytes 2162696 | tf_op jit(solution)/shard_map/ppermute | solution.py:34
  28.5 1.3 %copy-start.4 = (bf16[4,8,256,128]{3,2,1,0:T(8,128)(2,1)}, bf16[4,8,256,128]{3,2,1,0:T(8,128)(2,1)S(1)}, u32[]{:S(2)}) copy-start(bf16[4,8,256,128]{3,2,1,0:T(8,128)(2,1)S(1)} %get-tuple-element.59) | copy-start | bytes 6291460
  29.9 7.6 %collective-permute-start.6 = (bf16[176,1024]{1,0:T(8,128)(2,1)S(1)}, bf16[176,1024]{1,0:T(8,128)(2,1)S(1)}, u32[]{:S(2)}, u32[]{:S(2)}) collective-permute-start(bf16[176,1024]{1,0:T(8,128)(2,1)S(1)} %slice.75), channel_id=1, source_target_pairs={{0,2},{1,15},{2,0},{3,5},{4,6},{5,3},{6,4},{7,9},{8,10},{9,7},{10,... | collective-permute-start | bytes 1081352 | tf_op jit(solution)/shard_map/ppermute | solution.py:34
  33.6 7.6 %collective-permute-start.3 = (bf16[176,1024]{1,0:T(8,128)(2,1)S(1)}, bf16[176,1024]{1,0:T(8,128)(2,1)S(1)}, u32[]{:S(2)}, u32[]{:S(2)}) collective-permute-start(bf16[176,1024]{1,0:T(8,128)(2,1)S(1)} %slice.76), channel_id=1, source_target_pairs={{0,16},{1,49},{2,18},{3,51},{4,20},{5,53},{6,22},{7,55},{8,24},{9,... | collective-permute-start | bytes 1081352 | tf_op jit(solution)/shard_map/ppermute | solution.py:34
  34.3 7.4 %collective-permute-start.9 = (bf16[160,1024]{1,0:T(8,128)(2,1)S(1)}, bf16[160,1024]{1,0:T(8,128)(2,1)S(1)}, u32[]{:S(2)}, u32[]{:S(2)}) collective-permute-start(bf16[160,1024]{1,0:T(8,128)(2,1)S(1)} %slice.77), channel_id=1, source_target_pairs={{0,64},{1,193},{2,66},{3,195},{4,68},{5,197},{6,70},{7,199},{8,72}... | collective-permute-start | bytes 983048 | tf_op jit(solution)/shard_map/ppermute | solution.py:34
  37.6 9.6 %collective-permute-start.7 = (bf16[176,512]{1,0:T(8,128)(2,1)S(1)}, bf16[176,512]{1,0:T(8,128)(2,1)S(1)}, u32[]{:S(2)}, u32[]{:S(2)}) collective-permute-start(bf16[176,512]{1,0:T(8,128)(2,1)S(1)} %slice.78), channel_id=1, source_target_pairs={{0,64},{1,193},{2,66},{3,195},{4,68},{5,197},{6,70},{7,199},{8,72}... | collective-permute-start | bytes 540680 | tf_op jit(solution)/shard_map/ppermute | solution.py:34
  41.3 5.9 %collective-permute-start.4 = (bf16[176,512]{1,0:T(8,128)(2,1)S(1)}, bf16[176,512]{1,0:T(8,128)(2,1)S(1)}, u32[]{:S(2)}, u32[]{:S(2)}) collective-permute-start(bf16[176,512]{1,0:T(8,128)(2,1)S(1)} %slice.79), channel_id=1, source_target_pairs={{0,2},{1,15},{2,0},{3,5},{4,6},{5,3},{6,4},{7,9},{8,10},{9,7},{10,... | collective-permute-start | bytes 540680 | tf_op jit(solution)/shard_map/ppermute | solution.py:34
  41.8 5.5 %collective-permute-start.10 = (bf16[160,512]{1,0:T(8,128)(2,1)S(1)}, bf16[160,512]{1,0:T(8,128)(2,1)S(1)}, u32[]{:S(2)}, u32[]{:S(2)}) collective-permute-start(bf16[160,512]{1,0:T(8,128)(2,1)S(1)} %slice.80), channel_id=1, source_target_pairs={{0,16},{1,49},{2,18},{3,51},{4,20},{5,53},{6,22},{7,55},{8,24},{9,... | collective-permute-start | bytes 491528 | tf_op jit(solution)/shard_map/ppermute | solution.py:34
  44.6 28.8 %copy-start = (f32[32,512]{1,0:T(8,128)S(1)}, f32[32,512]{1,0:T(8,128)}, u32[]{:S(2)}) copy-start(f32[32,512]{1,0:T(8,128)} %master_ref.1) | copy-start | bytes 196612
  44.6 28.8 %copy-start.1 = (f32[32,512]{1,0:T(8,128)S(1)}, f32[32,512]{1,0:T(8,128)}, u32[]{:S(2)}) copy-start(f32[32,512]{1,0:T(8,128)} %one_ref.1) | copy-start | bytes 196612
  44.7 28.8 %copy-start.2 = (f32[32,512]{1,0:T(8,128)S(1)}, f32[32,512]{1,0:T(8,128)}, u32[]{:S(2)}) copy-start(f32[32,512]{1,0:T(8,128)} %two_ref.1) | copy-start | bytes 196612
  74.5 22.5 %all-to-all-start.1 = ((bf16[16,32,512]{2,1,0:T(8,128)(2,1)}), bf16[16,32,512]{2,1,0:T(8,128)(2,1)S(1)}, u32[]{:S(2)}, u32[]{:S(2)}) async-start(bf16[16,32,512]{2,1,0:T(8,128)(2,1)} %get-tuple-element.55), calls=%async_computation.1 | async-start | bytes 1048576 | tf_op jit(solution)/shard_map/all_to_all | solution.py:246
  79.0 37.7 %collective-permute-start.20 = (bf16[4,8,256,128]{3,2,1,0:T(8,128)(2,1)}, bf16[4,8,256,128]{3,2,1,0:T(8,128)(2,1)}, u32[]{:S(2)}, u32[]{:S(2)}) collective-permute-start(bf16[4,8,256,128]{3,2,1,0:T(8,128)(2,1)} %copy-done.4), channel_id=1, source_target_pairs={{0,1},{1,0},{2,3},{3,2},{4,5},{5,4},{6,7},{7,6},{8,9},{9,8},{10,11... | collective-permute-start | bytes 6291464 | tf_op jit(solution)/shard_map/ppermute | solution.py:34
  97.2 6.0 %collective-permute-start.17 = (bf16[160,512]{1,0:T(8,128)(2,1)S(1)}, bf16[160,512]{1,0:T(8,128)(2,1)S(1)}, u32[]{:S(2)}, u32[]{:S(2)}) collective-permute-start(bf16[160,512]{1,0:T(8,128)(2,1)S(1)} %get-tuple-element.58), channel_id=1, source_target_pairs={{0,16},{1,49},{2,18},{3,51},{4,20},{5,53},{6,22},{7,55},{8,24},{9,... | collective-permute-start | bytes 491528 | tf_op jit(solution)/shard_map/ppermute | solution.py:34
  97.3 7.5 %collective-permute-start.14 = (bf16[176,512]{1,0:T(8,128)(2,1)S(1)}, bf16[176,512]{1,0:T(8,128)(2,1)S(1)}, u32[]{:S(2)}, u32[]{:S(2)}) collective-permute-start(bf16[176,512]{1,0:T(8,128)(2,1)S(1)} %get-tuple-element.57), channel_id=1, source_target_pairs={{0,64},{1,193},{2,66},{3,195},{4,68},{5,197},{6,70},{7,199},{8,72}... | collective-permute-start | bytes 540680 | tf_op jit(solution)/shard_map/ppermute | solution.py:34
  99.5 6.6 %collective-permute-start.11 = (bf16[176,512]{1,0:T(8,128)(2,1)S(1)}, bf16[176,512]{1,0:T(8,128)(2,1)S(1)}, u32[]{:S(2)}, u32[]{:S(2)}) collective-permute-start(bf16[176,512]{1,0:T(8,128)(2,1)S(1)} %get-tuple-element.56), channel_id=1, source_target_pairs={{0,2},{1,15},{2,0},{3,5},{4,6},{5,3},{6,4},{7,9},{8,10},{9,7},{10,... | collective-permute-start | bytes 540680 | tf_op jit(solution)/shard_map/ppermute | solution.py:34
  103.2 13.2 %collective-permute-start.18 = (bf16[160,1024]{1,0:T(8,128)(2,1)S(1)}, bf16[160,1024]{1,0:T(8,128)(2,1)S(1)}, u32[]{:S(2)}, u32[]{:S(2)}) collective-permute-start(bf16[160,1024]{1,0:T(8,128)(2,1)S(1)} %pad_maximum_fusion.2), channel_id=1, source_target_pairs={{0,64},{1,193},{2,66},{3,195},{4,68},{5,197},{6,70},{7,199},{8,72}... | collective-permute-start | bytes 983048 | tf_op jit(solution)/shard_map/ppermute | solution.py:34
  104.9 7.6 %collective-permute-start.15 = (bf16[176,1024]{1,0:T(8,128)(2,1)S(1)}, bf16[176,1024]{1,0:T(8,128)(2,1)S(1)}, u32[]{:S(2)}, u32[]{:S(2)}) collective-permute-start(bf16[176,1024]{1,0:T(8,128)(2,1)S(1)} %pad_maximum_fusion.1), channel_id=1, source_target_pairs={{0,2},{1,15},{2,0},{3,5},{4,6},{5,3},{6,4},{7,9},{8,10},{9,7},{10,... | collective-permute-start | bytes 1081352 | tf_op jit(solution)/shard_map/ppermute | solution.py:34
  106.1 7.6 %collective-permute-start.12 = (bf16[176,1024]{1,0:T(8,128)(2,1)S(1)}, bf16[176,1024]{1,0:T(8,128)(2,1)S(1)}, u32[]{:S(2)}, u32[]{:S(2)}) collective-permute-start(bf16[176,1024]{1,0:T(8,128)(2,1)S(1)} %pad_maximum_fusion), channel_id=1, source_target_pairs={{0,16},{1,49},{2,18},{3,51},{4,20},{5,53},{6,22},{7,55},{8,24},{9,... | collective-permute-start | bytes 1081352 | tf_op jit(solution)/shard_map/ppermute | solution.py:34
  112.5 14.7 %collective-permute-start.16 = (bf16[176,2048]{1,0:T(8,128)(2,1)S(1)}, bf16[176,2048]{1,0:T(8,128)(2,1)S(1)}, u32[]{:S(2)}, u32[]{:S(2)}) collective-permute-start(bf16[176,2048]{1,0:T(8,128)(2,1)S(1)} %constant_dynamic-update-slice_fusion.3.refs_1_), channel_id=1, source_target_pairs={{0,16},{1,49},{2,18},{3,51},{4,20},{5,53},{6,22},{7,55},{8,24},{9,... | collective-permute-start | bytes 2162696 | tf_op jit(solution)/shard_map/ppermute | solution.py:34
  113.7 13.5 %collective-permute-start.13 = (bf16[176,2048]{1,0:T(8,128)(2,1)S(1)}, bf16[176,2048]{1,0:T(8,128)(2,1)S(1)}, u32[]{:S(2)}, u32[]{:S(2)}) collective-permute-start(bf16[176,2048]{1,0:T(8,128)(2,1)S(1)} %constant_dynamic-update-slice_fusion.refs_0_), channel_id=1, source_target_pairs={{0,64},{1,193},{2,66},{3,195},{4,68},{5,197},{6,70},{7,199},{8,72}... | collective-permute-start | bytes 2162696 | tf_op jit(solution)/shard_map/ppermute | solution.py:34
  116.5 10.7 %collective-permute-start.19 = (bf16[160,2048]{1,0:T(8,128)(2,1)S(1)}, bf16[160,2048]{1,0:T(8,128)(2,1)S(1)}, u32[]{:S(2)}, u32[]{:S(2)}) collective-permute-start(bf16[160,2048]{1,0:T(8,128)(2,1)S(1)} %constant_dynamic-update-slice_fusion.6.refs_2_), channel_id=1, source_target_pairs={{0,2},{1,15},{2,0},{3,5},{4,6},{5,3},{6,4},{7,9},{8,10},{9,7},{10,... | collective-permute-start | bytes 1966088 | tf_op jit(solution)/shard_map/ppermute | solution.py:34
  128.3 3.6 %collective-permute-start.21 = (bf16[256,512]{1,0:T(8,128)(2,1)S(1)}, bf16[256,512]{1,0:T(8,128)(2,1)S(1)}, u32[]{:S(2)}, u32[]{:S(2)}) collective-permute-start(bf16[256,512]{1,0:T(8,128)(2,1)S(1)} %forward_theirs.1), channel_id=1, source_target_pairs={{0,1},{1,0},{2,3},{3,2},{4,5},{5,4},{6,7},{7,6},{8,9},{9,8},{10,11... | collective-permute-start | bytes 786440 | tf_op jit(solution)/shard_map/ppermute | solution.py:34

commit v6 on v5

--- a/solution.py
+++ b/solution.py
@@ -34,11 +34,19 @@
     return lax.ppermute(value, AXES, [(d, target(d)) for d in range(DEVICES)])
 
 
+def side(v, c):
+    return (v // 2) ^ (v % 2 * (1 - c))
+
+
+def rest(v, c):
+    return v // 2 * (1 - c) + v % 2 * c
+
+
 def groups():
     seen = {}
     for d in range(DEVICES):
         x, y, z, c = coordinates(d)
-        seen.setdefault((x % 2, y % 2, z % 2, c), []).append(d)
+        seen.setdefault((side(x, c), side(y, c), z % 2, c), []).append(d)
     return list(seen.values())
 
 
@@ -56,9 +64,12 @@
 def sort_kernel(at_ref, in_ref, my_ref, other_ref, chunks, sems):
     c, x0, y0, z0 = (at_ref[i] for i in range(4))
     wide = chunks.shape[2]
-    copies = []
+    copies, theirs = [], []
     for i in range(4):
-        start = pl.multiple_of((2 * (i % 2) + (x0 ^ (i // 2))) * wide, wide)
+        near, far = x0 ^ (i // 2), i % 2
+        x = jnp.where(c == 0, 2 * far + (near ^ far), 2 * near + far)
+        theirs.append((at_ref[4] ^ side(x, 1 - c)) * 2 + rest(x, 1 - c))
+        start = pl.multiple_of(x * wide, wide)
         copies.append(pltpu.make_async_copy(in_ref.at[:, pl.ds(start, wide)], chunks.at[i], sems.at[i]))
         copies[-1].start()
     n = 4 * LANES
@@ -72,10 +83,11 @@
         for y in range(4):
             turned = jnp.dot(chunks[i, :, y * n : (y + 1) * n], move, preferred_element_type=jnp.float32)
             turned = turned.astype(my_ref.dtype)
-            where = (y0 ^ (y % 2)) * 4 + (y // 2) * 2
+            where = (y0 ^ side(y, c)) * 4 + rest(y, c) * 2
+            there = (at_ref[5] ^ side(y, 1 - c)) * 4 + rest(y, 1 - c) * 2
             for rz in range(2):
                 my_ref[i, where + rz] = turned[:, rz * LANES : (rz + 1) * LANES]
-                other_ref[i, where + rz] = turned[:, (2 + rz) * LANES : (3 + rz) * LANES]
+                other_ref[theirs[i], there + rz] = turned[:, (2 + rz) * LANES : (3 + rz) * LANES]
 
 
 def sort_columns(at, tokens, limit):
@@ -197,7 +209,7 @@
     parts = part_rows(f)
     me = lax.axis_index("grp") * 32 + lax.axis_index("intra")
     x, y, z, c = coordinates(me)
-    at = jnp.stack([c, x % 2, y % 2, z % 2]).astype(jnp.int32)
+    at = jnp.stack([c, side(x, c), side(y, c), z % 2, side(x, 1 - c), side(y, 1 - c)]).astype(jnp.int32)
     bf16 = lambda *shape: jax.ShapeDtypeStruct(shape, jnp.bfloat16)
     f32 = lambda *shape: jax.ShapeDtypeStruct(shape, jnp.float32)
     other_core = lambda v: permute(v, lambda d: d ^ 1)

time: 133 us -> 126 us (0.947)
  blocking collectives: 26 us -> 21.8 us
  waiting for transfers between devices: 39.3 us -> 35.4 us
  starting transfers between devices: 44.7 us -> 46.1 us
    all_to_all x1, waiting for transfers between devices: 16.5 us -> 10.9 us  [on_device(): lax.all_to_all(copies, AXES, 0, 0, tiled=True, axis_index_groups=groups())]
    all_to_all x1, blocking collectives: 26 us -> 21.8 us  [on_device(): lax.all_to_all(partial, AXES, 0, 0, tiled=True, axis_index_groups=groups())]
    ppermute x22, starting transfers between devices: 40.2 us -> 42 us  [permute(): return lax.ppermute(value, AXES, [(d, target(d)) for d in range(DEVICES)])]
    ppermute x22, waiting for transfers between devices: 22.8 us -> 24.5 us  [permute(): return lax.ppermute(value, AXES, [(d, target(d)) for d in range(DEVICES)])]
  transfers between devices with their start and end apart: 23 -> 23, of which waited for: 9 -> 11; matrix products, arithmetic and copies ran while one was open for 1% -> 1% of each run, Pallas kernels for 7% -> 7%
where the time goes in v6:
time: 126 us
  starting transfers between devices  46.1 us (37%)
  waiting for transfers between devices  35.4 us (28%)
  blocking collectives  21.8 us (17%)
  Pallas kernels  18.2 us (14%)
  local copies, waits for them, and re-layouts  1.68 us (1%)
  other arithmetic  1.66 us (1%)
    ppermute x22, starting transfers between devices, permute(): return lax.ppermute(value, AXES, [(d, target(d)) for d in range(DEVICES)])  42 us
    ppermute x22, waiting for transfers between devices, permute(): return lax.ppermute(value, AXES, [(d, target(d)) for d in range(DEVICES)])  24.5 us
    all_to_all x1, blocking collectives, on_device(): lax.all_to_all(partial, AXES, 0, 0, tiled=True, axis_index_groups=groups())  21.8 us
    all_to_all x1, waiting for transfers between devices, on_device(): lax.all_to_all(copies, AXES, 0, 0, tiled=True, axis_index_groups=groups())  10.9 us
    pallas_call x7, Pallas kernels, vmem_call(): pl.pallas_call(kernel, in_specs=[space] * len(operands), out_specs=[space...  9.49 us
    pallas_call x2, Pallas kernels, sort_columns(): pl.pallas_call(sort_kernel, in_specs=[pl.BlockSpec(memory_space=pltpu.SME...  8.69 us
    all_to_all x1, starting transfers between devices, on_device(): lax.all_to_all(copies, AXES, 0, 0, tiled=True, axis_index_groups=groups())  4.06 us
  transfers between devices with their start and end apart: 23, of which 11 were waited for; matrix products, arithmetic and copies ran while one was open for 1% of the time, Pallas kernels for 7%

profile of v6, /device:TPU:1, one launch (start us, length us, event | category | flops | bytes accessed | tf_op | source)
XLA Modules:
  0.0 126.0 jit_solution(13402805048416468027)
XLA Ops:
  0.9 4.6 %sort_columns.2 = (bf16[4,8,256,128]{3,2,1,0:T(8,128)(2,1)S(1)}, bf16[4,8,256,128]{3,2,1,0:T(8,128)(2,1)S(1)}) custom-call(s32[6]{0:T(128)S(1)} %stack.27.at_ref, bf16[256,8192]{1,0:T(8,128)(2,1)} %in_ref.2), custom_call_target="tpu_custom_call" | custom-call | flops 2147483648 | bytes 8388608 | tf_op jit(solution)/shard_map/sort_columns/pallas_call | solution.py:96
  5.5 3.3 %collective-permute-start = (bf16[4,8,256,128]{3,2,1,0:T(8,128)(2,1)S(1)}, bf16[4,8,256,128]{3,2,1,0:T(8,128)(2,1)S(1)}, u32[]{:S(2)}, u32[]{:S(2)}) collective-permute-start(bf16[4,8,256,128]{3,2,1,0:T(8,128)(2,1)S(1)} %get-tuple-element.35), channel_id=1, source_target_pairs={{0,1},{1,0},{2,3},{3,2},{4,5},{5,4},{6,7},{7,6},{8,9},{9,8},{10,11... | collective-permute-start | bytes 6291464 | tf_op jit(solution)/shard_map/ppermute | solution.py:34
  9.0 4.1 %collective-permute-done.1.their_cot_ref = bf16[256,512]{1,0:T(8,128)(2,1)S(1)} collective-permute-done((bf16[256,512]{1,0:T(8,128)(2,1)S(1)}, bf16[256,512]{1,0:T(8,128)(2,1)S(1)}, u32[]{:S(2)}, u32[]{:S(2)}) %collective-permute-start.1) | collective-permute-done | bytes 262176 | tf_op jit(solution)/shard_map/ppermute | solution.py:34
  13.0 2.4 %gradient.1 = (bf16[176,2048]{1,0:T(8,128)(2,1)S(1)}, bf16[176,2048]{1,0:T(8,128)(2,1)S(1)}, bf16[176,2048]{1,0:T(8,128)(2,1)S(1)}, bf16[176,2048]{1,0:T(8,128)(...) custom-call(bf16[4,8,256,128]{3,2,1,0:T(8,128)(2,1)S(1)} %get-tuple-element.34.mine_ref, ...), custom_call_target="tpu_custom_call" | custom-call | flops 2147483648 | bytes 8912896 | tf_op jit(solution)/shard_map/gradient/pallas_call | solution.py:133
  15.4 1.1 collective-permute-start.5
  16.5 5.6 %collective-permute-start.8 = (bf16[160,2048]{1,0:T(8,128)(2,1)S(1)}, bf16[160,2048]{1,0:T(8,128)(2,1)S(1)}, u32[]{:S(2)}, u32[]{:S(2)}) collective-permute-start(bf16[160,2048]{1,0:T(8,128)(2,1)S(1)} %get-tuple-element.50), channel_id=1, source_target_pairs={{0,2},{1,15},{2,0},{3,5},{4,6},{5,3},{6,4},{7,9},{8,10},{9,7},{10,... | collective-permute-start | bytes 1966088 | tf_op jit(solution)/shard_map/ppermute | solution.py:34
  22.1 2.5 %collective-permute-start.2 = (bf16[176,2048]{1,0:T(8,128)(2,1)S(1)}, bf16[176,2048]{1,0:T(8,128)(2,1)S(1)}, u32[]{:S(2)}, u32[]{:S(2)}) collective-permute-start(bf16[176,2048]{1,0:T(8,128)(2,1)S(1)} %get-tuple-element.43), channel_id=1, source_target_pairs={{0,64},{1,193},{2,66},{3,195},{4,68},{5,197},{6,70},{7,199},{8,72}... | collective-permute-start | bytes 2162696 | tf_op jit(solution)/shard_map/ppermute | solution.py:34
  24.5 4.0 %sort_columns.3 = (bf16[4,8,256,128]{3,2,1,0:T(8,128)(2,1)S(1)}, bf16[4,8,256,128]{3,2,1,0:T(8,128)(2,1)S(1)}) custom-call(s32[6]{0:T(128)S(1)} %stack.27.at_ref, bf16[256,8192]{1,0:T(8,128)(2,1)S(1)} %copy-done.3), custom_call_target="tpu_custom_call" | custom-call | flops 2147483648 | bytes 8388608 | tf_op jit(solution)/shard_map/sort_columns/pallas_call | solution.py:96
  28.8 1.1 copy-done.4
  30.0 1.1 collective-permute-start.6
  31.1 2.3 %collective-permute-done.2 = bf16[176,2048]{1,0:T(8,128)(2,1)S(1)} collective-permute-done((bf16[176,2048]{1,0:T(8,128)(2,1)S(1)}, bf16[176,2048]{1,0:T(8,128)(2,1)S(1)}, u32[]{:S(2)}, u32[]{:S(2)}) %collective-permute-start.2) | collective-permute-done | bytes 720928 | tf_op jit(solution)/shard_map/ppermute | solution.py:34
  34.3 2.6 %collective-permute-start.9 = (bf16[160,1024]{1,0:T(8,128)(2,1)S(1)}, bf16[160,1024]{1,0:T(8,128)(2,1)S(1)}, u32[]{:S(2)}, u32[]{:S(2)}) collective-permute-start(bf16[160,1024]{1,0:T(8,128)(2,1)S(1)} %slice.77), channel_id=1, source_target_pairs={{0,64},{1,193},{2,66},{3,195},{4,68},{5,197},{6,70},{7,199},{8,72}... | collective-permute-start | bytes 983048 | tf_op jit(solution)/shard_map/ppermute | solution.py:34
  37.7 1.1 collective-permute-start.7
  38.8 2.5 %collective-permute-done.3 = bf16[176,1024]{1,0:T(8,128)(2,1)S(1)} collective-permute-done((bf16[176,1024]{1,0:T(8,128)(2,1)S(1)}, bf16[176,1024]{1,0:T(8,128)(2,1)S(1)}, u32[]{:S(2)}, u32[]{:S(2)}) %collective-permute-start.3) | collective-permute-done | bytes 360480 | tf_op jit(solution)/shard_map/ppermute | solution.py:34
  41.8 2.8 %collective-permute-start.10 = (bf16[160,512]{1,0:T(8,128)(2,1)S(1)}, bf16[160,512]{1,0:T(8,128)(2,1)S(1)}, u32[]{:S(2)}, u32[]{:S(2)}) collective-permute-start(bf16[160,512]{1,0:T(8,128)(2,1)S(1)} %slice.80), channel_id=1, source_target_pairs={{0,16},{1,49},{2,18},{3,51},{4,20},{5,53},{6,22},{7,55},{8,24},{9,... | collective-permute-start | bytes 491528 | tf_op jit(solution)/shard_map/ppermute | solution.py:34
  44.7 2.6 %collective-permute-done.10.refs_5_ = bf16[160,512]{1,0:T(8,128)(2,1)S(1)} collective-permute-done((bf16[160,512]{1,0:T(8,128)(2,1)S(1)}, bf16[160,512]{1,0:T(8,128)(2,1)S(1)}, u32[]{:S(2)}, u32[]{:S(2)}) %collective-permute-start.10) | collective-permute-done | bytes 163872 | tf_op jit(solution)/shard_map/ppermute | solution.py:34
  47.5 21.8 %all_to_all.10.partial_ref = bf16[16,32,512]{2,1,0:T(8,128)(2,1)S(1)} all-to-all(bf16[16,32,512]{2,1,0:T(8,128)(2,1)S(1)} %bitcast.9), channel_id=1, replica_groups={{0,4,8,12,48,52,56,60,192,196,200,204,240,244,248,252},{1,5,9,13,17,21,..., dimensions={0} | all-to-all | bytes 1048576 | tf_op jit(solution)/shard_map/all_to_all | solution.py:245
  69.3 1.0 update.1
  70.3 4.1 %all-to-all-start.1 = ((bf16[16,32,512]{2,1,0:T(8,128)(2,1)}), bf16[16,32,512]{2,1,0:T(8,128)(2,1)S(1)}, u32[]{:S(2)}, u32[]{:S(2)}) async-start(bf16[16,32,512]{2,1,0:T(8,128)(2,1)} %get-tuple-element.55), calls=%async_computation.1 | async-start | bytes 1048576 | tf_op jit(solution)/shard_map/all_to_all | solution.py:258
  74.4 4.2 %collective-permute-start.20 = (bf16[4,8,256,128]{3,2,1,0:T(8,128)(2,1)}, bf16[4,8,256,128]{3,2,1,0:T(8,128)(2,1)}, u32[]{:S(2)}, u32[]{:S(2)}) collective-permute-start(bf16[4,8,256,128]{3,2,1,0:T(8,128)(2,1)} %copy-done.4), channel_id=1, source_target_pairs={{0,1},{1,0},{2,3},{3,2},{4,5},{5,4},{6,7},{7,6},{8,9},{9,8},{10,11... | collective-permute-start | bytes 6291464 | tf_op jit(solution)/shard_map/ppermute | solution.py:34
  78.6 10.9 %all-to-all-done.1 = bf16[16,32,512]{2,1,0:T(8,128)(2,1)S(1)} async-done(((bf16[16,32,512]{2,1,0:T(8,128)(2,1)}), bf16[16,32,512]{2,1,0:T(8,128)(2,1)S(1)}, u32[]{:S(2)}, u32[]{:S(2)}) %all-to-all-start.1) | async-done | bytes 524320 | tf_op jit(solution)/shard_map/all_to_all | solution.py:258
  89.9 5.0 %collective-permute-start.14 = (bf16[176,512]{1,0:T(8,128)(2,1)S(1)}, bf16[176,512]{1,0:T(8,128)(2,1)S(1)}, u32[]{:S(2)}, u32[]{:S(2)}) collective-permute-start(bf16[176,512]{1,0:T(8,128)(2,1)S(1)} %get-tuple-element.57), channel_id=1, source_target_pairs={{0,64},{1,193},{2,66},{3,195},{4,68},{5,197},{6,70},{7,199},{8,72}... | collective-permute-start | bytes 540680 | tf_op jit(solution)/shard_map/ppermute | solution.py:34
  95.6 4.7 %collective-permute-start.18 = (bf16[160,1024]{1,0:T(8,128)(2,1)S(1)}, bf16[160,1024]{1,0:T(8,128)(2,1)S(1)}, u32[]{:S(2)}, u32[]{:S(2)}) collective-permute-start(bf16[160,1024]{1,0:T(8,128)(2,1)S(1)} %pad_maximum_fusion.2), channel_id=1, source_target_pairs={{0,64},{1,193},{2,66},{3,195},{4,68},{5,197},{6,70},{7,199},{8,72}... | collective-permute-start | bytes 983048 | tf_op jit(solution)/shard_map/ppermute | solution.py:34
  100.6 2.7 %collective-permute-start.12 = (bf16[176,1024]{1,0:T(8,128)(2,1)S(1)}, bf16[176,1024]{1,0:T(8,128)(2,1)S(1)}, u32[]{:S(2)}, u32[]{:S(2)}) collective-permute-start(bf16[176,1024]{1,0:T(8,128)(2,1)S(1)} %pad_maximum_fusion), channel_id=1, source_target_pairs={{0,16},{1,49},{2,18},{3,51},{4,20},{5,53},{6,22},{7,55},{8,24},{9,... | collective-permute-start | bytes 1081352 | tf_op jit(solution)/shard_map/ppermute | solution.py:34
  103.3 4.6 %collective-permute-done.15 = bf16[176,1024]{1,0:T(8,128)(2,1)S(1)} collective-permute-done((bf16[176,1024]{1,0:T(8,128)(2,1)S(1)}, bf16[176,1024]{1,0:T(8,128)(2,1)S(1)}, u32[]{:S(2)}, u32[]{:S(2)}) %collective-permute-start.15) | collective-permute-done | bytes 360480 | tf_op jit(solution)/shard_map/ppermute | solution.py:34
  108.2 2.7 %collective-permute-start.13 = (bf16[176,2048]{1,0:T(8,128)(2,1)S(1)}, bf16[176,2048]{1,0:T(8,128)(2,1)S(1)}, u32[]{:S(2)}, u32[]{:S(2)}) collective-permute-start(bf16[176,2048]{1,0:T(8,128)(2,1)S(1)} %constant_dynamic-update-slice_fusion.refs_0_), channel_id=1, source_target_pairs={{0,64},{1,193},{2,66},{3,195},{4,68},{5,197},{6,70},{7,199},{8,72}... | collective-permute-start | bytes 2162696 | tf_op jit(solution)/shard_map/ppermute | solution.py:34
  111.1 3.5 %forward_own.1 = (f32[512,176]{1,0:T(8,128)S(1)}, f32[512,176]{1,0:T(8,128)S(1)}, f32[512,160]{1,0:T(8,128)S(1)}, bf16[4,8,256,128]{3,2,1,0:T(8,128)(2,1)S(1)}) custom-call(bf16[4,8,256,128]{3,2,1,0:T(8,128)(2,1)S(1)} %get-tuple-element.54.mine_ref.tokens_ref, bf16[4,8,256,128]{3,2,1,0:T(8,128)(2,1)} %collective-permute-done.20.theirs_ref, ...), custom_call_target="tpu_custom_call" | custom-call | flops 1073741824 | bytes 9437184 | tf_op jit(solution)/shard_map/forward_own/pallas_call | solution.py:133
  114.6 7.0 %collective-permute-done.19.refs_2_ = bf16[160,2048]{1,0:T(8,128)(2,1)S(1)} collective-permute-done((bf16[160,2048]{1,0:T(8,128)(2,1)S(1)}, bf16[160,2048]{1,0:T(8,128)(2,1)S(1)}, u32[]{:S(2)}, u32[]{:S(2)}) %collective-permute-start.19) | collective-permute-done | bytes 655392 | tf_op jit(solution)/shard_map/ppermute | solution.py:34
  121.6 1.1 forward_theirs.1
  122.7 1.3 %collective-permute-start.21 = (bf16[256,512]{1,0:T(8,128)(2,1)S(1)}, bf16[256,512]{1,0:T(8,128)(2,1)S(1)}, u32[]{:S(2)}, u32[]{:S(2)}) collective-permute-start(bf16[256,512]{1,0:T(8,128)(2,1)S(1)} %forward_theirs.1), channel_id=1, source_target_pairs={{0,1},{1,0},{2,3},{3,2},{4,5},{5,4},{6,7},{7,6},{8,9},{9,8},{10,11... | collective-permute-start | bytes 786440 | tf_op jit(solution)/shard_map/ppermute | solution.py:34
  124.0 1.1 forward_mine.1
  125.2 0.8 add_convert_fusion
  (64 shorter events, 4.8 us)
Async XLA Ops:
  0.9 8.0 %copy-start.5 = (bf16[256,512]{1,0:T(8,128)(2,1)S(1)}, bf16[256,512]{1,0:T(8,128)(2,1)}, u32[]{:S(2)}) copy-start(bf16[256,512]{1,0:T(8,128)(2,1)} %my_cot_ref.1) | copy-start | bytes 786436
  5.5 7.5 %collective-permute-start = (bf16[4,8,256,128]{3,2,1,0:T(8,128)(2,1)S(1)}, bf16[4,8,256,128]{3,2,1,0:T(8,128)(2,1)S(1)}, u32[]{:S(2)}, u32[]{:S(2)}) collective-permute-start(bf16[4,8,256,128]{3,2,1,0:T(8,128)(2,1)S(1)} %get-tuple-element.35), channel_id=1, source_target_pairs={{0,1},{1,0},{2,3},{3,2},{4,5},{5,4},{6,7},{7,6},{8,9},{9,8},{10,11... | collective-permute-start | bytes 6291464 | tf_op jit(solution)/shard_map/ppermute | solution.py:34
  8.8 4.2 %collective-permute-start.1 = (bf16[256,512]{1,0:T(8,128)(2,1)S(1)}, bf16[256,512]{1,0:T(8,128)(2,1)S(1)}, u32[]{:S(2)}, u32[]{:S(2)}) collective-permute-start(bf16[256,512]{1,0:T(8,128)(2,1)S(1)} %copy-done.5), channel_id=1, source_target_pairs={{0,1},{1,0},{2,3},{3,2},{4,5},{5,4},{6,7},{7,6},{8,9},{9,8},{10,11... | collective-permute-start | bytes 786440 | tf_op jit(solution)/shard_map/ppermute | solution.py:34
  13.0 11.5 %copy-start.3 = (bf16[256,8192]{1,0:T(8,128)(2,1)S(1)}, bf16[256,8192]{1,0:T(8,128)(2,1)}, u32[]{:S(2)}) copy-start(bf16[256,8192]{1,0:T(8,128)(2,1)} %in_ref.3) | copy-start | bytes 12582916
  15.4 13.2 %collective-permute-start.5 = (bf16[176,2048]{1,0:T(8,128)(2,1)S(1)}, bf16[176,2048]{1,0:T(8,128)(2,1)S(1)}, u32[]{:S(2)}, u32[]{:S(2)}) collective-permute-start(bf16[176,2048]{1,0:T(8,128)(2,1)S(1)} %get-tuple-element.48), channel_id=1, source_target_pairs={{0,16},{1,49},{2,18},{3,51},{4,20},{5,53},{6,22},{7,55},{8,24},{9,... | collective-permute-start | bytes 2162696 | tf_op jit(solution)/shard_map/ppermute | solution.py:34
  16.5 17.6 %collective-permute-start.8 = (bf16[160,2048]{1,0:T(8,128)(2,1)S(1)}, bf16[160,2048]{1,0:T(8,128)(2,1)S(1)}, u32[]{:S(2)}, u32[]{:S(2)}) collective-permute-start(bf16[160,2048]{1,0:T(8,128)(2,1)S(1)} %get-tuple-element.50), channel_id=1, source_target_pairs={{0,2},{1,15},{2,0},{3,5},{4,6},{5,3},{6,4},{7,9},{8,10},{9,7},{10,... | collective-permute-start | bytes 1966088 | tf_op jit(solution)/shard_map/ppermute | solution.py:34
  22.1 11.3 %collective-permute-start.2 = (bf16[176,2048]{1,0:T(8,128)(2,1)S(1)}, bf16[176,2048]{1,0:T(8,128)(2,1)S(1)}, u32[]{:S(2)}, u32[]{:S(2)}) collective-permute-start(bf16[176,2048]{1,0:T(8,128)(2,1)S(1)} %get-tuple-element.43), channel_id=1, source_target_pairs={{0,64},{1,193},{2,66},{3,195},{4,68},{5,197},{6,70},{7,199},{8,72}... | collective-permute-start | bytes 2162696 | tf_op jit(solution)/shard_map/ppermute | solution.py:34
  28.6 1.3 %copy-start.4 = (bf16[4,8,256,128]{3,2,1,0:T(8,128)(2,1)}, bf16[4,8,256,128]{3,2,1,0:T(8,128)(2,1)S(1)}, u32[]{:S(2)}) copy-start(bf16[4,8,256,128]{3,2,1,0:T(8,128)(2,1)S(1)} %get-tuple-element.59) | copy-start | bytes 6291460
  30.0 7.6 %collective-permute-start.6 = (bf16[176,1024]{1,0:T(8,128)(2,1)S(1)}, bf16[176,1024]{1,0:T(8,128)(2,1)S(1)}, u32[]{:S(2)}, u32[]{:S(2)}) collective-permute-start(bf16[176,1024]{1,0:T(8,128)(2,1)S(1)} %slice.75), channel_id=1, source_target_pairs={{0,2},{1,15},{2,0},{3,5},{4,6},{5,3},{6,4},{7,9},{8,10},{9,7},{10,... | collective-permute-start | bytes 1081352 | tf_op jit(solution)/shard_map/ppermute | solution.py:34
  33.6 7.6 %collective-permute-start.3 = (bf16[176,1024]{1,0:T(8,128)(2,1)S(1)}, bf16[176,1024]{1,0:T(8,128)(2,1)S(1)}, u32[]{:S(2)}, u32[]{:S(2)}) collective-permute-start(bf16[176,1024]{1,0:T(8,128)(2,1)S(1)} %slice.76), channel_id=1, source_target_pairs={{0,16},{1,49},{2,18},{3,51},{4,20},{5,53},{6,22},{7,55},{8,24},{9,... | collective-permute-start | bytes 1081352 | tf_op jit(solution)/shard_map/ppermute | solution.py:34
  34.3 7.4 %collective-permute-start.9 = (bf16[160,1024]{1,0:T(8,128)(2,1)S(1)}, bf16[160,1024]{1,0:T(8,128)(2,1)S(1)}, u32[]{:S(2)}, u32[]{:S(2)}) collective-permute-start(bf16[160,1024]{1,0:T(8,128)(2,1)S(1)} %slice.77), channel_id=1, source_target_pairs={{0,64},{1,193},{2,66},{3,195},{4,68},{5,197},{6,70},{7,199},{8,72}... | collective-permute-start | bytes 983048 | tf_op jit(solution)/shard_map/ppermute | solution.py:34
  37.7 9.6 %collective-permute-start.7 = (bf16[176,512]{1,0:T(8,128)(2,1)S(1)}, bf16[176,512]{1,0:T(8,128)(2,1)S(1)}, u32[]{:S(2)}, u32[]{:S(2)}) collective-permute-start(bf16[176,512]{1,0:T(8,128)(2,1)S(1)} %slice.78), channel_id=1, source_target_pairs={{0,64},{1,193},{2,66},{3,195},{4,68},{5,197},{6,70},{7,199},{8,72}... | collective-permute-start | bytes 540680 | tf_op jit(solution)/shard_map/ppermute | solution.py:34
  41.4 5.9 %collective-permute-start.4 = (bf16[176,512]{1,0:T(8,128)(2,1)S(1)}, bf16[176,512]{1,0:T(8,128)(2,1)S(1)}, u32[]{:S(2)}, u32[]{:S(2)}) collective-permute-start(bf16[176,512]{1,0:T(8,128)(2,1)S(1)} %slice.79), channel_id=1, source_target_pairs={{0,2},{1,15},{2,0},{3,5},{4,6},{5,3},{6,4},{7,9},{8,10},{9,7},{10,... | collective-permute-start | bytes 540680 | tf_op jit(solution)/shard_map/ppermute | solution.py:34
  41.8 5.5 %collective-permute-start.10 = (bf16[160,512]{1,0:T(8,128)(2,1)S(1)}, bf16[160,512]{1,0:T(8,128)(2,1)S(1)}, u32[]{:S(2)}, u32[]{:S(2)}) collective-permute-start(bf16[160,512]{1,0:T(8,128)(2,1)S(1)} %slice.80), channel_id=1, source_target_pairs={{0,16},{1,49},{2,18},{3,51},{4,20},{5,53},{6,22},{7,55},{8,24},{9,... | collective-permute-start | bytes 491528 | tf_op jit(solution)/shard_map/ppermute | solution.py:34
  44.6 24.7 %copy-start = (f32[32,512]{1,0:T(8,128)S(1)}, f32[32,512]{1,0:T(8,128)}, u32[]{:S(2)}) copy-start(f32[32,512]{1,0:T(8,128)} %master_ref.1) | copy-start | bytes 196612
  44.7 24.7 %copy-start.1 = (f32[32,512]{1,0:T(8,128)S(1)}, f32[32,512]{1,0:T(8,128)}, u32[]{:S(2)}) copy-start(f32[32,512]{1,0:T(8,128)} %one_ref.1) | copy-start | bytes 196612
  44.7 24.6 %copy-start.2 = (f32[32,512]{1,0:T(8,128)S(1)}, f32[32,512]{1,0:T(8,128)}, u32[]{:S(2)}) copy-start(f32[32,512]{1,0:T(8,128)} %two_ref.1) | copy-start | bytes 196612
  70.3 19.2 %all-to-all-start.1 = ((bf16[16,32,512]{2,1,0:T(8,128)(2,1)}), bf16[16,32,512]{2,1,0:T(8,128)(2,1)S(1)}, u32[]{:S(2)}, u32[]{:S(2)}) async-start(bf16[16,32,512]{2,1,0:T(8,128)(2,1)} %get-tuple-element.55), calls=%async_computation.1 | async-start | bytes 1048576 | tf_op jit(solution)/shard_map/all_to_all | solution.py:258
  74.4 36.7 %collective-permute-start.20 = (bf16[4,8,256,128]{3,2,1,0:T(8,128)(2,1)}, bf16[4,8,256,128]{3,2,1,0:T(8,128)(2,1)}, u32[]{:S(2)}, u32[]{:S(2)}) collective-permute-start(bf16[4,8,256,128]{3,2,1,0:T(8,128)(2,1)} %copy-done.4), channel_id=1, source_target_pairs={{0,1},{1,0},{2,3},{3,2},{4,5},{5,4},{6,7},{7,6},{8,9},{9,8},{10,11... | collective-permute-start | bytes 6291464 | tf_op jit(solution)/shard_map/ppermute | solution.py:34
  89.8 5.8 %collective-permute-start.17 = (bf16[160,512]{1,0:T(8,128)(2,1)S(1)}, bf16[160,512]{1,0:T(8,128)(2,1)S(1)}, u32[]{:S(2)}, u32[]{:S(2)}) collective-permute-start(bf16[160,512]{1,0:T(8,128)(2,1)S(1)} %get-tuple-element.58), channel_id=1, source_target_pairs={{0,16},{1,49},{2,18},{3,51},{4,20},{5,53},{6,22},{7,55},{8,24},{9,... | collective-permute-start | bytes 491528 | tf_op jit(solution)/shard_map/ppermute | solution.py:34
  89.9 10.4 %collective-permute-start.14 = (bf16[176,512]{1,0:T(8,128)(2,1)S(1)}, bf16[176,512]{1,0:T(8,128)(2,1)S(1)}, u32[]{:S(2)}, u32[]{:S(2)}) collective-permute-start(bf16[176,512]{1,0:T(8,128)(2,1)S(1)} %get-tuple-element.57), channel_id=1, source_target_pairs={{0,64},{1,193},{2,66},{3,195},{4,68},{5,197},{6,70},{7,199},{8,72}... | collective-permute-start | bytes 540680 | tf_op jit(solution)/shard_map/ppermute | solution.py:34
  94.9 5.6 %collective-permute-start.11 = (bf16[176,512]{1,0:T(8,128)(2,1)S(1)}, bf16[176,512]{1,0:T(8,128)(2,1)S(1)}, u32[]{:S(2)}, u32[]{:S(2)}) collective-permute-start(bf16[176,512]{1,0:T(8,128)(2,1)S(1)} %get-tuple-element.56), channel_id=1, source_target_pairs={{0,2},{1,15},{2,0},{3,5},{4,6},{5,3},{6,4},{7,9},{8,10},{9,7},{10,... | collective-permute-start | bytes 540680 | tf_op jit(solution)/shard_map/ppermute | solution.py:34
  95.6 15.3 %collective-permute-start.18 = (bf16[160,1024]{1,0:T(8,128)(2,1)S(1)}, bf16[160,1024]{1,0:T(8,128)(2,1)S(1)}, u32[]{:S(2)}, u32[]{:S(2)}) collective-permute-start(bf16[160,1024]{1,0:T(8,128)(2,1)S(1)} %pad_maximum_fusion.2), channel_id=1, source_target_pairs={{0,64},{1,193},{2,66},{3,195},{4,68},{5,197},{6,70},{7,199},{8,72}... | collective-permute-start | bytes 983048 | tf_op jit(solution)/shard_map/ppermute | solution.py:34
  100.3 7.6 %collective-permute-start.15 = (bf16[176,1024]{1,0:T(8,128)(2,1)S(1)}, bf16[176,1024]{1,0:T(8,128)(2,1)S(1)}, u32[]{:S(2)}, u32[]{:S(2)}) collective-permute-start(bf16[176,1024]{1,0:T(8,128)(2,1)S(1)} %pad_maximum_fusion.1), channel_id=1, source_target_pairs={{0,2},{1,15},{2,0},{3,5},{4,6},{5,3},{6,4},{7,9},{8,10},{9,7},{10,... | collective-permute-start | bytes 1081352 | tf_op jit(solution)/shard_map/ppermute | solution.py:34
  100.6 7.6 %collective-permute-start.12 = (bf16[176,1024]{1,0:T(8,128)(2,1)S(1)}, bf16[176,1024]{1,0:T(8,128)(2,1)S(1)}, u32[]{:S(2)}, u32[]{:S(2)}) collective-permute-start(bf16[176,1024]{1,0:T(8,128)(2,1)S(1)} %pad_maximum_fusion), channel_id=1, source_target_pairs={{0,16},{1,49},{2,18},{3,51},{4,20},{5,53},{6,22},{7,55},{8,24},{9,... | collective-permute-start | bytes 1081352 | tf_op jit(solution)/shard_map/ppermute | solution.py:34
  107.9 13.7 %collective-permute-start.16 = (bf16[176,2048]{1,0:T(8,128)(2,1)S(1)}, bf16[176,2048]{1,0:T(8,128)(2,1)S(1)}, u32[]{:S(2)}, u32[]{:S(2)}) collective-permute-start(bf16[176,2048]{1,0:T(8,128)(2,1)S(1)} %constant_dynamic-update-slice_fusion.3.refs_1_), channel_id=1, source_target_pairs={{0,16},{1,49},{2,18},{3,51},{4,20},{5,53},{6,22},{7,55},{8,24},{9,... | collective-permute-start | bytes 2162696 | tf_op jit(solution)/shard_map/ppermute | solution.py:34
  108.2 13.4 %collective-permute-start.13 = (bf16[176,2048]{1,0:T(8,128)(2,1)S(1)}, bf16[176,2048]{1,0:T(8,128)(2,1)S(1)}, u32[]{:S(2)}, u32[]{:S(2)}) collective-permute-start(bf16[176,2048]{1,0:T(8,128)(2,1)S(1)} %constant_dynamic-update-slice_fusion.refs_0_), channel_id=1, source_target_pairs={{0,64},{1,193},{2,66},{3,195},{4,68},{5,197},{6,70},{7,199},{8,72}... | collective-permute-start | bytes 2162696 | tf_op jit(solution)/shard_map/ppermute | solution.py:34
  110.9 10.7 %collective-permute-start.19 = (bf16[160,2048]{1,0:T(8,128)(2,1)S(1)}, bf16[160,2048]{1,0:T(8,128)(2,1)S(1)}, u32[]{:S(2)}, u32[]{:S(2)}) collective-permute-start(bf16[160,2048]{1,0:T(8,128)(2,1)S(1)} %constant_dynamic-update-slice_fusion.6.refs_2_), channel_id=1, source_target_pairs={{0,2},{1,15},{2,0},{3,5},{4,6},{5,3},{6,4},{7,9},{8,10},{9,7},{10,... | collective-permute-start | bytes 1966088 | tf_op jit(solution)/shard_map/ppermute | solution.py:34
  122.7 2.5 %collective-permute-start.21 = (bf16[256,512]{1,0:T(8,128)(2,1)S(1)}, bf16[256,512]{1,0:T(8,128)(2,1)S(1)}, u32[]{:S(2)}, u32[]{:S(2)}) collective-permute-start(bf16[256,512]{1,0:T(8,128)(2,1)S(1)} %forward_theirs.1), channel_id=1, source_target_pairs={{0,1},{1,0},{2,3},{3,2},{4,5},{5,4},{6,7},{7,6},{8,9},{9,8},{10,11... | collective-permute-start | bytes 786440 | tf_op jit(solution)/shard_map/ppermute | solution.py:34
